TPU v7x, 512 devices: a whole 4x8x8 slice. The times are simulated.
512 devices in a mesh: ia: 16 (over z_lo, x, core), ja: 8 (over y), ka: 4 (over z_hi).
Axes of the slice: x: 4, y: 8, z: 8 (z_hi: 4, z_lo: 2; z = z_hi * 2 + z_lo), core: 2. Of those that a mesh axis runs over, the one named last changes fastest.
Arguments:
- tensor: float32 [512, 1024, 512], P('ia', 'ja', 'ka'), may hold values from -200 to 200
- factor_b: float32 [1024, 4, 96], P(('ja', 'ka')), may hold values from -4 to 4
- factor_c: float32 [512, 4, 96], P(('ka', 'ja')), may hold values from -4 to 4
Outputs:
- factor_a: float32 [512, 4, 96], P(('ia', 'ja', 'ka'))
- weights: float32 [4, 96], replicated
All inputs are finite; a program needn't handle non-finite values.
Results may differ from a plain program's by a relative error of at most 0.0003.
Values sent between devices are 32-bit elements; how exact they have to be, the bound alone decides.
No kernel may reach another device: no remote copies, remote signals or barrier semaphores. Data moves between devices by JAX's collectives and lax.ppermute only.
A program may use at most 64 MiB of HBM per device.

v0:
```python
import jax
import jax.numpy as jnp
from jax import lax
from jax.sharding import PartitionSpec as P

highest = lax.Precision.HIGHEST


def gram_of(rows):
    return jnp.einsum(
        "jsr,jsq->srq", rows, rows, precision=highest, preferred_element_type=jnp.float32
    )


def solve_normal(rows, gram_b, gram_c):
    columns = []
    for member in range(rows.shape[1]):
        normal_mat = gram_b[member] * gram_c[member]
        factor_l = jnp.linalg.cholesky(normal_mat)
        right_side = rows[:, member, :].T
        lower_sol = lax.linalg.triangular_solve(factor_l, right_side, left_side=True, lower=True)
        upper_sol = lax.linalg.triangular_solve(
            factor_l, lower_sol, left_side=True, lower=True, transpose_a=True
        )
        columns.append(upper_sol.T)
    return jnp.stack(columns, axis=1)


def shards(tensor, factor_b, factor_c):
    rows_i, rows_j, rows_k = tensor.shape
    starts, col_count = (factor_b.shape[1], factor_b.shape[2])
    width = starts * col_count
    c_block = lax.all_gather(factor_c, "ja", axis=0, tiled=True)
    partial_value = jnp.dot(
        tensor.reshape(rows_i * rows_j, rows_k),
        c_block.reshape(rows_k, width),
        precision=highest,
        preferred_element_type=jnp.float32,
    ).reshape(rows_i, rows_j, width)
    piece = lax.all_gather(factor_b, "ka", axis=0, tiled=True)
    gram_sum = jnp.zeros((starts, col_count, col_count), jnp.float32)
    count = piece.shape[0]
    flat_rows = piece.reshape(count, width)
    mttkrp = jnp.einsum(
        "ijr,jr->ir",
        partial_value,
        flat_rows,
        precision=highest,
        preferred_element_type=jnp.float32,
    )
    mttkrp, gram_rows = (mttkrp, gram_sum)
    gram_b, gram_c = lax.psum((gram_of(factor_b), gram_of(factor_c)), ("ja", "ka"))
    slab_rows = lax.psum_scatter(mttkrp, "ja", scatter_dimension=0, tiled=True)
    owned = lax.psum_scatter(slab_rows, "ka", scatter_dimension=0, tiled=True)
    owned = owned.reshape(owned.shape[0], starts, col_count)
    factor_raw = solve_normal(owned, gram_b, gram_c)
    squares = jnp.sum(factor_raw * factor_raw, axis=0)
    total = lax.psum(squares, ("ia", "ja", "ka"))
    row_total = rows_i * lax.axis_size("ia")
    weights = jnp.sqrt(total / row_total + 1e-06)
    return (factor_raw / weights[None], weights)


def solution(mesh):
    in_specs = (P("ia", "ja", "ka"), P(("ja", "ka"), None, None), P(("ka", "ja"), None, None))
    out_specs = (P(("ia", "ja", "ka"), None, None), P())
    return jax.shard_map(shards, mesh=mesh, in_specs=in_specs, out_specs=out_specs, check_vma=False)
```

profile of v0, /device:TPU:1, one launch (start us, length us, event | category | flops | bytes accessed | tf_op | source)
XLA Modules:
  0.0 503.4 jit_solution(228719153162087754)
XLA Ops:
  7.2 2.1 fusion.22
  9.3 2.1 fusion
  11.4 18.7 %all_gather.7 = f32[128,4,96]{2,1,0:T(4,128)S(1)} all-gather(f32[32,4,96]{2,1,0:T(4,128)} %param.9), channel_id=1, replica_groups=mesh['ia'=16,'ja'=8,'ka'=4] {'ka'}, dimensions={0}, use_global_device_ids=true | all-gather | bytes 245760 | tf_op jit(solution)/shard_map/all_gather | solution.py:40
  30.1 22.2 %all_gather.6 = f32[128,4,96]{2,1,0:T(4,128)S(1)} all-gather(f32[16,4,96]{2,1,0:T(4,128)} %param.10), channel_id=1, replica_groups=mesh['ia'=16,'ja'=8,'ka'=4] {'ja'}, dimensions={0}, use_global_device_ids=true | all-gather | bytes 221184 | tf_op jit(solution)/shard_map/all_gather | solution.py:33
  52.7 1.3 dynamic-slice
  54.0 1.3 dynamic-slice.2
  55.9 5.5 %multiply_reduce_fusion = f32[384,32]{0,1:T(8,128)S(1)} fusion(f32[384,128]{0,1:T(8,128)S(1)} %copy.52, f32[32,128,128]{2,1,0:T(8,128)S(1)} %copy-done, f32[128,384,1]{0,1,2:T(8,128)S(1)} %bitcast.141), kind=kOutput, calls=%fused_computation | convolution fusion | flops 2419052544 | bytes 2539520 | tf_op jit(solution)/shard_map/dot_general | solution.py:34
  61.4 23.5 %all-reduce = f32[32,384]{1,0:T(8,128)S(1)} all-reduce(f32[32,384]{1,0:T(8,128)S(1)} %bitcast.142), channel_id=2, replica_groups=mesh['ia'=16,'ja'=8,'ka'=4] {'ja'}, use_global_device_ids=true, to_apply=%region_4.0.clone | all-reduce | flops 12288 | bytes 98304
  84.9 9.5 %all-reduce.1 = f32[4,384]{1,0:T(4,128)S(1)} all-reduce(f32[4,384]{1,0:T(4,128)S(1)} %constant_dynamic-slice_fusion), channel_id=3, replica_groups=mesh['ia'=16,'ja'=8,'ka'=4] {'ka'}, use_global_device_ids=true, to_apply=%region_5.0.clone | all-reduce | flops 1536 | bytes 12288
  94.5 0.7 dynamic-slice_reduce_fusion
  95.2 210.4 %all-reduce.5.cloned.1.call-done = (f32[4,96,96]{1,2,0:T(8,128)}, f32[4,96,96]{1,2,0:T(8,128)}) async-done(((f32[4,96,96]{1,2,0:T(8,128)}, f32[4,96,96]{1,2,0:T(8,128)}), (f32[4,96,96]{1,2,0:T(8,128)}, f32[4,96,96]{1,2,0:T(8,128)})) %all-reduce.5.cloned.1.call-update) | async-done | bytes 294928 | tf_op jit(solution)/shard_map/psum | solution.py:52
  305.6 1.0 fusion.24
  307.0 1.0 fusion.9
  308.0 8.8 %cholesky.107 = f32[96,96]{1,0:T(8,128)S(1)} custom-call(f32[96,96]{1,0:T(8,128)S(1)} %get-tuple-element.10), custom_call_target="Cholesky" | custom-call | tf_op jit(solution)/shard_map/jit(cholesky)/cholesky | solution.py:19
  317.5 0.7 fusion.5
  318.1 7.4 %custom-call.21 = f32[1,96,96]{1,2,0:T(8,128)S(1)} custom-call(f32[1,96,96]{2,1,0:T(8,128)S(1)} %fusion.5), custom_call_target="InvertDiagBlocksLowerTriangular" | custom-call | tf_op jit(solution)/shard_map/triangular_solve/custom-call.2 | solution.py:22
  325.8 8.8 %cholesky.96 = f32[96,96]{1,0:T(8,128)S(1)} custom-call(f32[96,96]{1,0:T(8,128)S(1)} %get-tuple-element.11), custom_call_target="Cholesky" | custom-call | tf_op jit(solution)/shard_map/jit(cholesky)/cholesky | solution.py:19
  335.3 0.7 fusion.4
  336.0 7.4 %custom-call.19 = f32[1,96,96]{1,2,0:T(8,128)S(1)} custom-call(f32[1,96,96]{2,1,0:T(8,128)S(1)} %fusion.4), custom_call_target="InvertDiagBlocksLowerTriangular" | custom-call | tf_op jit(solution)/shard_map/triangular_solve/custom-call.2 | solution.py:22
  343.7 8.8 %cholesky.85 = f32[96,96]{1,0:T(8,128)S(1)} custom-call(f32[96,96]{1,0:T(8,128)S(1)} %get-tuple-element.12), custom_call_target="Cholesky" | custom-call | tf_op jit(solution)/shard_map/jit(cholesky)/cholesky | solution.py:19
  353.8 7.4 %custom-call.17 = f32[1,96,96]{1,2,0:T(8,128)S(1)} custom-call(f32[1,96,96]{2,1,0:T(8,128)S(1)} %fusion.3), custom_call_target="InvertDiagBlocksLowerTriangular" | custom-call | tf_op jit(solution)/shard_map/triangular_solve/custom-call.2 | solution.py:22
  361.5 9.0 %cholesky.74 = f32[96,96]{1,0:T(8,128)S(1)} custom-call(f32[96,96]{1,0:T(8,128)S(1)} %get-tuple-element.9), custom_call_target="Cholesky" | custom-call | tf_op jit(solution)/shard_map/jit(cholesky)/cholesky | solution.py:19
  371.9 7.4 %custom-call.15 = f32[1,96,96]{1,2,0:T(8,128)S(1)} custom-call(f32[1,96,96]{2,1,0:T(8,128)S(1)} %fusion.2), custom_call_target="InvertDiagBlocksLowerTriangular" | custom-call | tf_op jit(solution)/shard_map/triangular_solve/custom-call.2 | solution.py:22
  379.6 116.4 %psum.23 = f32[4,96]{1,0:T(4,128)S(1)} all-reduce(f32[4,96]{1,0:T(4,128)S(1)} %fusion.36), channel_id=1, replica_groups=mesh['ia'=16,'ja'=8,'ka'=4] {'ia','ja','ka'}, use_global_device_ids=true, to_apply=%region_6.10 | all-reduce | flops 384 | bytes 3072 | tf_op jit(solution)/shard_map/psum | solution.py:58
  (33 shorter events, 6.8 us)
Async XLA Ops:
  7.2 48.7 %copy-start = (f32[32,128,128]{2,1,0:T(8,128)S(1)}, f32[32,128,128]{2,1,0:T(8,128)}, u32[]{:S(2)}) copy-start(f32[32,128,128]{2,1,0:T(8,128)} %param.8) | copy-start | bytes 6291460
  7.2 298.5 %all-reduce.5.cloned.1.call-start = ((), (), s32[]{:S(2)}) async-start(), calls=%async_computation | async-start | bytes 786432 | tf_op jit(solution)/shard_map/psum | solution.py:52
Sparse Core Ops, SparseCore 0:
  11.5 294.0 all-reduce.4
where the time goes:
time: 504 us; the launch traced here: 503 us
  waiting for transfers between devices  210 us (42%)
  blocking collectives  190 us (38%)
  other arithmetic  72.8 us (14%)
  between operations  14.9 us (3%)
  matrix products  11 us (2%)
    psum x1, waiting for transfers between devices, shards(): lax.psum((gram_of(factor_b), gram_of(factor_c)), ('ja', 'ka'))  210 us
    psum x1, blocking collectives, shards(): total = lax.psum(squares, ('ia', 'ja', 'ka'))  116 us
    another operation x12, other arithmetic, solve_normal(): factor_l = jnp.linalg.cholesky(normal_mat)  38.1 us
    unnamed x2, blocking collectives  33 us
    another operation x8, other arithmetic, solve_normal(): lax.linalg.triangular_solve(factor_l, lower_sol, left_side=True, lower=Tr...  32 us
    all_gather x1, blocking collectives, shards(): c_block = lax.all_gather(factor_c, 'ja', axis=0, tiled=True)  22.2 us
    all_gather x1, blocking collectives, shards(): piece = lax.all_gather(factor_b, 'ka', axis=0, tiled=True)  18.7 us
  transfers between devices with their start and end apart: 1, of which 1 were waited for; matrix products, arithmetic and copies ran while one was open for 2% of the time, Pallas kernels for 0%

commit v1 on v0

v1 whole, which is shorter than its diff:
```python
import jax
import jax.numpy as jnp
from jax import lax
from jax.experimental import pallas as pl
from jax.experimental.pallas import tpu as pltpu
from jax.sharding import PartitionSpec as P

highest = lax.Precision.HIGHEST
f32 = jnp.float32
bf16 = jnp.bfloat16

R = 96
S = 4
W = S * R
VMEM = pl.BlockSpec(memory_space=pltpu.VMEM)


def dot(a, b, dims, precision=highest):
    return lax.dot_general(a, b, (dims, ((), ())), precision=precision, preferred_element_type=f32)


def lanes(shape):
    return lax.broadcasted_iota(jnp.int32, shape, 1)


def rows(shape):
    return lax.broadcasted_iota(jnp.int32, shape, 0)


def call(body, out, cost=None, scratch=()):
    shapes = [jax.ShapeDtypeStruct(o, f32) for o in out]

    def run(*args):
        return pl.pallas_call(
            body,
            out_shape=shapes,
            in_specs=[VMEM] * len(args),
            out_specs=[VMEM] * len(shapes),
            scratch_shapes=list(scratch),
            compiler_params=pltpu.CompilerParams(vmem_limit_bytes=32 * 1024 * 1024),
            cost_estimate=cost,
        )(*args)

    return run


def prepare(fb_ref, fc_ref, out_ref, z_ref):
    nc = fc_ref.shape[0]
    parts, depth = out_ref.shape[0], z_ref.shape[0] // out_ref.shape[0]
    low = lanes((R, 128)) <= rows((R, 128))
    flat = []
    for s in range(S):
        b = fb_ref[:, s, :]
        c = fc_ref[:, s, :]
        flat.append(c)
        wide_b = jnp.concatenate([b, jnp.zeros((b.shape[0], 128 - R), f32)], axis=1)
        wide_c = jnp.concatenate([c, jnp.zeros((c.shape[0], 128 - R), f32)], axis=1)
        gram_b = dot(b, wide_b, ((0,), (0,)))
        gram_c = dot(c, pltpu.roll(wide_c, 1, 1), ((0,), (0,)))
        z_ref[s * R : (s + 1) * R, :] = jnp.where(low, gram_b, gram_c)
    c_flat = jnp.concatenate(flat, axis=1)
    third = depth // 3
    for p in range(parts):
        out_ref[p, 0:nc, :] = c_flat
        for q in range(3):
            at = p * depth + q * third
            out_ref[p, nc : nc + third, q * 128 : (q + 1) * 128] = z_ref[at : at + third, :]


def middle(got_ref, fb_ref, out_ref, z_ref):
    parts = out_ref.shape[0]
    nb = fb_ref.shape[0]
    peers, third = got_ref.shape[0], z_ref.shape[0] // 3
    nc = got_ref.shape[1] - third
    share = got_ref[0, nc:, :]
    for p in range(1, peers):
        share = share + got_ref[p, nc:, :]
    for q in range(3):
        z_ref[q * third : (q + 1) * third, :] = share[:, q * 128 : (q + 1) * 128]
    b_flat = jnp.concatenate([fb_ref[:, s, :] for s in range(S)], axis=1)
    depth = z_ref.shape[0] // parts
    step = depth // 3
    for p in range(parts):
        out_ref[p, 0:nb, :] = b_flat
        for q in range(3):
            at = p * depth + q * step
            out_ref[p, nb : nb + step, q * 128 : (q + 1) * 128] = z_ref[at : at + step, :]
        out_ref[p, nb + step :, :] = jnp.zeros((out_ref.shape[1] - nb - step, W), f32)


def contract(t_ref, c_got_ref, b_got_ref, out_ref, m_ref):
    ni, nj, nk = t_ref.shape
    nc = nk // c_got_ref.shape[0]
    nb = nj // b_got_ref.shape[0]
    c = jnp.concatenate([c_got_ref[p, 0:nc, :] for p in range(c_got_ref.shape[0])], axis=0)
    b = jnp.concatenate([b_got_ref[p, 0:nb, :] for p in range(b_got_ref.shape[0])], axis=0)
    c_high = c.astype(bf16)
    c_low = (c - c_high.astype(f32)).astype(bf16)
    twice = jnp.concatenate([c_high, c_high], axis=0)
    group = 8
    for at in range(0, ni, group):
        t = t_ref[at : at + group, :, :].reshape(group * nj, nk)
        t_high = t.astype(bf16)
        t_low = (t - t_high.astype(f32)).astype(bf16)
        both = jnp.concatenate([t_high, t_low], axis=1)
        value = dot(both, twice, ((1,), (0,)), None) + dot(t_high, c_low, ((1,), (0,)), None)
        value = value.reshape(group, nj, W) * b[None]
        m_ref[at : at + group, :] = jnp.sum(value, axis=1)
    share = b_got_ref[0, nb : nb + 8, :]
    for p in range(1, b_got_ref.shape[0]):
        share = share + b_got_ref[p, nb : nb + 8, :]
    step = 4
    z = jnp.concatenate([share[0:step, q * 128 : (q + 1) * 128] for q in range(3)], axis=0)
    for p in range(out_ref.shape[0]):
        out_ref[p, 0 : 3 * step, :] = z
    pad = jnp.zeros((ni, 128 - R), f32)
    for s in range(S):
        one = jnp.concatenate([m_ref[:, s * R : (s + 1) * R], pad], axis=1)
        out_ref[:, 3 * step + s, :] = one


def own_row(got_ref, out_ref):
    total = jnp.sum(got_ref[:, 12:16, :], axis=0)
    out_ref[...] = jnp.broadcast_to(total[None], out_ref.shape)


def invert(got_ref, out_ref, z_ref):
    for p in range(got_ref.shape[0]):
        z_ref[12 * p : 12 * (p + 1), :] = got_ref[p, 0:12, :]
    lane, row = lanes((R, 128)), rows((R, 128))
    fill = jnp.zeros((128 - R, 128), f32)
    mats = []
    for s in range(S):
        z = z_ref[s * R : (s + 1) * R, :]
        low = jnp.where(lane <= row, z, 0.0)
        b_up = jnp.concatenate([low, fill], axis=0).T[0:R]
        c_up = pltpu.roll(z, 127, 1)
        up = jnp.where((lane >= row) & (lane < R), b_up * c_up, 0.0)
        strict = jnp.where(lane > row, up, 0.0)
        mats.append(up + jnp.concatenate([strict, fill], axis=0).T[0:R])
    lane1 = lanes((1, 128))
    for k in range(R):
        for s in range(S):
            a = mats[s]
            col = a[:, k : k + 1]
            top = a[k : k + 1, :]
            inv = 1.0 / top[:, k : k + 1]
            scaled = jnp.where(lane1 == k, inv, top * inv)
            here = row[:, 0:1] == k
            col = jnp.where(here, -1.0, col)
            kept = jnp.where((lane == k) | (row == k), 0.0, a)
            mats[s] = kept - col * scaled
    for s in range(S):
        out_ref[s] = mats[s]


def solve(m_ref, own_ref, inv_ref, out_ref, raw_ref):
    squares = []
    for s in range(S):
        inv = inv_ref[s]
        raw = dot(m_ref[:, s, 0:R], inv, ((1,), (0,)))
        squares.append(jnp.sum(raw * raw, axis=0, keepdims=True))
        raw_ref[s : s + 1, :] = dot(own_ref[0, :, 0:R], inv, ((1,), (0,)))[s : s + 1]
    total = jnp.concatenate(squares, axis=0)
    out_ref[...] = jnp.broadcast_to(total[None], out_ref.shape)


def finish_of(row_total):
    def finish(got_ref, raw_ref, fa_ref, w_ref):
        total = jnp.sum(got_ref[...], axis=0)
        weights = jnp.sqrt(total / row_total + 1e-06)
        w_ref[...] = weights[:, 0:R]
        fa_ref[0] = (raw_ref[...] / weights)[:, 0:R]

    return finish


def shards(tensor, factor_b, factor_c):
    ni = tensor.shape[0]
    ia, ja, ka = (lax.axis_size(a) for a in ("ia", "ja", "ka"))
    depth = S * R // ja
    slots_c = call(prepare, [(ja, factor_c.shape[0] + depth // 3, W)], scratch=[pltpu.VMEM((S * R, 128), f32)])(
        factor_b, factor_c
    )[0]
    got_c = lax.all_to_all(slots_c, "ja", 0, 0)
    slots_b = call(middle, [(ka, factor_b.shape[0] + 8, W)], scratch=[pltpu.VMEM((depth, 128), f32)])(got_c, factor_b)[0]
    got_b = lax.all_to_all(slots_b, "ka", 0, 0)
    slots_m = call(contract, [(ja * ka, 16, 128)], scratch=[pltpu.VMEM((ni, W), f32)])(tensor, got_c, got_b)[0]
    got_m = lax.all_to_all(slots_m, ("ja", "ka"), 0, 0)
    own = call(own_row, [(ja * ka, S, 128)])(got_m)[0]
    all_rows = lax.all_to_all(own, ("ja", "ka"), 0, 0)
    cost = pl.CostEstimate(flops=int(1e10), bytes_accessed=int(4e7), transcendentals=0)
    inverse = call(invert, [(S, R, 128)], cost=cost, scratch=[pltpu.VMEM((S * R, 128), f32)])(got_m)[0]
    squares, raw = call(solve, [(ia, S, 128), (S, 128)])(all_rows, own, inverse)
    got_s = lax.all_to_all(squares, "ia", 0, 0)
    return tuple(call(finish_of(ni * ia), [(1, S, R), (S, R)])(got_s, raw))


def solution(mesh):
    in_specs = (P("ia", "ja", "ka"), P(("ja", "ka"), None, None), P(("ka", "ja"), None, None))
    out_specs = (P(("ia", "ja", "ka"), None, None), P())
    return jax.shard_map(shards, mesh=mesh, in_specs=in_specs, out_specs=out_specs, check_vma=False)
```

time: 504 us -> 95.1 us (0.19)
  waiting for transfers between devices: 210 us -> 0.01 us
  blocking collectives: 190 us -> 68.9 us
  other arithmetic: 72.8 us -> 0 us
  Pallas kernels: 0 us -> 16.9 us
  between operations: 14.9 us -> 0.69 us
  matrix products: 11 us -> 0 us
  starting transfers between devices: 0.04 us -> 6.51 us
    psum x1 -> x0, waiting for transfers between devices: 210 us -> none  [shards(): lax.psum((gram_of(factor_b), gram_of(factor_c)), ('ja', 'ka'))]
    psum x1 -> x0, blocking collectives: 116 us -> none  [shards(): total = lax.psum(squares, ('ia', 'ja', 'ka'))]
    another operation x20 -> x0, other arithmetic: 70.2 us -> none  [the longest x12 38.1 us: solve_normal(): factor_l = jnp.linalg.cholesky(normal_mat)]
    all_to_all x0 -> x4, blocking collectives: none -> 68.9 us  [the longest x1 19.9 us: shards(): got_c = lax.all_to_all(slots_c, 'ja', 0, 0)]
    all_gather x2 -> x0, blocking collectives: 40.9 us -> none  [the longest x1 22.2 us: shards(): c_block = lax.all_gather(factor_c, 'ja', axis=0, tiled=True)]
    unnamed x2 -> x0, blocking collectives: 33 us -> none
    pallas_call x0 -> x7, Pallas kernels: none -> 16.9 us  [run(): pl.pallas_call(body, out_shape=shapes, in_specs=[VMEM] * len(args), out_s...]
    dot_general x3 -> x0, matrix products: 9.69 us -> none  [the longest x1 5.52 us: shards(): jnp.dot(tensor.reshape(rows_i * rows_j, rows_k), c_block.reshape(rows_k,...]
  transfers between devices with their start and end apart: 1 -> 1, of which waited for: 1 -> 0; matrix products, arithmetic and copies ran while one was open for 2% -> 0% of each run, Pallas kernels for 0% -> 12%
where the time goes in v1:
time: 95.1 us; the launch traced here: 94.7 us
  blocking collectives  68.9 us (72%)
  Pallas kernels  16.9 us (18%)
  starting transfers between devices  6.51 us (7%)
  local copies, waits for them, and re-layouts  1.59 us (2%)
    all_to_all x1, blocking collectives, shards(): got_c = lax.all_to_all(slots_c, 'ja', 0, 0)  19.9 us
    all_to_all x1, blocking collectives, shards(): got_b = lax.all_to_all(slots_b, 'ka', 0, 0)  19.8 us
    pallas_call x7, Pallas kernels, run(): pl.pallas_call(body, out_shape=shapes, in_specs=[VMEM] * len(args), out_s...  16.9 us
    all_to_all x1, blocking collectives, shards(): got_m = lax.all_to_all(slots_m, ('ja', 'ka'), 0, 0)  16.8 us
    all_to_all x1, blocking collectives, shards(): got_s = lax.all_to_all(squares, 'ia', 0, 0)  12.3 us
    all_to_all x1, starting transfers between devices, shards(): all_rows = lax.all_to_all(own, ('ja', 'ka'), 0, 0)  6.51 us
  transfers between devices with their start and end apart: 1, of which 0 were waited for; matrix products, arithmetic and copies ran while one was open for 0% of the time, Pallas kernels for 12%

profile of v1, /device:TPU:1, one launch (start us, length us, event | category | flops | bytes accessed | tf_op | source)
XLA Modules:
  0.0 94.7 jit_solution(17179028626721146891)
XLA Ops:
  0.6 0.0 copy-start.1
  0.6 0.8 copy-done.1
  1.5 0.0 copy-start.2
  1.5 0.8 copy-done.2
  2.2 0.0 copy-start
  2.2 0.5 shard_map.50
  2.8 19.9 %all_to_all.25.got_ref.c_got_ref = f32[8,32,384]{2,1,0:T(8,128)S(1)} all-to-all(f32[8,32,384]{2,1,0:T(8,128)S(1)} %shard_map.50), channel_id=1, replica_groups=mesh['ia'=16,'ja'=8,'ka'=4] {'ja'}, dimensions={0} | all-to-all | bytes 786432 | tf_op jit(solution)/shard_map/all_to_all | solution.py:185
  22.7 0.1 shard_map.51
  22.8 19.8 %all_to_all.26.b_got_ref = f32[4,40,384]{2,1,0:T(8,128)S(1)} all-to-all(f32[4,40,384]{2,1,0:T(8,128)S(1)} %shard_map.51), channel_id=1, replica_groups=mesh['ia'=16,'ja'=8,'ka'=4] {'ka'}, dimensions={0} | all-to-all | bytes 491520 | tf_op jit(solution)/shard_map/all_to_all | solution.py:187
  42.6 0.0 copy-done
  42.6 2.2 %shard_map.52 = f32[32,16,128]{2,1,0:T(8,128)S(1)} custom-call(f32[32,128,128]{2,1,0:T(8,128)S(1)} %copy-done, f32[8,32,384]{2,1,0:T(8,128)S(1)} %all_to_all.25.got_ref.c_got_ref, f32[4,40,384]{2,1,0:T(8,128)S(1)} %all_to_all.26.b_got_ref), custom_call_target="tpu_custom_call" | custom-call | tf_op jit(solution)/shard_map/pallas_call | solution.py:34
  44.8 16.8 %all_to_all.27.got_ref = f32[32,16,128]{2,1,0:T(8,128)S(1)} all-to-all(f32[32,16,128]{2,1,0:T(8,128)S(1)} %shard_map.52), channel_id=1, replica_groups=mesh['ia'=16,'ja'=8,'ka'=4] {'ja','ka'}, dimensions={0} | all-to-all | bytes 524288 | tf_op jit(solution)/shard_map/all_to_all | solution.py:189
  61.6 0.7 shard_map.53.own_ref
  62.3 6.5 %all-to-all-start.3 = ((f32[32,4,128]{2,1,0:T(4,128)}), f32[32,4,128]{2,1,0:T(4,128)S(1)}, u32[]{:S(2)}, u32[]{:S(2)}) async-start(f32[32,4,128]{2,1,0:T(4,128)} %shard_map.53.own_ref), calls=%async_computation.3 | async-start | bytes 131072 | tf_op jit(solution)/shard_map/all_to_all | solution.py:191
  68.8 11.6 %shard_map.54.inv_ref = f32[4,96,128]{2,1,0:T(8,128)S(1)} custom-call(f32[32,16,128]{2,1,0:T(8,128)S(1)} %all_to_all.27.got_ref), custom_call_target="tpu_custom_call" | custom-call | flops 10000000000 | bytes 40000000 | tf_op jit(solution)/shard_map/pallas_call | solution.py:34
  80.5 0.0 all-to-all-done.3.m_ref
  80.5 1.3 %shard_map.55 = (f32[16,4,128]{2,1,0:T(4,128)S(1)}, f32[4,128]{1,0:T(4,128)S(1)}) custom-call(f32[32,4,128]{2,1,0:T(4,128)S(1)} %all-to-all-done.3.m_ref, f32[32,4,128]{2,1,0:T(4,128)} %shard_map.53.own_ref, f32[4,96,128]{2,1,0:T(8,128)S(1)} %shard_map.54.inv_ref), custom_call_target="tpu_custom_call" | custom-call | tf_op jit(solution)/shard_map/pallas_call | solution.py:34
  81.7 12.3 %all_to_all.28.got_ref = f32[16,4,128]{2,1,0:T(4,128)S(1)} all-to-all(f32[16,4,128]{2,1,0:T(4,128)S(1)} %get-tuple-element.4), channel_id=1, replica_groups=mesh['ia'=16,'ja'=8,'ka'=4] {'ia'}, dimensions={0} | all-to-all | bytes 65536 | tf_op jit(solution)/shard_map/all_to_all | solution.py:195
  94.1 0.6 shard_map.56
Async XLA Ops:
  0.6 0.8 copy-start.1
  1.5 0.8 copy-start.2
  2.2 40.4 %copy-start = (f32[32,128,128]{2,1,0:T(8,128)S(1)}, f32[32,128,128]{2,1,0:T(8,128)}, u32[]{:S(2)}) copy-start(f32[32,128,128]{2,1,0:T(8,128)} %t_ref.1) | copy-start | bytes 6291460
  62.3 18.2 %all-to-all-start.3 = ((f32[32,4,128]{2,1,0:T(4,128)}), f32[32,4,128]{2,1,0:T(4,128)S(1)}, u32[]{:S(2)}, u32[]{:S(2)}) async-start(f32[32,4,128]{2,1,0:T(4,128)} %shard_map.53.own_ref), calls=%async_computation.3 | async-start | bytes 131072 | tf_op jit(solution)/shard_map/all_to_all | solution.py:191

commit v2 on v1

--- a/solution.py
+++ b/solution.py
@@ -44,11 +44,16 @@
     return run
 
 
-def prepare(fb_ref, fc_ref, out_ref, z_ref):
+def work(flops, nbytes):
+    return pl.CostEstimate(flops=int(flops), bytes_accessed=int(nbytes), transcendentals=0)
+
+
+def prepare(fb_ref, fc_ref, out_ref, b_ref, z_ref):
     nc = fc_ref.shape[0]
     parts, depth = out_ref.shape[0], z_ref.shape[0] // out_ref.shape[0]
     low = lanes((R, 128)) <= rows((R, 128))
     flat = []
+    b_ref[...] = jnp.concatenate([fb_ref[:, s, :] for s in range(S)], axis=1)
     for s in range(S):
         b = fb_ref[:, s, :]
         c = fc_ref[:, s, :]
@@ -67,9 +72,8 @@
             out_ref[p, nc : nc + third, q * 128 : (q + 1) * 128] = z_ref[at : at + third, :]
 
 
-def middle(got_ref, fb_ref, out_ref, z_ref):
+def middle(got_ref, out_ref, z_ref):
     parts = out_ref.shape[0]
-    nb = fb_ref.shape[0]
     peers, third = got_ref.shape[0], z_ref.shape[0] // 3
     nc = got_ref.shape[1] - third
     share = got_ref[0, nc:, :]
@@ -77,23 +81,17 @@
         share = share + got_ref[p, nc:, :]
     for q in range(3):
         z_ref[q * third : (q + 1) * third, :] = share[:, q * 128 : (q + 1) * 128]
-    b_flat = jnp.concatenate([fb_ref[:, s, :] for s in range(S)], axis=1)
-    depth = z_ref.shape[0] // parts
-    step = depth // 3
+    step = z_ref.shape[0] // parts
     for p in range(parts):
-        out_ref[p, 0:nb, :] = b_flat
-        for q in range(3):
-            at = p * depth + q * step
-            out_ref[p, nb : nb + step, q * 128 : (q + 1) * 128] = z_ref[at : at + step, :]
-        out_ref[p, nb + step :, :] = jnp.zeros((out_ref.shape[1] - nb - step, W), f32)
-
-
-def contract(t_ref, c_got_ref, b_got_ref, out_ref, m_ref):
+        out_ref[p, 0:step, :] = z_ref[p * step : (p + 1) * step, :]
+        out_ref[p, step:, :] = jnp.zeros((out_ref.shape[1] - step, 128), f32)
+
+
+def contract(t_ref, c_got_ref, b_ref, out_ref):
     ni, nj, nk = t_ref.shape
     nc = nk // c_got_ref.shape[0]
-    nb = nj // b_got_ref.shape[0]
     c = jnp.concatenate([c_got_ref[p, 0:nc, :] for p in range(c_got_ref.shape[0])], axis=0)
-    b = jnp.concatenate([b_got_ref[p, 0:nb, :] for p in range(b_got_ref.shape[0])], axis=0)
+    b = b_ref[...]
     c_high = c.astype(bf16)
     c_low = (c - c_high.astype(f32)).astype(bf16)
     twice = jnp.concatenate([c_high, c_high], axis=0)
@@ -105,18 +103,16 @@
         both = jnp.concatenate([t_high, t_low], axis=1)
         value = dot(both, twice, ((1,), (0,)), None) + dot(t_high, c_low, ((1,), (0,)), None)
         value = value.reshape(group, nj, W) * b[None]
-        m_ref[at : at + group, :] = jnp.sum(value, axis=1)
-    share = b_got_ref[0, nb : nb + 8, :]
-    for p in range(1, b_got_ref.shape[0]):
-        share = share + b_got_ref[p, nb : nb + 8, :]
-    step = 4
-    z = jnp.concatenate([share[0:step, q * 128 : (q + 1) * 128] for q in range(3)], axis=0)
-    for p in range(out_ref.shape[0]):
-        out_ref[p, 0 : 3 * step, :] = z
-    pad = jnp.zeros((ni, 128 - R), f32)
+        out_ref[at : at + group, :] = jnp.sum(value, axis=1)
+
+
+def pack(m_ref, z_got_ref, out_ref):
+    share = jnp.sum(z_got_ref[...], axis=0)
+    out_ref[:, 0:12, :] = jnp.broadcast_to(share[None, 0:12], (out_ref.shape[0], 12, 128))
+    pad = jnp.zeros((m_ref.shape[0], 128 - R), f32)
     for s in range(S):
         one = jnp.concatenate([m_ref[:, s * R : (s + 1) * R], pad], axis=1)
-        out_ref[:, 3 * step + s, :] = one
+        out_ref[:, 12 + s, :] = one
 
 
 def own_row(got_ref, out_ref):
@@ -138,20 +134,26 @@
         up = jnp.where((lane >= row) & (lane < R), b_up * c_up, 0.0)
         strict = jnp.where(lane > row, up, 0.0)
         mats.append(up + jnp.concatenate([strict, fill], axis=0).T[0:R])
-    lane1 = lanes((1, 128))
+    lane1, lane8, row8 = lanes((1, 128)), lanes((8, 128)), rows((8, 1))
+    count = R // 8
+    blocks = [[mats[s][8 * i : 8 * i + 8] for i in range(count)] for s in range(S)]
+    scale = [jnp.zeros((1, 128), f32)] * S
     for k in range(R):
+        own, at = divmod(k, 8)
         for s in range(S):
-            a = mats[s]
-            col = a[:, k : k + 1]
-            top = a[k : k + 1, :]
-            inv = 1.0 / top[:, k : k + 1]
-            scaled = jnp.where(lane1 == k, inv, top * inv)
-            here = row[:, 0:1] == k
-            col = jnp.where(here, -1.0, col)
-            kept = jnp.where((lane == k) | (row == k), 0.0, a)
-            mats[s] = kept - col * scaled
-    for s in range(S):
-        out_ref[s] = mats[s]
+            top = blocks[s][own][at : at + 1]
+            inv = 1.0 / jnp.broadcast_to(top[:, k : k + 1], (1, 128))
+            scale[s] = jnp.where(lane1 == k, inv, scale[s])
+            full = jnp.broadcast_to(jnp.where(lane1 == k, 1.0, top) * inv, (8, 128))
+            for i in range(own if at < 7 else own + 1, count):
+                a = blocks[s][i]
+                new = jnp.where(lane8 == k, 0.0, a) - a[:, k : k + 1] * full
+                blocks[s][i] = jnp.where(row8 > at, new, a) if i == own else new
+    for s in range(S):
+        w = jnp.concatenate(blocks[s], axis=0)
+        w = jnp.where(lane == row, 1.0, jnp.where(lane < row, w, 0.0))
+        inv = jnp.sum(jnp.where(lane == row, scale[s], 0.0), axis=1, keepdims=True)
+        out_ref[s] = dot(w[:, 0:R], w * inv, ((0,), (0,)))
 
 
 def solve(m_ref, own_ref, inv_ref, out_ref, raw_ref):
@@ -179,18 +181,20 @@
     ni = tensor.shape[0]
     ia, ja, ka = (lax.axis_size(a) for a in ("ia", "ja", "ka"))
     depth = S * R // ja
-    slots_c = call(prepare, [(ja, factor_c.shape[0] + depth // 3, W)], scratch=[pltpu.VMEM((S * R, 128), f32)])(
+    nb, nc = factor_b.shape[0], factor_c.shape[0]
+    slots_c, b_flat = call(prepare, [(ja, nc + depth // 3, W), (nb, W)], scratch=[pltpu.VMEM((S * R, 128), f32)])(
         factor_b, factor_c
-    )[0]
+    )
     got_c = lax.all_to_all(slots_c, "ja", 0, 0)
-    slots_b = call(middle, [(ka, factor_b.shape[0] + 8, W)], scratch=[pltpu.VMEM((depth, 128), f32)])(got_c, factor_b)[0]
-    got_b = lax.all_to_all(slots_b, "ka", 0, 0)
-    slots_m = call(contract, [(ja * ka, 16, 128)], scratch=[pltpu.VMEM((ni, W), f32)])(tensor, got_c, got_b)[0]
+    b_block = lax.all_gather(b_flat, "ka", axis=0, tiled=True)
+    slots_z = call(middle, [(ka, 16, 128)], scratch=[pltpu.VMEM((depth, 128), f32)])(got_c)[0]
+    got_z = lax.all_to_all(slots_z, "ka", 0, 0)
+    m_part = call(contract, [(ni, W)], cost=work(2e9, 4e6))(tensor, got_c, b_block)[0]
+    slots_m = call(pack, [(ja * ka, 16, 128)])(m_part, got_z)[0]
     got_m = lax.all_to_all(slots_m, ("ja", "ka"), 0, 0)
     own = call(own_row, [(ja * ka, S, 128)])(got_m)[0]
     all_rows = lax.all_to_all(own, ("ja", "ka"), 0, 0)
-    cost = pl.CostEstimate(flops=int(1e10), bytes_accessed=int(4e7), transcendentals=0)
-    inverse = call(invert, [(S, R, 128)], cost=cost, scratch=[pltpu.VMEM((S * R, 128), f32)])(got_m)[0]
+    inverse = call(invert, [(S, R, 128)], cost=work(1e10, 4e7), scratch=[pltpu.VMEM((S * R, 128), f32)])(got_m)[0]
     squares, raw = call(solve, [(ia, S, 128), (S, 128)])(all_rows, own, inverse)
     got_s = lax.all_to_all(squares, "ia", 0, 0)
     return tuple(call(finish_of(ni * ia), [(1, S, R), (S, R)])(got_s, raw))

time: 95.1 us -> 97.5 us (1.025)
  blocking collectives: 68.9 us -> 53 us
  starting transfers between devices: 6.51 us -> 19.1 us
  waiting for transfers between devices: 0.01 us -> 4.76 us
  local copies, waits for them, and re-layouts: 1.59 us -> 3.18 us
    all_to_all x2 -> x0, blocking collectives: 39.8 us -> none  [the longest x1 19.9 us: shards(): got_c = lax.all_to_all(slots_c, 'ja', 0, 0)]
    all_gather x0 -> x1, blocking collectives: none -> 17.2 us  [shards(): b_block = lax.all_gather(b_flat, 'ka', axis=0, tiled=True)]
    all_to_all x0 -> x2, starting transfers between devices: none -> 14.7 us  [the longest x1 7.65 us: shards(): got_c = lax.all_to_all(slots_c, 'ja', 0, 0)]
    all_to_all x1, blocking collectives: 12.3 us -> 17.8 us  [shards(): got_s = lax.all_to_all(squares, 'ia', 0, 0)]
    all_to_all x0 -> x2, waiting for transfers between devices: none -> 3.1 us  [the longest x1 3.1 us: shards(): got_z = lax.all_to_all(slots_z, 'ka', 0, 0)]
    all_to_all x1, starting transfers between devices: 6.51 us -> 4.41 us  [shards(): all_rows = lax.all_to_all(own, ('ja', 'ka'), 0, 0)]
    all_to_all x1, waiting for transfers between devices: 0.01 us -> 1.66 us  [shards(): all_rows = lax.all_to_all(own, ('ja', 'ka'), 0, 0)]
    unnamed x6, local copies, waits for them, and re-layouts: 1.59 us -> 3.18 us
  transfers between devices with their start and end apart: 1 -> 3, of which waited for: 0 -> 2; matrix products, arithmetic and copies ran while one was open for 0% -> 0% of each run, Pallas kernels for 12% -> 12%
where the time goes in v2:
time: 97.5 us; the launch traced here: 96.9 us
  blocking collectives  53 us (54%)
  starting transfers between devices  19.1 us (20%)
  Pallas kernels  16.2 us (17%)
  waiting for transfers between devices  4.76 us (5%)
  local copies, waits for them, and re-layouts  3.18 us (3%)
    all_to_all x1, blocking collectives, shards(): got_m = lax.all_to_all(slots_m, ('ja', 'ka'), 0, 0)  18 us
    all_to_all x1, blocking collectives, shards(): got_s = lax.all_to_all(squares, 'ia', 0, 0)  17.8 us
    all_gather x1, blocking collectives, shards(): b_block = lax.all_gather(b_flat, 'ka', axis=0, tiled=True)  17.2 us
    pallas_call x8, Pallas kernels, run(): pl.pallas_call(body, out_shape=shapes, in_specs=[VMEM] * len(args), out_s...  16.2 us
    all_to_all x1, starting transfers between devices, shards(): got_c = lax.all_to_all(slots_c, 'ja', 0, 0)  7.65 us
    all_to_all x1, starting transfers between devices, shards(): got_z = lax.all_to_all(slots_z, 'ka', 0, 0)  7.04 us
    all_to_all x1, starting transfers between devices, shards(): all_rows = lax.all_to_all(own, ('ja', 'ka'), 0, 0)  4.41 us
    unnamed x6, local copies, waits for them, and re-layouts  3.18 us
  transfers between devices with their start and end apart: 3, of which 2 were waited for; matrix products, arithmetic and copies ran while one was open for 0% of the time, Pallas kernels for 12%

profile of v2, /device:TPU:1, one launch (start us, length us, event | category | flops | bytes accessed | tf_op | source)
XLA Modules:
  0.0 96.9 jit_solution(14242440783466350326)
XLA Ops:
  0.6 0.0 copy-start
  0.6 0.8 copy-done
  1.5 0.0 copy-start.1
  1.5 0.8 copy-done.1
  2.2 1.3 %shard_map.50 = (f32[8,32,384]{2,1,0:T(8,128)}, f32[32,384]{1,0:T(8,128)S(1)}) custom-call(f32[32,4,96]{2,1,0:T(4,128)S(1)} %copy-done, f32[16,4,96]{2,1,0:T(4,128)S(1)} %copy-done.1), custom_call_target="tpu_custom_call" | custom-call | tf_op jit(solution)/shard_map/pallas_call | solution.py:34
  3.5 7.7 %all-to-all-start = ((f32[8,32,384]{2,1,0:T(8,128)}), f32[8,32,384]{2,1,0:T(8,128)S(1)}, u32[]{:S(2)}, u32[]{:S(2)}) async-start(f32[8,32,384]{2,1,0:T(8,128)} %get-tuple-element.6), calls=%async_computation | async-start | bytes 786432 | tf_op jit(solution)/shard_map/all_to_all | solution.py:188
  11.2 17.2 %all_gather.3.b_ref = f32[128,384]{1,0:T(8,128)S(1)} all-gather(f32[32,384]{1,0:T(8,128)S(1)} %get-tuple-element.7), channel_id=1, replica_groups=mesh['ia'=16,'ja'=8,'ka'=4] {'ka'}, dimensions={0}, use_global_device_ids=true | all-gather | bytes 245760 | tf_op jit(solution)/shard_map/all_gather | solution.py:189
  28.3 0.0 all-to-all-done.c_got_ref.got_ref
  28.3 0.6 shard_map.52
  29.0 7.0 %all-to-all-start.1 = ((f32[4,16,128]{2,1,0:T(8,128)}), f32[4,16,128]{2,1,0:T(8,128)S(1)}, u32[]{:S(2)}, u32[]{:S(2)}) async-start(f32[4,16,128]{2,1,0:T(8,128)} %shard_map.52), calls=%async_computation.1 | async-start | bytes 65536 | tf_op jit(solution)/shard_map/all_to_all | solution.py:191
  36.0 0.0 copy-start.2
  36.0 1.6 %copy-done.2 = f32[32,128,128]{2,1,0:T(8,128)S(1)} copy-done((f32[32,128,128]{2,1,0:T(8,128)S(1)}, f32[32,128,128]{2,1,0:T(8,128)}, u32[]{:S(2)}) %copy-start.2) | copy-done | bytes 2097176
  37.6 2.1 %shard_map.51.m_ref = f32[32,384]{1,0:T(8,128)S(1)} custom-call(f32[32,128,128]{2,1,0:T(8,128)S(1)} %copy-done.2, f32[8,32,384]{2,1,0:T(8,128)S(1)} %all-to-all-done.c_got_ref.got_ref, f32[128,384]{1,0:T(8,128)S(1)} %all_gather.3.b_ref), custom_call_target="tpu_custom_call" | custom-call | flops 2000000000 | bytes 4000000 | tf_op jit(solution)/shard_map/pallas_call | solution.py:34
  39.7 3.1 %all-to-all-done.1.z_got_ref = f32[4,16,128]{2,1,0:T(8,128)S(1)} async-done(((f32[4,16,128]{2,1,0:T(8,128)}), f32[4,16,128]{2,1,0:T(8,128)S(1)}, u32[]{:S(2)}, u32[]{:S(2)}) %all-to-all-start.1) | async-done | bytes 32800 | tf_op jit(solution)/shard_map/all_to_all | solution.py:191
  42.8 0.1 shard_map.53
  42.9 18.0 %all_to_all.25.got_ref = f32[32,16,128]{2,1,0:T(8,128)S(1)} all-to-all(f32[32,16,128]{2,1,0:T(8,128)S(1)} %shard_map.53), channel_id=1, replica_groups=mesh['ia'=16,'ja'=8,'ka'=4] {'ja','ka'}, dimensions={0} | all-to-all | bytes 524288 | tf_op jit(solution)/shard_map/all_to_all | solution.py:194
  60.9 0.7 shard_map.54.own_ref
  61.6 4.4 %all-to-all-start.3 = ((f32[32,4,128]{2,1,0:T(4,128)}), f32[32,4,128]{2,1,0:T(4,128)S(1)}, u32[]{:S(2)}, u32[]{:S(2)}) async-start(f32[32,4,128]{2,1,0:T(4,128)} %shard_map.54.own_ref), calls=%async_computation.3 | async-start | bytes 131072 | tf_op jit(solution)/shard_map/all_to_all | solution.py:196
  66.0 9.5 %shard_map.55.inv_ref = f32[4,96,128]{2,1,0:T(8,128)S(1)} custom-call(f32[32,16,128]{2,1,0:T(8,128)S(1)} %all_to_all.25.got_ref), custom_call_target="tpu_custom_call" | custom-call | flops 10000000000 | bytes 40000000 | tf_op jit(solution)/shard_map/pallas_call | solution.py:34
  75.5 1.7 %all-to-all-done.3.m_ref = f32[32,4,128]{2,1,0:T(4,128)S(1)} async-done(((f32[32,4,128]{2,1,0:T(4,128)}), f32[32,4,128]{2,1,0:T(4,128)S(1)}, u32[]{:S(2)}, u32[]{:S(2)}) %all-to-all-start.3) | async-done | bytes 65568 | tf_op jit(solution)/shard_map/all_to_all | solution.py:196
  77.2 1.3 %shard_map.56 = (f32[16,4,128]{2,1,0:T(4,128)S(1)}, f32[4,128]{1,0:T(4,128)S(1)}) custom-call(f32[32,4,128]{2,1,0:T(4,128)S(1)} %all-to-all-done.3.m_ref, f32[32,4,128]{2,1,0:T(4,128)} %shard_map.54.own_ref, f32[4,96,128]{2,1,0:T(8,128)S(1)} %shard_map.55.inv_ref), custom_call_target="tpu_custom_call" | custom-call | tf_op jit(solution)/shard_map/pallas_call | solution.py:34
  78.5 17.8 %all_to_all.26.got_ref = f32[16,4,128]{2,1,0:T(4,128)S(1)} all-to-all(f32[16,4,128]{2,1,0:T(4,128)S(1)} %get-tuple-element.8), channel_id=1, replica_groups=mesh['ia'=16,'ja'=8,'ka'=4] {'ia'}, dimensions={0} | all-to-all | bytes 65536 | tf_op jit(solution)/shard_map/all_to_all | solution.py:199
  96.3 0.6 shard_map.57
Async XLA Ops:
  0.6 0.8 copy-start
  1.5 0.8 copy-start.1
  3.5 24.8 %all-to-all-start = ((f32[8,32,384]{2,1,0:T(8,128)}), f32[8,32,384]{2,1,0:T(8,128)S(1)}, u32[]{:S(2)}, u32[]{:S(2)}) async-start(f32[8,32,384]{2,1,0:T(8,128)} %get-tuple-element.6), calls=%async_computation | async-start | bytes 786432 | tf_op jit(solution)/shard_map/all_to_all | solution.py:188
  29.0 13.8 %all-to-all-start.1 = ((f32[4,16,128]{2,1,0:T(8,128)}), f32[4,16,128]{2,1,0:T(8,128)S(1)}, u32[]{:S(2)}, u32[]{:S(2)}) async-start(f32[4,16,128]{2,1,0:T(8,128)} %shard_map.52), calls=%async_computation.1 | async-start | bytes 65536 | tf_op jit(solution)/shard_map/all_to_all | solution.py:191
  36.0 1.6 %copy-start.2 = (f32[32,128,128]{2,1,0:T(8,128)S(1)}, f32[32,128,128]{2,1,0:T(8,128)}, u32[]{:S(2)}) copy-start(f32[32,128,128]{2,1,0:T(8,128)} %t_ref.1) | copy-start | bytes 6291460
  61.6 15.6 %all-to-all-start.3 = ((f32[32,4,128]{2,1,0:T(4,128)}), f32[32,4,128]{2,1,0:T(4,128)S(1)}, u32[]{:S(2)}, u32[]{:S(2)}) async-start(f32[32,4,128]{2,1,0:T(4,128)} %shard_map.54.own_ref), calls=%async_computation.3 | async-start | bytes 131072 | tf_op jit(solution)/shard_map/all_to_all | solution.py:196

commit v3 on v2

v3 whole, which is shorter than its diff:
```python
import jax
import jax.numpy as jnp
from jax import lax
from jax.experimental import pallas as pl
from jax.experimental.pallas import tpu as pltpu
from jax.sharding import PartitionSpec as P

highest = lax.Precision.HIGHEST
f32 = jnp.float32
bf16 = jnp.bfloat16

R = 96
S = 4
W = S * R
VMEM = pl.BlockSpec(memory_space=pltpu.VMEM)
HBM = pl.BlockSpec(memory_space=pltpu.HBM)


def dot(a, b, dims, precision=highest):
    return lax.dot_general(a, b, (dims, ((), ())), precision=precision, preferred_element_type=f32)


def lanes(shape):
    return lax.broadcasted_iota(jnp.int32, shape, 1)


def rows(shape):
    return lax.broadcasted_iota(jnp.int32, shape, 0)


def call(body, out, cost=None, scratch=(), hbm=0, limit=32):
    shapes = [jax.ShapeDtypeStruct(o, f32) for o in out]

    def run(*args):
        return pl.pallas_call(
            body,
            out_shape=shapes,
            in_specs=[HBM] * hbm + [VMEM] * (len(args) - hbm),
            out_specs=[VMEM] * len(shapes),
            scratch_shapes=list(scratch),
            compiler_params=pltpu.CompilerParams(vmem_limit_bytes=limit * 1024 * 1024),
            cost_estimate=cost,
        )(*args)

    return run


def work(flops, nbytes):
    return pl.CostEstimate(flops=int(flops), bytes_accessed=int(nbytes), transcendentals=0)


def prepare(fb_hbm, fc_hbm, out_ref, b_ref, z_ref, fb_ref, fc_ref, sems):
    copy_c = pltpu.make_async_copy(fc_hbm, fc_ref, sems.at[0])
    copy_b = pltpu.make_async_copy(fb_hbm, fb_ref, sems.at[1])
    copy_c.start()
    copy_b.start()
    copy_c.wait()
    c_flat = jnp.concatenate([fc_ref[:, s, :] for s in range(S)], axis=1)
    out_ref[...] = jnp.broadcast_to(c_flat[None], out_ref.shape)
    copy_b.wait()
    b_ref[...] = jnp.concatenate([fb_ref[:, s, :] for s in range(S)], axis=1)
    low = lanes((R, 128)) <= rows((R, 128))
    for s in range(S):
        b = fb_ref[:, s, :]
        c = fc_ref[:, s, :]
        wide_b = jnp.concatenate([b, jnp.zeros((b.shape[0], 128 - R), f32)], axis=1)
        wide_c = jnp.concatenate([c, jnp.zeros((c.shape[0], 128 - R), f32)], axis=1)
        gram_b = dot(b, wide_b, ((0,), (0,)))
        gram_c = dot(c, pltpu.roll(wide_c, 1, 1), ((0,), (0,)))
        z_ref[s * R : (s + 1) * R, :] = jnp.where(low, gram_b, gram_c)


def contract(t_hbm, z_hbm, c_ref, b_ref, out_ref, t_ref, z_ref, m_ref, sems):
    ni, nj, nk = t_ref.shape
    steps = sems.shape[0] - 1
    group = ni // steps
    copy_z = pltpu.make_async_copy(z_hbm, z_ref, sems.at[steps])
    parts = [pl.ds(n * group, group) for n in range(steps)]
    copies = [pltpu.make_async_copy(t_hbm.at[p], t_ref.at[p], sems.at[n]) for n, p in enumerate(parts)]
    for copy in copies + [copy_z]:
        copy.start()
    c = c_ref[...].reshape(nk, W)
    c_high = c.astype(bf16)
    c_low = (c - c_high.astype(f32)).astype(bf16)
    twice = jnp.concatenate([c_high, c_high], axis=0)
    b = b_ref[...]
    for n in range(steps):
        copies[n].wait()
        at = n * group
        t = t_ref[at : at + group, :, :].reshape(group * nj, nk)
        t_high = t.astype(bf16)
        t_low = (t - t_high.astype(f32)).astype(bf16)
        both = jnp.concatenate([t_high, t_low], axis=1)
        value = dot(both, twice, ((1,), (0,)), None) + dot(t_high, c_low, ((1,), (0,)), None)
        value = value.reshape(group, nj, W) * b[None]
        m_ref[at : at + group, :] = jnp.sum(value, axis=1)
    copy_z.wait()
    for p in range(ni):
        out_ref[p, 0:12, :] = z_ref[12 * p : 12 * (p + 1), :]
    out_ref[:, 15, :] = jnp.zeros((ni, 128), f32)
    for q in range(3):
        out_ref[:, 12 + q, :] = m_ref[:, q * 128 : (q + 1) * 128]


def total(got_ref, out_ref):
    out_ref[...] = jnp.broadcast_to(jnp.sum(got_ref[...], axis=0)[None], out_ref.shape)


def block(got_ref, out_ref):
    flat = jnp.concatenate([got_ref[:, 12 + q, :] for q in range(3)], axis=1)
    out_ref[...] = jnp.broadcast_to(flat[None], out_ref.shape)


def invert(got_ref, own_ref, out_ref, raw_ref, z_ref):
    for p in range(got_ref.shape[0]):
        z_ref[12 * p : 12 * (p + 1), :] = got_ref[p, 0:12, :]
    lane, row = lanes((R, 128)), rows((R, 128))
    fill = jnp.zeros((128 - R, 128), f32)
    mats = []
    for s in range(S):
        z = z_ref[s * R : (s + 1) * R, :]
        low = jnp.where(lane <= row, z, 0.0)
        b_up = jnp.concatenate([low, fill], axis=0).T[0:R]
        c_up = pltpu.roll(z, 127, 1)
        up = jnp.where((lane >= row) & (lane < R), b_up * c_up, 0.0)
        strict = jnp.where(lane > row, up, 0.0)
        mats.append(up + jnp.concatenate([strict, fill], axis=0).T[0:R])
    lane1, lane8, row8 = lanes((1, 128)), lanes((8, 128)), rows((8, 1))
    count = R // 8
    blocks = [[mats[s][8 * i : 8 * i + 8] for i in range(count)] for s in range(S)]
    scale = [jnp.zeros((1, 128), f32)] * S
    for k in range(R):
        own, at = divmod(k, 8)
        for s in range(S):
            top = blocks[s][own][at : at + 1]
            inv = 1.0 / jnp.broadcast_to(top[:, k : k + 1], (1, 128))
            scale[s] = jnp.where(lane1 == k, inv, scale[s])
            full = jnp.broadcast_to(jnp.where(lane1 == k, 1.0, top) * inv, (8, 128))
            for i in range(own if at < 7 else own + 1, count):
                a = blocks[s][i]
                new = jnp.where(lane8 == k, 0.0, a) - a[:, k : k + 1] * full
                blocks[s][i] = jnp.where(row8 > at, new, a) if i == own else new
    for s in range(S):
        w = jnp.concatenate(blocks[s], axis=0)
        w = jnp.where(lane == row, 1.0, jnp.where(lane < row, w, 0.0))
        inv = jnp.sum(jnp.where(lane == row, scale[s], 0.0), axis=1, keepdims=True)
        inverse = dot(w[:, 0:R], w * inv, ((0,), (0,)))[:, 0:R]
        sides = [jnp.zeros((R, n * R), f32) for n in (s, S - 1 - s) if n]
        parts = [inverse] + sides if s == 0 else sides[:1] + [inverse] + sides[1:]
        out_ref[s * R : (s + 1) * R, :] = jnp.concatenate(parts, axis=1)
    row_own = jnp.concatenate([own_ref[0, 12 + q : 13 + q, :] for q in range(3)], axis=1)
    raw_ref[...] = dot(row_own, out_ref[...], ((1,), (0,)))


def finish(m_ref, inv_ref, raw_ref, fa_ref, w_ref):
    count = m_ref.shape[0] * m_ref.shape[1]
    raw = dot(m_ref[...].reshape(count, W), inv_ref[...], ((1,), (0,)))
    squares = jnp.sum(raw * raw, axis=0, keepdims=True)
    weights = jnp.sqrt(squares / count + 1e-06)
    scaled = raw_ref[...] / weights
    for s in range(S):
        fa_ref[0, s : s + 1, :] = scaled[:, s * R : (s + 1) * R]
        w_ref[s : s + 1, :] = weights[:, s * R : (s + 1) * R]


def shards(tensor, factor_b, factor_c):
    ni = tensor.shape[0]
    ia, ja, ka = (lax.axis_size(a) for a in ("ia", "ja", "ka"))
    nb, nc = factor_b.shape[0], factor_c.shape[0]
    slots_c, b_flat, share = call(
        prepare,
        [(ja, nc, W), (nb, W), (S * R, 128)],
        scratch=[pltpu.VMEM(factor_b.shape, f32), pltpu.VMEM(factor_c.shape, f32), pltpu.SemaphoreType.DMA((2,))],
        hbm=2,
        limit=56,
    )(factor_b, factor_c)
    got_c = lax.all_to_all(slots_c, "ja", 0, 0)
    b_block = lax.all_gather(b_flat, "ka", axis=0, tiled=True)
    slots_m = call(
        contract,
        [(ja * ka, 16, 128)],
        scratch=[pltpu.VMEM(v, f32) for v in (tensor.shape, share.shape, (ni, W))] + [pltpu.SemaphoreType.DMA((5,))],
        hbm=2,
        limit=52,
    )(tensor, share, got_c, b_block)[0]
    got_m = lax.all_to_all(slots_m, ("ja", "ka"), 0, 0)
    own = call(total, [(ja * ka, 16, 128)])(got_m)[0]
    got_all = lax.all_to_all(own, ("ja", "ka"), 0, 0)
    slots_i = call(block, [(ia, ni, W)])(got_all)[0]
    m_all = lax.all_to_all(slots_i, "ia", 0, 0)
    inverse, raw = call(invert, [(W, W), (1, W)], cost=work(1e10, 4e7), scratch=[pltpu.VMEM((S * R, 128), f32)])(
        got_all, own
    )
    return tuple(call(finish, [(1, S, R), (S, R)])(m_all, inverse, raw))


def solution(mesh):
    in_specs = (P("ia", "ja", "ka"), P(("ja", "ka"), None, None), P(("ka", "ja"), None, None))
    out_specs = (P(("ia", "ja", "ka"), None, None), P())
    return jax.shard_map(shards, mesh=mesh, in_specs=in_specs, out_specs=out_specs, check_vma=False)
```

time: 97.5 us -> 98.4 us (level)
  Pallas kernels: 16.2 us -> 19.6 us
  local copies, waits for them, and re-layouts: 3.18 us -> 0.93 us
  waiting for transfers between devices: 4.76 us -> 2.83 us
  blocking collectives: 53 us -> 54.8 us
    all_to_all x1, blocking collectives: 18 us -> 21.7 us  [shards(): got_m = lax.all_to_all(slots_m, ('ja', 'ka'), 0, 0)]
    pallas_call x8 -> x6, Pallas kernels: 16.2 us -> 19.6 us  [run(): pl.pallas_call(body, out_shape=shapes, in_specs=[HBM] * hbm + [VMEM] * (l...]
    unnamed x6 -> x2, local copies, waits for them, and re-layouts: 3.18 us -> 0.93 us
    all_to_all x1, blocking collectives: 17.8 us -> 15.7 us  [shards(): got_all = lax.all_to_all(own, ('ja', 'ka'), 0, 0)]
    all_to_all x2 -> x1, waiting for transfers between devices: 4.76 us -> 2.83 us  [shards(): m_all = lax.all_to_all(slots_i, 'ia', 0, 0)]
    all_to_all x2 -> x1, starting transfers between devices: 11.4 us -> 11.4 us  [shards(): m_all = lax.all_to_all(slots_i, 'ia', 0, 0)]
  transfers between devices with their start and end apart: 3 -> 2, of which waited for: 2 -> 1; matrix products, arithmetic and copies ran while one was open for 0% -> 0% of each run, Pallas kernels for 12% -> 10%
where the time goes in v3:
time: 98.4 us; the launch traced here: 97.9 us
  blocking collectives  54.8 us (56%)
  Pallas kernels  19.6 us (20%)
  starting transfers between devices  19.1 us (19%)
  waiting for transfers between devices  2.83 us (3%)
    all_to_all x1, blocking collectives, shards(): got_m = lax.all_to_all(slots_m, ('ja', 'ka'), 0, 0)  21.7 us
    pallas_call x6, Pallas kernels, run(): pl.pallas_call(body, out_shape=shapes, in_specs=[HBM] * hbm + [VMEM] * (l...  19.6 us
    all_gather x1, blocking collectives, shards(): b_block = lax.all_gather(b_flat, 'ka', axis=0, tiled=True)  17.4 us
    all_to_all x1, blocking collectives, shards(): got_all = lax.all_to_all(own, ('ja', 'ka'), 0, 0)  15.7 us
    all_to_all x1, starting transfers between devices, shards(): m_all = lax.all_to_all(slots_i, 'ia', 0, 0)  11.4 us
    all_to_all x1, starting transfers between devices, shards(): got_c = lax.all_to_all(slots_c, 'ja', 0, 0)  7.66 us
    all_to_all x1, waiting for transfers between devices, shards(): m_all = lax.all_to_all(slots_i, 'ia', 0, 0)  2.83 us
  transfers between devices with their start and end apart: 2, of which 1 were waited for; matrix products, arithmetic and copies ran while one was open for 0% of the time, Pallas kernels for 10%

profile of v3, /device:TPU:1, one launch (start us, length us, event | category | flops | bytes accessed | tf_op | source)
XLA Modules:
  0.0 97.9 jit_solution(12472215454620351853)
XLA Ops:
  0.6 2.1 %shard_map.50 = (f32[8,16,384]{2,1,0:T(8,128)}, f32[32,384]{1,0:T(8,128)}, f32[384,128]{1,0:T(8,128)}) custom-call(f32[32,4,96]{2,1,0:T(4,128)} %fb_hbm.1, f32[16,4,96]{2,1,0:T(4,128)} %fc_hbm.1), custom_call_target="tpu_custom_call" | custom-call | tf_op jit(solution)/shard_map/pallas_call | solution.py:35
  2.7 7.7 %all-to-all-start = ((f32[8,16,384]{2,1,0:T(8,128)}), f32[8,16,384]{2,1,0:T(8,128)S(1)}, u32[]{:S(2)}, u32[]{:S(2)}) async-start(f32[8,16,384]{2,1,0:T(8,128)} %get-tuple-element.8), calls=%async_computation | async-start | bytes 393216 | tf_op jit(solution)/shard_map/all_to_all | solution.py:177
  10.4 17.4 %all_gather.3.b_ref = f32[128,384]{1,0:T(8,128)S(1)} all-gather(f32[32,384]{1,0:T(8,128)} %get-tuple-element.9), channel_id=1, replica_groups=mesh['ia'=16,'ja'=8,'ka'=4] {'ka'}, dimensions={0}, use_global_device_ids=true | all-gather | bytes 245760 | tf_op jit(solution)/shard_map/all_gather | solution.py:178
  27.8 0.0 all-to-all-done.c_ref
  27.8 0.0 copy-start
  27.8 0.9 copy-done
  28.7 4.0 %shard_map.51 = f32[32,16,128]{2,1,0:T(8,128)S(1)} custom-call(f32[32,128,128]{2,1,0:T(8,128)} %t_hbm.1, f32[384,128]{1,0:T(8,128)S(1)} %copy-done, f32[8,16,384]{2,1,0:T(8,128)S(1)} %all-to-all-done.c_ref, f32[128,384]{1,0:T(8,128)S(1)} %all_gather.3.b_ref), custom_call_target="tpu_custom_call" | custom-call | tf_op jit(solution)/shard_map/pallas_call | solution.py:35
  32.7 21.7 %all_to_all.20.got_ref = f32[32,16,128]{2,1,0:T(8,128)S(1)} all-to-all(f32[32,16,128]{2,1,0:T(8,128)S(1)} %shard_map.51), channel_id=1, replica_groups=mesh['ia'=16,'ja'=8,'ka'=4] {'ja','ka'}, dimensions={0} | all-to-all | bytes 524288 | tf_op jit(solution)/shard_map/all_to_all | solution.py:186
  54.4 0.1 shard_map.52.own_ref
  54.4 15.7 %all_to_all.21.got_ref = f32[32,16,128]{2,1,0:T(8,128)S(1)} all-to-all(f32[32,16,128]{2,1,0:T(8,128)S(1)} %shard_map.52.own_ref), channel_id=1, replica_groups=mesh['ia'=16,'ja'=8,'ka'=4] {'ja','ka'}, dimensions={0} | all-to-all | bytes 524288 | tf_op jit(solution)/shard_map/all_to_all | solution.py:188
  70.2 1.0 shard_map.53
  71.1 11.4 %all-to-all-start.3 = ((f32[16,32,384]{2,1,0:T(8,128)}), f32[16,32,384]{2,1,0:T(8,128)S(1)}, u32[]{:S(2)}, u32[]{:S(2)}) async-start(f32[16,32,384]{2,1,0:T(8,128)} %shard_map.53), calls=%async_computation.3 | async-start | bytes 1572864 | tf_op jit(solution)/shard_map/all_to_all | solution.py:190
  82.6 10.2 %shard_map.54 = (f32[384,384]{1,0:T(8,128)S(1)}, f32[1,384]{1,0:T(1,128)S(1)}) custom-call(f32[32,16,128]{2,1,0:T(8,128)S(1)} %all_to_all.21.got_ref, f32[32,16,128]{2,1,0:T(8,128)S(1)} %shard_map.52.own_ref), custom_call_target="tpu_custom_call" | custom-call | flops 10000000000 | bytes 40000000 | tf_op jit(solution)/shard_map/pallas_call | solution.py:35
  92.7 2.8 %all-to-all-done.3.m_ref = f32[16,32,384]{2,1,0:T(8,128)S(1)} async-done(((f32[16,32,384]{2,1,0:T(8,128)}), f32[16,32,384]{2,1,0:T(8,128)S(1)}, u32[]{:S(2)}, u32[]{:S(2)}) %all-to-all-start.3) | async-done | bytes 786464 | tf_op jit(solution)/shard_map/all_to_all | solution.py:190
  95.6 2.3 %shard_map.55 = (f32[1,4,96]{2,1,0:T(4,128)}, f32[4,96]{1,0:T(4,128)}) custom-call(f32[16,32,384]{2,1,0:T(8,128)S(1)} %all-to-all-done.3.m_ref, f32[384,384]{1,0:T(8,128)S(1)} %get-tuple-element.10.inv_ref, f32[1,384]{1,0:T(1,128)S(1)} %get-tuple-element.11.raw_ref), custom_call_target="tpu_custom_call" | custom-call | tf_op jit(solution)/shard_map/pallas_call | solution.py:35
Async XLA Ops:
  2.7 25.0 %all-to-all-start = ((f32[8,16,384]{2,1,0:T(8,128)}), f32[8,16,384]{2,1,0:T(8,128)S(1)}, u32[]{:S(2)}, u32[]{:S(2)}) async-start(f32[8,16,384]{2,1,0:T(8,128)} %get-tuple-element.8), calls=%async_computation | async-start | bytes 393216 | tf_op jit(solution)/shard_map/all_to_all | solution.py:177
  27.8 0.9 copy-start
  71.1 24.4 %all-to-all-start.3 = ((f32[16,32,384]{2,1,0:T(8,128)}), f32[16,32,384]{2,1,0:T(8,128)S(1)}, u32[]{:S(2)}, u32[]{:S(2)}) async-start(f32[16,32,384]{2,1,0:T(8,128)} %shard_map.53), calls=%async_computation.3 | async-start | bytes 1572864 | tf_op jit(solution)/shard_map/all_to_all | solution.py:190

commit v4 on v3

v4 whole, which is shorter than its diff:
```python
import jax
import jax.numpy as jnp
from jax import lax
from jax.experimental import pallas as pl
from jax.experimental.pallas import tpu as pltpu
from jax.sharding import PartitionSpec as P

highest = lax.Precision.HIGHEST
f32 = jnp.float32
bf16 = jnp.bfloat16

R = 96
S = 4
W = S * R
VMEM = pl.BlockSpec(memory_space=pltpu.VMEM)
HBM = pl.BlockSpec(memory_space=pltpu.HBM)


def dot(a, b, dims, precision=highest):
    return lax.dot_general(a, b, (dims, ((), ())), precision=precision, preferred_element_type=f32)


def lanes(shape):
    return lax.broadcasted_iota(jnp.int32, shape, 1)


def rows(shape):
    return lax.broadcasted_iota(jnp.int32, shape, 0)


def call(body, out, cost=None, scratch=(), hbm=0, limit=32):
    shapes = [jax.ShapeDtypeStruct(o, f32) for o in out]

    def run(*args):
        return pl.pallas_call(
            body,
            out_shape=shapes,
            in_specs=[HBM] * hbm + [VMEM] * (len(args) - hbm),
            out_specs=[VMEM] * len(shapes),
            scratch_shapes=list(scratch),
            compiler_params=pltpu.CompilerParams(vmem_limit_bytes=limit * 1024 * 1024),
            cost_estimate=cost,
        )(*args)

    return run


def prepare(fb_hbm, fc_hbm, out_ref, b_ref, z_ref, fb_ref, fc_ref, sems):
    copy_c = pltpu.make_async_copy(fc_hbm, fc_ref, sems.at[0])
    copy_b = pltpu.make_async_copy(fb_hbm, fb_ref, sems.at[1])
    copy_c.start()
    copy_b.start()
    copy_c.wait()
    parts, nc = out_ref.shape[0], fc_ref.shape[0]
    third = S * R // parts // 3
    c_flat = jnp.concatenate([fc_ref[:, s, :] for s in range(S)], axis=1)
    for p in range(parts):
        out_ref[p, 0:nc, :] = c_flat
    copy_b.wait()
    b_ref[...] = jnp.concatenate([fb_ref[:, s, :] for s in range(S)], axis=1)
    low = lanes((R, 128)) <= rows((R, 128))
    for s in range(S):
        b = fb_ref[:, s, :]
        c = fc_ref[:, s, :]
        wide_b = jnp.concatenate([b, jnp.zeros((b.shape[0], 128 - R), f32)], axis=1)
        wide_c = jnp.concatenate([c, jnp.zeros((c.shape[0], 128 - R), f32)], axis=1)
        gram_b = dot(b, wide_b, ((0,), (0,)))
        gram_c = dot(c, pltpu.roll(wide_c, 1, 1), ((0,), (0,)))
        z_ref[s * R : (s + 1) * R, :] = jnp.where(low, gram_b, gram_c)
    for p in range(parts):
        for q in range(3):
            at = (3 * p + q) * third
            out_ref[p, nc : nc + third, q * 128 : (q + 1) * 128] = z_ref[at : at + third, :]


def contract(t_hbm, c_got_ref, b_ref, out_ref, share_ref, t_ref, sems):
    ni, nj, nk = t_ref.shape
    steps = sems.shape[0]
    group = ni // steps
    parts = [pl.ds(n * group, group) for n in range(steps)]
    copies = [pltpu.make_async_copy(t_hbm.at[p], t_ref.at[p], sems.at[n]) for n, p in enumerate(parts)]
    for copy in copies:
        copy.start()
    nc = nk // c_got_ref.shape[0]
    share_ref[...] = jnp.sum(c_got_ref[:, nc:, :], axis=0)
    c = c_got_ref[:, 0:nc, :].reshape(nk, W)
    b = b_ref[...]
    c_high = c.astype(bf16)
    c_low = (c - c_high.astype(f32)).astype(bf16)
    twice = jnp.concatenate([c_high, c_high], axis=0)
    each = out_ref.shape[1]
    for n in range(steps):
        copies[n].wait()
        at = n * group
        t = t_ref[at : at + group, :, :].reshape(group * nj, nk)
        t_high = t.astype(bf16)
        t_low = (t - t_high.astype(f32)).astype(bf16)
        both = jnp.concatenate([t_high, t_low], axis=1)
        value = dot(both, twice, ((1,), (0,)), None) + dot(t_high, c_low, ((1,), (0,)), None)
        value = jnp.sum(value.reshape(group, nj, W) * b[None], axis=1)
        for p in range(group // each):
            out_ref[at // each + p] = value[p * each : (p + 1) * each]


def mix(m_ref, share_ref, out_ref):
    depth, each = share_ref.shape[0], m_ref.shape[1]
    out_ref[0:depth, :] = share_ref[...]
    out_ref[depth : depth + each, :] = jnp.sum(m_ref[...], axis=0)
    out_ref[depth + each :, :] = jnp.zeros((out_ref.shape[0] - depth - each, W), f32)


def spread(x_ref, out_ref):
    out_ref[...] = jnp.broadcast_to(x_ref[...][None], out_ref.shape)


def wide(v):
    return jnp.broadcast_to(v, (8, 128))


def eliminate(blocks, scale, k, q, lane8, row8):
    own, m = divmod(k, 8)
    hit = (lane8 >= k) & (lane8 < k + q)
    mine = blocks[own]
    row = [wide(mine[m + p : m + p + 1]) for p in range(q)]
    cols = [wide(mine[:, k + j : k + j + 1]) for j in range(q)]
    a = {(p, j): wide(cols[j][m + p : m + p + 1]) for p in range(q) for j in range(p, q)}
    inv, u, unit = [], {}, []
    for p in range(q):
        inv.append(1.0 / a[p, p])
        unit.append(jnp.where(lane8 == k + p, 1.0, row[p]))
        scale = jnp.where(lane8 == k + p, inv[p], scale)
        for i in range(p + 1, q):
            u[i, p] = a[p, i] * inv[p]
            for j in range(i, q):
                a[i, j] = a[i, j] - u[i, p] * a[p, j]
        for i in range(p + 1, q):
            row[i] = jnp.where(lane8 == k + p, 0.0, row[i]) - u[i, p] * unit[p]
    steps = [None] * q
    for p in reversed(range(q)):
        step = jnp.where((lane8 > k + p) & hit, 0.0, unit[p]) * inv[p]
        for j in range(p + 1, q):
            step = step - u[j, p] * steps[j]
        steps[p] = step
    for i in range(own, len(blocks)):
        old = blocks[i]
        new = jnp.where(hit, 0.0, old)
        for p in range(q):
            new = new - wide(old[:, k + p : k + p + 1]) * steps[p]
        if i == own:
            new = jnp.where(row8 >= m + q, new, old)
            for p in range(1, q):
                new = jnp.where(row8 == m + p, row[p], new)
        blocks[i] = new
    return scale


def solve(got_ref, own_ref, out_ref, raw_ref, z_ref, m_ref):
    peers = got_ref.shape[0]
    third = S * R // peers // 3
    each = m_ref.shape[0] // peers - 1
    for p in range(peers):
        m_ref[each * p : each * (p + 1), :] = got_ref[p, third : third + each, :]
        for q in range(3):
            at = (3 * p + q) * third
            z_ref[at : at + third, :] = got_ref[p, 0:third, q * 128 : (q + 1) * 128]
    count = each * peers
    mine = own_ref[pl.ds(third + lax.axis_index("ka"), 1), :]
    m_ref[count:, :] = jnp.broadcast_to(mine, (m_ref.shape[0] - count, W))
    lane, row = lanes((R, 128)), rows((R, 128))
    fill = jnp.zeros((128 - R, 128), f32)
    blocks = []
    for s in range(S):
        z = z_ref[s * R : (s + 1) * R, :]
        low = jnp.where(lane <= row, z, 0.0)
        b_up = jnp.concatenate([low, fill], axis=0).T[0:R]
        c_up = pltpu.roll(z, 127, 1)
        up = jnp.where((lane >= row) & (lane < R), b_up * c_up, 0.0)
        strict = jnp.where(lane > row, up, 0.0)
        full = up + jnp.concatenate([strict, fill], axis=0).T[0:R]
        blocks.append([full[8 * i : 8 * i + 8] for i in range(R // 8)])
    lane8, row8 = lanes((8, 128)), rows((8, 1))
    scale = [jnp.zeros((8, 128), f32)] * S
    for k in range(0, R, 4):
        for s in range(S):
            scale[s] = eliminate(blocks[s], scale[s], k, 4, lane8, row8)
    squares = []
    for s in range(S):
        w = jnp.concatenate(blocks[s], axis=0)
        w = jnp.where(lane == row, 1.0, jnp.where(lane < row, w, 0.0))
        half = dot(m_ref[:, s * R : (s + 1) * R], w[:, 0:R], ((1,), (1,))) * scale[s][0:1, 0:R]
        raw = dot(half, w, ((1,), (0,)))
        squares.append(jnp.sum(raw[0:count] * raw[0:count], axis=0, keepdims=True))
        raw_ref[s : s + 1, :] = raw[count : count + 1]
    out_ref[...] = jnp.broadcast_to(jnp.concatenate(squares, axis=0)[None], out_ref.shape)


def finish_of(row_total):
    def finish(got_ref, raw_ref, fa_ref, w_ref):
        total = jnp.sum(got_ref[...], axis=0)
        weights = jnp.sqrt(total / row_total + 1e-06)
        w_ref[...] = weights[:, 0:R]
        fa_ref[0] = (raw_ref[...] / weights)[:, 0:R]

    return finish


def shards(tensor, factor_b, factor_c):
    ni = tensor.shape[0]
    ia, ja, ka = (lax.axis_size(a) for a in ("ia", "ja", "ka"))
    nb, nc = factor_b.shape[0], factor_c.shape[0]
    third = S * R // ja // 3
    each = ni // ja
    grams = pltpu.VMEM((S * R, 128), f32)
    slots_c, b_flat = call(
        prepare,
        [(ja, nc + third, W), (nb, W)],
        scratch=[grams, pltpu.VMEM(factor_b.shape, f32), pltpu.VMEM(factor_c.shape, f32), pltpu.SemaphoreType.DMA((2,))],
        hbm=2,
        limit=56,
    )(factor_b, factor_c)
    got_c = lax.all_to_all(slots_c, "ja", 0, 0)
    b_block = lax.all_gather(b_flat, "ka", axis=0, tiled=True)
    slots_m, share = call(
        contract,
        [(ja, each, W), (third, W)],
        scratch=[pltpu.VMEM(tensor.shape, f32), pltpu.SemaphoreType.DMA((4,))],
        hbm=1,
        limit=52,
    )(tensor, got_c, b_block)
    got_m = lax.all_to_all(slots_m, "ja", 0, 0)
    sums = lax.psum(call(mix, [(third + 8, W)])(got_m, share)[0], "ka")
    got_all = lax.all_to_all(call(spread, [(ja, third + 8, W)])(sums)[0], "ja", 0, 0)
    squares, raw = call(solve, [(ia, S, 128), (S, 128)], scratch=[grams, pltpu.VMEM((ni + ja, W), f32)])(got_all, sums)
    got_s = lax.all_to_all(squares, "ia", 0, 0)
    return tuple(call(finish_of(ni * ia), [(1, S, R), (S, R)])(got_s, raw))


def solution(mesh):
    in_specs = (P("ia", "ja", "ka"), P(("ja", "ka"), None, None), P(("ka", "ja"), None, None))
    out_specs = (P(("ia", "ja", "ka"), None, None), P())
    return jax.shard_map(shards, mesh=mesh, in_specs=in_specs, out_specs=out_specs, check_vma=False)
```

time: 98.4 us -> 105 us (1.067)
  blocking collectives: 54.8 us -> 80 us
  starting transfers between devices: 19.1 us -> 7.66 us
  Pallas kernels: 19.6 us -> 16 us
  waiting for transfers between devices: 2.83 us -> 0.01 us
    psum x0 -> x1, blocking collectives: none -> 15.7 us  [shards(): sums = lax.psum(call(mix, [(third + 8, W)])(got_m, share)[0], 'ka')]
    all_to_all x1 -> x0, starting transfers between devices: 11.4 us -> none  [shards(): m_all = lax.all_to_all(slots_i, 'ia', 0, 0)]
    all_to_all x2 -> x3, blocking collectives: 37.4 us -> 46.9 us  [the longest x1 21.5 us: shards(): got_s = lax.all_to_all(squares, 'ia', 0, 0)]
    pallas_call x6, Pallas kernels: 19.6 us -> 16 us  [run(): pl.pallas_call(body, out_shape=shapes, in_specs=[HBM] * hbm + [VMEM] * (l...]
    all_to_all x1 -> x0, waiting for transfers between devices: 2.83 us -> none  [shards(): m_all = lax.all_to_all(slots_i, 'ia', 0, 0)]
  transfers between devices with their start and end apart: 2 -> 1, of which waited for: 1 -> 0; matrix products, arithmetic and copies ran while one was open for 0% -> 0% of each run, Pallas kernels for 10% -> 0%
where the time goes in v4:
time: 105 us; the launch traced here: 104 us
  blocking collectives  80 us (76%)
  Pallas kernels  16 us (15%)
  starting transfers between devices  7.66 us (7%)
    all_to_all x1, blocking collectives, shards(): got_s = lax.all_to_all(squares, 'ia', 0, 0)  21.5 us
    all_gather x1, blocking collectives, shards(): b_block = lax.all_gather(b_flat, 'ka', axis=0, tiled=True)  17.4 us
    pallas_call x6, Pallas kernels, run(): pl.pallas_call(body, out_shape=shapes, in_specs=[HBM] * hbm + [VMEM] * (l...  16 us
    psum x1, blocking collectives, shards(): sums = lax.psum(call(mix, [(third + 8, W)])(got_m, share)[0], 'ka')  15.7 us
    all_to_all x1, blocking collectives, shards(): got_m = lax.all_to_all(slots_m, 'ja', 0, 0)  13.3 us
    all_to_all x1, blocking collectives, shards(): lax.all_to_all(call(spread, [(ja, third + 8, W)])(sums)[0], 'ja', 0, 0)  12.1 us
    all_to_all x1, starting transfers between devices, shards(): got_c = lax.all_to_all(slots_c, 'ja', 0, 0)  7.66 us
  transfers between devices with their start and end apart: 1, of which 0 were waited for; matrix products, arithmetic and copies ran while one was open for 0% of the time, Pallas kernels for 0%

profile of v4, /device:TPU:1, one launch (start us, length us, event | category | flops | bytes accessed | tf_op | source)
XLA Modules:
  0.0 104.3 jit_solution(15709336550571374595)
XLA Ops:
  0.6 2.2 %shard_map.50 = (f32[8,32,384]{2,1,0:T(8,128)}, f32[32,384]{1,0:T(8,128)}) custom-call(f32[32,4,96]{2,1,0:T(4,128)} %fb_hbm.1, f32[16,4,96]{2,1,0:T(4,128)} %fc_hbm.1), custom_call_target="tpu_custom_call" | custom-call | tf_op jit(solution)/shard_map/pallas_call | solution.py:35
  2.8 7.7 %all-to-all-start = ((f32[8,32,384]{2,1,0:T(8,128)}), f32[8,32,384]{2,1,0:T(8,128)S(1)}, u32[]{:S(2)}, u32[]{:S(2)}) async-start(f32[8,32,384]{2,1,0:T(8,128)} %get-tuple-element.8), calls=%async_computation | async-start | bytes 786432 | tf_op jit(solution)/shard_map/all_to_all | solution.py:221
  10.5 17.4 %all_gather.3.b_ref = f32[128,384]{1,0:T(8,128)S(1)} all-gather(f32[32,384]{1,0:T(8,128)} %get-tuple-element.9), channel_id=1, replica_groups=mesh['ia'=16,'ja'=8,'ka'=4] {'ka'}, dimensions={0}, use_global_device_ids=true | all-gather | bytes 245760 | tf_op jit(solution)/shard_map/all_gather | solution.py:222
  27.8 0.0 all-to-all-done.c_got_ref
  27.8 3.9 %shard_map.51 = (f32[8,4,384]{2,1,0:T(4,128)S(1)}, f32[16,384]{1,0:T(8,128)S(1)}) custom-call(f32[32,128,128]{2,1,0:T(8,128)} %t_hbm.1, f32[8,32,384]{2,1,0:T(8,128)S(1)} %all-to-all-done.c_got_ref, f32[128,384]{1,0:T(8,128)S(1)} %all_gather.3.b_ref), custom_call_target="tpu_custom_call" | custom-call | tf_op jit(solution)/shard_map/pallas_call | solution.py:35
  31.8 13.3 %all_to_all.20.m_ref = f32[8,4,384]{2,1,0:T(4,128)S(1)} all-to-all(f32[8,4,384]{2,1,0:T(4,128)S(1)} %get-tuple-element.10), channel_id=1, replica_groups=mesh['ia'=16,'ja'=8,'ka'=4] {'ja'}, dimensions={0} | all-to-all | bytes 98304 | tf_op jit(solution)/shard_map/all_to_all | solution.py:230
  45.1 15.7 %psum.7.x_ref.own_ref = f32[24,384]{1,0:T(8,128)S(1)} all-reduce(f32[24,384]{1,0:T(8,128)S(1)} %shard_map.52), channel_id=1, replica_groups=mesh['ia'=16,'ja'=8,'ka'=4] {'ka'}, use_global_device_ids=true, to_apply=%region_0.0 | all-reduce | flops 9216 | bytes 73728 | tf_op jit(solution)/shard_map/psum | solution.py:231
  60.8 12.1 %all_to_all.21.got_ref = f32[8,24,384]{2,1,0:T(8,128)S(1)} all-to-all(f32[8,24,384]{2,1,0:T(8,128)S(1)} %shard_map.53), channel_id=1, replica_groups=mesh['ia'=16,'ja'=8,'ka'=4] {'ja'}, dimensions={0} | all-to-all | bytes 589824 | tf_op jit(solution)/shard_map/all_to_all | solution.py:232
  72.9 9.3 %shard_map.54 = (f32[16,4,128]{2,1,0:T(4,128)S(1)}, f32[4,128]{1,0:T(4,128)S(1)}) custom-call(f32[8,24,384]{2,1,0:T(8,128)S(1)} %all_to_all.21.got_ref, f32[24,384]{1,0:T(8,128)S(1)} %psum.7.x_ref.own_ref), custom_call_target="tpu_custom_call" | custom-call | tf_op jit(solution)/shard_map/pallas_call | solution.py:35
  82.2 21.5 %all_to_all.22.got_ref = f32[16,4,128]{2,1,0:T(4,128)S(1)} all-to-all(f32[16,4,128]{2,1,0:T(4,128)S(1)} %get-tuple-element.12), channel_id=1, replica_groups=mesh['ia'=16,'ja'=8,'ka'=4] {'ia'}, dimensions={0} | all-to-all | bytes 65536 | tf_op jit(solution)/shard_map/all_to_all | solution.py:234
  103.7 0.6 shard_map.55
  (2 shorter events, 0.0 us)
Async XLA Ops:
  2.8 25.0 %all-to-all-start = ((f32[8,32,384]{2,1,0:T(8,128)}), f32[8,32,384]{2,1,0:T(8,128)S(1)}, u32[]{:S(2)}, u32[]{:S(2)}) async-start(f32[8,32,384]{2,1,0:T(8,128)} %get-tuple-element.8), calls=%async_computation | async-start | bytes 786432 | tf_op jit(solution)/shard_map/all_to_all | solution.py:221

commit v5 on v1

--- a/solution.py
+++ b/solution.py
@@ -124,12 +124,53 @@
     out_ref[...] = jnp.broadcast_to(total[None], out_ref.shape)
 
 
+def wide(v):
+    return jnp.broadcast_to(v, (8, 128))
+
+
+def eliminate(blocks, scale, k, q, lane8, row8):
+    own, m = divmod(k, 8)
+    hit = (lane8 >= k) & (lane8 < k + q)
+    mine = blocks[own]
+    row = [wide(mine[m + p : m + p + 1]) for p in range(q)]
+    cols = [wide(mine[:, k + j : k + j + 1]) for j in range(q)]
+    a = {(p, j): wide(cols[j][m + p : m + p + 1]) for p in range(q) for j in range(p, q)}
+    inv, u, unit = [], {}, []
+    for p in range(q):
+        inv.append(1.0 / a[p, p])
+        unit.append(jnp.where(lane8 == k + p, 1.0, row[p]))
+        scale = jnp.where(lane8 == k + p, inv[p], scale)
+        for i in range(p + 1, q):
+            u[i, p] = a[p, i] * inv[p]
+            for j in range(i, q):
+                a[i, j] = a[i, j] - u[i, p] * a[p, j]
+        for i in range(p + 1, q):
+            row[i] = jnp.where(lane8 == k + p, 0.0, row[i]) - u[i, p] * unit[p]
+    steps = [None] * q
+    for p in reversed(range(q)):
+        step = jnp.where((lane8 > k + p) & hit, 0.0, unit[p]) * inv[p]
+        for j in range(p + 1, q):
+            step = step - u[j, p] * steps[j]
+        steps[p] = step
+    for i in range(own, len(blocks)):
+        old = blocks[i]
+        new = jnp.where(hit, 0.0, old)
+        for p in range(q):
+            new = new - wide(old[:, k + p : k + p + 1]) * steps[p]
+        if i == own:
+            new = jnp.where(row8 >= m + q, new, old)
+            for p in range(1, q):
+                new = jnp.where(row8 == m + p, row[p], new)
+        blocks[i] = new
+    return scale
+
+
 def invert(got_ref, out_ref, z_ref):
     for p in range(got_ref.shape[0]):
         z_ref[12 * p : 12 * (p + 1), :] = got_ref[p, 0:12, :]
     lane, row = lanes((R, 128)), rows((R, 128))
     fill = jnp.zeros((128 - R, 128), f32)
-    mats = []
+    blocks = []
     for s in range(S):
         z = z_ref[s * R : (s + 1) * R, :]
         low = jnp.where(lane <= row, z, 0.0)
@@ -137,21 +178,18 @@
         c_up = pltpu.roll(z, 127, 1)
         up = jnp.where((lane >= row) & (lane < R), b_up * c_up, 0.0)
         strict = jnp.where(lane > row, up, 0.0)
-        mats.append(up + jnp.concatenate([strict, fill], axis=0).T[0:R])
-    lane1 = lanes((1, 128))
-    for k in range(R):
+        full = up + jnp.concatenate([strict, fill], axis=0).T[0:R]
+        blocks.append([full[8 * i : 8 * i + 8] for i in range(R // 8)])
+    lane8, row8 = lanes((8, 128)), rows((8, 1))
+    scale = [jnp.zeros((8, 128), f32)] * S
+    for k in range(0, R, 4):
         for s in range(S):
-            a = mats[s]
-            col = a[:, k : k + 1]
-            top = a[k : k + 1, :]
-            inv = 1.0 / top[:, k : k + 1]
-            scaled = jnp.where(lane1 == k, inv, top * inv)
-            here = row[:, 0:1] == k
-            col = jnp.where(here, -1.0, col)
-            kept = jnp.where((lane == k) | (row == k), 0.0, a)
-            mats[s] = kept - col * scaled
-    for s in range(S):
-        out_ref[s] = mats[s]
+            scale[s] = eliminate(blocks[s], scale[s], k, 4, lane8, row8)
+    for s in range(S):
+        w = jnp.concatenate(blocks[s], axis=0)
+        w = jnp.where(lane == row, 1.0, jnp.where(lane < row, w, 0.0))
+        inv = jnp.sum(jnp.where(lane == row, scale[s][0:1], 0.0), axis=1, keepdims=True)
+        out_ref[s] = dot(w[:, 0:R], w * inv, ((0,), (0,)))
 
 
 def solve(m_ref, own_ref, inv_ref, out_ref, raw_ref):
@@ -179,9 +217,8 @@
     ni = tensor.shape[0]
     ia, ja, ka = (lax.axis_size(a) for a in ("ia", "ja", "ka"))
     depth = S * R // ja
-    slots_c = call(prepare, [(ja, factor_c.shape[0] + depth // 3, W)], scratch=[pltpu.VMEM((S * R, 128), f32)])(
-        factor_b, factor_c
-    )[0]
+    grams = pltpu.VMEM((S * R, 128), f32)
+    slots_c = call(prepare, [(ja, factor_c.shape[0] + depth // 3, W)], scratch=[grams])(factor_b, factor_c)[0]
     got_c = lax.all_to_all(slots_c, "ja", 0, 0)
     slots_b = call(middle, [(ka, factor_b.shape[0] + 8, W)], scratch=[pltpu.VMEM((depth, 128), f32)])(got_c, factor_b)[0]
     got_b = lax.all_to_all(slots_b, "ka", 0, 0)
@@ -190,7 +227,7 @@
     own = call(own_row, [(ja * ka, S, 128)])(got_m)[0]
     all_rows = lax.all_to_all(own, ("ja", "ka"), 0, 0)
     cost = pl.CostEstimate(flops=int(1e10), bytes_accessed=int(4e7), transcendentals=0)
-    inverse = call(invert, [(S, R, 128)], cost=cost, scratch=[pltpu.VMEM((S * R, 128), f32)])(got_m)[0]
+    inverse = call(invert, [(S, R, 128)], cost=cost, scratch=[grams])(got_m)[0]
     squares, raw = call(solve, [(ia, S, 128), (S, 128)])(all_rows, own, inverse)
     got_s = lax.all_to_all(squares, "ia", 0, 0)
     return tuple(call(finish_of(ni * ia), [(1, S, R), (S, R)])(got_s, raw))

time: 95.1 us -> 95.1 us (level)
  Pallas kernels: 16.9 us -> 12.4 us
  waiting for transfers between devices: 0.01 us -> 4.06 us
    pallas_call x7, Pallas kernels: 16.9 us -> 12.4 us  [run(): pl.pallas_call(body, out_shape=shapes, in_specs=[VMEM] * len(args), out_s...]
    all_to_all x1, waiting for transfers between devices: 0.01 us -> 4.06 us  [shards(): all_rows = lax.all_to_all(own, ('ja', 'ka'), 0, 0)]
  transfers between devices with their start and end apart: 1 -> 1, of which waited for: 0 -> 1; matrix products, arithmetic and copies ran while one was open for 0% -> 0% of each run, Pallas kernels for 12% -> 8%
where the time goes in v5:
time: 95.1 us; the launch traced here: 94.7 us
  blocking collectives  69.4 us (73%)
  Pallas kernels  12.4 us (13%)
  starting transfers between devices  6.51 us (7%)
  waiting for transfers between devices  4.06 us (4%)
  local copies, waits for them, and re-layouts  1.59 us (2%)
    all_to_all x1, blocking collectives, shards(): got_c = lax.all_to_all(slots_c, 'ja', 0, 0)  19.9 us
    all_to_all x1, blocking collectives, shards(): got_b = lax.all_to_all(slots_b, 'ka', 0, 0)  19.8 us
    all_to_all x1, blocking collectives, shards(): got_m = lax.all_to_all(slots_m, ('ja', 'ka'), 0, 0)  16.8 us
    all_to_all x1, blocking collectives, shards(): got_s = lax.all_to_all(squares, 'ia', 0, 0)  12.8 us
    pallas_call x7, Pallas kernels, run(): pl.pallas_call(body, out_shape=shapes, in_specs=[VMEM] * len(args), out_s...  12.4 us
    all_to_all x1, starting transfers between devices, shards(): all_rows = lax.all_to_all(own, ('ja', 'ka'), 0, 0)  6.51 us
    all_to_all x1, waiting for transfers between devices, shards(): all_rows = lax.all_to_all(own, ('ja', 'ka'), 0, 0)  4.06 us
  transfers between devices with their start and end apart: 1, of which 1 were waited for; matrix products, arithmetic and copies ran while one was open for 0% of the time, Pallas kernels for 8%

profile of v5, /device:TPU:1, one launch (start us, length us, event | category | flops | bytes accessed | tf_op | source)
XLA Modules:
  0.0 94.7 jit_solution(16356869903994377472)
XLA Ops:
  0.6 0.0 copy-start.1
  0.6 0.8 copy-done.1
  1.5 0.0 copy-start.2
  1.5 0.8 copy-done.2
  2.2 0.0 copy-start
  2.2 0.5 shard_map.50
  2.8 19.9 %all_to_all.25.got_ref.c_got_ref = f32[8,32,384]{2,1,0:T(8,128)S(1)} all-to-all(f32[8,32,384]{2,1,0:T(8,128)S(1)} %shard_map.50), channel_id=1, replica_groups=mesh['ia'=16,'ja'=8,'ka'=4] {'ja'}, dimensions={0} | all-to-all | bytes 786432 | tf_op jit(solution)/shard_map/all_to_all | solution.py:222
  22.7 0.1 shard_map.51
  22.8 19.8 %all_to_all.26.b_got_ref = f32[4,40,384]{2,1,0:T(8,128)S(1)} all-to-all(f32[4,40,384]{2,1,0:T(8,128)S(1)} %shard_map.51), channel_id=1, replica_groups=mesh['ia'=16,'ja'=8,'ka'=4] {'ka'}, dimensions={0} | all-to-all | bytes 491520 | tf_op jit(solution)/shard_map/all_to_all | solution.py:224
  42.6 0.0 copy-done
  42.6 2.2 %shard_map.52 = f32[32,16,128]{2,1,0:T(8,128)S(1)} custom-call(f32[32,128,128]{2,1,0:T(8,128)S(1)} %copy-done, f32[8,32,384]{2,1,0:T(8,128)S(1)} %all_to_all.25.got_ref.c_got_ref, f32[4,40,384]{2,1,0:T(8,128)S(1)} %all_to_all.26.b_got_ref), custom_call_target="tpu_custom_call" | custom-call | tf_op jit(solution)/shard_map/pallas_call | solution.py:34
  44.8 16.8 %all_to_all.27.got_ref = f32[32,16,128]{2,1,0:T(8,128)S(1)} all-to-all(f32[32,16,128]{2,1,0:T(8,128)S(1)} %shard_map.52), channel_id=1, replica_groups=mesh['ia'=16,'ja'=8,'ka'=4] {'ja','ka'}, dimensions={0} | all-to-all | bytes 524288 | tf_op jit(solution)/shard_map/all_to_all | solution.py:226
  61.6 0.7 shard_map.53.own_ref
  62.3 6.5 %all-to-all-start.3 = ((f32[32,4,128]{2,1,0:T(4,128)}), f32[32,4,128]{2,1,0:T(4,128)S(1)}, u32[]{:S(2)}, u32[]{:S(2)}) async-start(f32[32,4,128]{2,1,0:T(4,128)} %shard_map.53.own_ref), calls=%async_computation.3 | async-start | bytes 131072 | tf_op jit(solution)/shard_map/all_to_all | solution.py:228
  68.8 7.1 %shard_map.54.inv_ref = f32[4,96,128]{2,1,0:T(8,128)S(1)} custom-call(f32[32,16,128]{2,1,0:T(8,128)S(1)} %all_to_all.27.got_ref), custom_call_target="tpu_custom_call" | custom-call | flops 10000000000 | bytes 40000000 | tf_op jit(solution)/shard_map/pallas_call | solution.py:34
  75.9 4.1 %all-to-all-done.3.m_ref = f32[32,4,128]{2,1,0:T(4,128)S(1)} async-done(((f32[32,4,128]{2,1,0:T(4,128)}), f32[32,4,128]{2,1,0:T(4,128)S(1)}, u32[]{:S(2)}, u32[]{:S(2)}) %all-to-all-start.3) | async-done | bytes 65568 | tf_op jit(solution)/shard_map/all_to_all | solution.py:228
  80.0 1.3 %shard_map.55 = (f32[16,4,128]{2,1,0:T(4,128)S(1)}, f32[4,128]{1,0:T(4,128)S(1)}) custom-call(f32[32,4,128]{2,1,0:T(4,128)S(1)} %all-to-all-done.3.m_ref, f32[32,4,128]{2,1,0:T(4,128)} %shard_map.53.own_ref, f32[4,96,128]{2,1,0:T(8,128)S(1)} %shard_map.54.inv_ref), custom_call_target="tpu_custom_call" | custom-call | tf_op jit(solution)/shard_map/pallas_call | solution.py:34
  81.3 12.8 %all_to_all.28.got_ref = f32[16,4,128]{2,1,0:T(4,128)S(1)} all-to-all(f32[16,4,128]{2,1,0:T(4,128)S(1)} %get-tuple-element.4), channel_id=1, replica_groups=mesh['ia'=16,'ja'=8,'ka'=4] {'ia'}, dimensions={0} | all-to-all | bytes 65536 | tf_op jit(solution)/shard_map/all_to_all | solution.py:232
  94.1 0.6 shard_map.56
Async XLA Ops:
  0.6 0.8 copy-start.1
  1.5 0.8 copy-start.2
  2.2 40.4 %copy-start = (f32[32,128,128]{2,1,0:T(8,128)S(1)}, f32[32,128,128]{2,1,0:T(8,128)}, u32[]{:S(2)}) copy-start(f32[32,128,128]{2,1,0:T(8,128)} %t_ref.1) | copy-start | bytes 6291460
  62.3 17.7 %all-to-all-start.3 = ((f32[32,4,128]{2,1,0:T(4,128)}), f32[32,4,128]{2,1,0:T(4,128)S(1)}, u32[]{:S(2)}, u32[]{:S(2)}) async-start(f32[32,4,128]{2,1,0:T(4,128)} %shard_map.53.own_ref), calls=%async_computation.3 | async-start | bytes 131072 | tf_op jit(solution)/shard_map/all_to_all | solution.py:228

commit v6 on v5

--- a/solution.py
+++ b/solution.py
@@ -67,33 +67,22 @@
             out_ref[p, nc : nc + third, q * 128 : (q + 1) * 128] = z_ref[at : at + third, :]
 
 
-def middle(got_ref, fb_ref, out_ref, z_ref):
-    parts = out_ref.shape[0]
+def middle(got_ref, fb_ref, out_ref):
     nb = fb_ref.shape[0]
-    peers, third = got_ref.shape[0], z_ref.shape[0] // 3
-    nc = got_ref.shape[1] - third
-    share = got_ref[0, nc:, :]
-    for p in range(1, peers):
-        share = share + got_ref[p, nc:, :]
-    for q in range(3):
-        z_ref[q * third : (q + 1) * third, :] = share[:, q * 128 : (q + 1) * 128]
+    nc = got_ref.shape[1] - (out_ref.shape[1] - nb)
+    share = jnp.sum(got_ref[:, nc:, :], axis=0)
     b_flat = jnp.concatenate([fb_ref[:, s, :] for s in range(S)], axis=1)
-    depth = z_ref.shape[0] // parts
-    step = depth // 3
-    for p in range(parts):
+    for p in range(out_ref.shape[0]):
         out_ref[p, 0:nb, :] = b_flat
-        for q in range(3):
-            at = p * depth + q * step
-            out_ref[p, nb : nb + step, q * 128 : (q + 1) * 128] = z_ref[at : at + step, :]
-        out_ref[p, nb + step :, :] = jnp.zeros((out_ref.shape[1] - nb - step, W), f32)
+        out_ref[p, nb:, :] = share
 
 
 def contract(t_ref, c_got_ref, b_got_ref, out_ref, m_ref):
     ni, nj, nk = t_ref.shape
     nc = nk // c_got_ref.shape[0]
     nb = nj // b_got_ref.shape[0]
-    c = jnp.concatenate([c_got_ref[p, 0:nc, :] for p in range(c_got_ref.shape[0])], axis=0)
-    b = jnp.concatenate([b_got_ref[p, 0:nb, :] for p in range(b_got_ref.shape[0])], axis=0)
+    c = c_got_ref[:, 0:nc, :].reshape(nk, W)
+    b = b_got_ref[:, 0:nb, :].reshape(nj, W)
     c_high = c.astype(bf16)
     c_low = (c - c_high.astype(f32)).astype(bf16)
     twice = jnp.concatenate([c_high, c_high], axis=0)
@@ -106,21 +95,20 @@
         value = dot(both, twice, ((1,), (0,)), None) + dot(t_high, c_low, ((1,), (0,)), None)
         value = value.reshape(group, nj, W) * b[None]
         m_ref[at : at + group, :] = jnp.sum(value, axis=1)
-    share = b_got_ref[0, nb : nb + 8, :]
-    for p in range(1, b_got_ref.shape[0]):
-        share = share + b_got_ref[p, nb : nb + 8, :]
-    step = 4
-    z = jnp.concatenate([share[0:step, q * 128 : (q + 1) * 128] for q in range(3)], axis=0)
+    share = jnp.sum(b_got_ref[:, nb:, :], axis=0)
+    depth = share.shape[0]
+    each = ni // out_ref.shape[0]
+    pad = jnp.zeros((out_ref.shape[1] - depth - each, W), f32)
     for p in range(out_ref.shape[0]):
-        out_ref[p, 0 : 3 * step, :] = z
-    pad = jnp.zeros((ni, 128 - R), f32)
-    for s in range(S):
-        one = jnp.concatenate([m_ref[:, s * R : (s + 1) * R], pad], axis=1)
-        out_ref[:, 3 * step + s, :] = one
-
-
-def own_row(got_ref, out_ref):
-    total = jnp.sum(got_ref[:, 12:16, :], axis=0)
+        out_ref[p, 0:depth, :] = share
+        out_ref[p, depth : depth + each, :] = m_ref[each * p : each * (p + 1), :]
+        out_ref[p, depth + each :, :] = pad
+
+
+def own_rows(got_ref, out_ref):
+    each = out_ref.shape[1]
+    depth = S * R // got_ref.shape[0] // 3
+    total = jnp.sum(got_ref[:, depth : depth + each, :], axis=0)
     out_ref[...] = jnp.broadcast_to(total[None], out_ref.shape)
 
 
@@ -166,8 +154,11 @@
 
 
 def invert(got_ref, out_ref, z_ref):
+    third = S * R // got_ref.shape[0] // 3
     for p in range(got_ref.shape[0]):
-        z_ref[12 * p : 12 * (p + 1), :] = got_ref[p, 0:12, :]
+        for q in range(3):
+            at = (3 * p + q) * third
+            z_ref[at : at + third, :] = got_ref[p, 0:third, q * 128 : (q + 1) * 128]
     lane, row = lanes((R, 128)), rows((R, 128))
     fill = jnp.zeros((128 - R, 128), f32)
     blocks = []
@@ -192,15 +183,21 @@
         out_ref[s] = dot(w[:, 0:R], w * inv, ((0,), (0,)))
 
 
-def solve(m_ref, own_ref, inv_ref, out_ref, raw_ref):
+def solve(got_ref, inv_ref, out_ref, raw_ref, m_ref):
+    peers = got_ref.shape[0]
+    each = got_ref.shape[1]
+    ka = lax.axis_size("ka")
+    count = m_ref.shape[0] - 8
+    for p in range(peers // ka):
+        m_ref[each * p : each * (p + 1), :] = jnp.sum(got_ref[ka * p : ka * (p + 1)], axis=0)
+    mine = m_ref[pl.ds(lax.axis_index("ia") * each + lax.axis_index("ka"), 1), :]
+    m_ref[count:, :] = jnp.broadcast_to(mine, (8, W))
     squares = []
     for s in range(S):
-        inv = inv_ref[s]
-        raw = dot(m_ref[:, s, 0:R], inv, ((1,), (0,)))
-        squares.append(jnp.sum(raw * raw, axis=0, keepdims=True))
-        raw_ref[s : s + 1, :] = dot(own_ref[0, :, 0:R], inv, ((1,), (0,)))[s : s + 1]
-    total = jnp.concatenate(squares, axis=0)
-    out_ref[...] = jnp.broadcast_to(total[None], out_ref.shape)
+        raw = dot(m_ref[:, s * R : (s + 1) * R], inv_ref[s], ((1,), (0,)))
+        squares.append(jnp.sum(raw[0:count] * raw[0:count], axis=0, keepdims=True))
+        raw_ref[s : s + 1, :] = raw[count : count + 1]
+    out_ref[...] = jnp.broadcast_to(jnp.concatenate(squares, axis=0)[None], out_ref.shape)
 
 
 def finish_of(row_total):
@@ -216,20 +213,22 @@
 def shards(tensor, factor_b, factor_c):
     ni = tensor.shape[0]
     ia, ja, ka = (lax.axis_size(a) for a in ("ia", "ja", "ka"))
-    depth = S * R // ja
+    nb, nc = factor_b.shape[0], factor_c.shape[0]
+    third = S * R // ja // 3
+    each = ni // ja
     grams = pltpu.VMEM((S * R, 128), f32)
-    slots_c = call(prepare, [(ja, factor_c.shape[0] + depth // 3, W)], scratch=[grams])(factor_b, factor_c)[0]
+    slots_c = call(prepare, [(ja, nc + third, W)], scratch=[grams])(factor_b, factor_c)[0]
     got_c = lax.all_to_all(slots_c, "ja", 0, 0)
-    slots_b = call(middle, [(ka, factor_b.shape[0] + 8, W)], scratch=[pltpu.VMEM((depth, 128), f32)])(got_c, factor_b)[0]
+    slots_b = call(middle, [(ka, nb + third, W)])(got_c, factor_b)[0]
     got_b = lax.all_to_all(slots_b, "ka", 0, 0)
-    slots_m = call(contract, [(ja * ka, 16, 128)], scratch=[pltpu.VMEM((ni, W), f32)])(tensor, got_c, got_b)[0]
-    got_m = lax.all_to_all(slots_m, ("ja", "ka"), 0, 0)
-    own = call(own_row, [(ja * ka, S, 128)])(got_m)[0]
-    all_rows = lax.all_to_all(own, ("ja", "ka"), 0, 0)
+    slots_m = call(contract, [(ja, third + 8, W)], scratch=[pltpu.VMEM((ni, W), f32)])(tensor, got_c, got_b)[0]
+    got_m = lax.all_to_all(slots_m, "ja", 0, 0)
+    own = call(own_rows, [(ia * ka, each, W)])(got_m)[0]
+    got_t = lax.all_to_all(own, ("ia", "ka"), 0, 0)
     cost = pl.CostEstimate(flops=int(1e10), bytes_accessed=int(4e7), transcendentals=0)
     inverse = call(invert, [(S, R, 128)], cost=cost, scratch=[grams])(got_m)[0]
-    squares, raw = call(solve, [(ia, S, 128), (S, 128)])(all_rows, own, inverse)
-    got_s = lax.all_to_all(squares, "ia", 0, 0)
+    squares, raw = call(solve, [(ja, S, 128), (S, 128)], scratch=[pltpu.VMEM((ia * each + 8, W), f32)])(got_t, inverse)
+    got_s = lax.all_to_all(squares, "ja", 0, 0)
     return tuple(call(finish_of(ni * ia), [(1, S, R), (S, R)])(got_s, raw))
 
 

time: 95.1 us -> 96.1 us (1.011)
  blocking collectives: 69.4 us -> 61.2 us
  starting transfers between devices: 6.51 us -> 11.8 us
  waiting for transfers between devices: 4.06 us -> 8.59 us
    all_to_all x2, blocking collectives: 29.6 us -> 21 us  [the longest x1 12.1 us: shards(): got_m = lax.all_to_all(slots_m, 'ja', 0, 0)]
    all_to_all x1, starting transfers between devices: 6.51 us -> 11.8 us  [shards(): got_t = lax.all_to_all(own, ('ia', 'ka'), 0, 0)]
    all_to_all x1, waiting for transfers between devices: 4.06 us -> 8.59 us  [shards(): got_t = lax.all_to_all(own, ('ia', 'ka'), 0, 0)]
  transfers between devices with their start and end apart: 1 -> 1, of which waited for: 1 -> 1; matrix products, arithmetic and copies ran while one was open for 0% -> 0% of each run, Pallas kernels for 8% -> 7%
where the time goes in v6:
time: 96.1 us; the launch traced here: 95.7 us
  blocking collectives  61.2 us (64%)
  starting transfers between devices  11.8 us (12%)
  Pallas kernels  11.7 us (12%)
  waiting for transfers between devices  8.59 us (9%)
  local copies, waits for them, and re-layouts  1.59 us (2%)
    all_to_all x1, blocking collectives, shards(): got_b = lax.all_to_all(slots_b, 'ka', 0, 0)  20.3 us
    all_to_all x1, blocking collectives, shards(): got_c = lax.all_to_all(slots_c, 'ja', 0, 0)  19.9 us
    all_to_all x1, blocking collectives, shards(): got_m = lax.all_to_all(slots_m, 'ja', 0, 0)  12.1 us
    all_to_all x1, starting transfers between devices, shards(): got_t = lax.all_to_all(own, ('ia', 'ka'), 0, 0)  11.8 us
    pallas_call x7, Pallas kernels, run(): pl.pallas_call(body, out_shape=shapes, in_specs=[VMEM] * len(args), out_s...  11.7 us
    all_to_all x1, blocking collectives, shards(): got_s = lax.all_to_all(squares, 'ja', 0, 0)  8.98 us
    all_to_all x1, waiting for transfers between devices, shards(): got_t = lax.all_to_all(own, ('ia', 'ka'), 0, 0)  8.59 us
  transfers between devices with their start and end apart: 1, of which 1 were waited for; matrix products, arithmetic and copies ran while one was open for 0% of the time, Pallas kernels for 7%

profile of v6, /device:TPU:1, one launch (start us, length us, event | category | flops | bytes accessed | tf_op | source)
XLA Modules:
  0.0 95.7 jit_solution(1646538692602476770)
XLA Ops:
  0.6 0.0 copy-start.1
  0.6 0.8 copy-done.1
  1.5 0.0 copy-start.2
  1.5 0.8 copy-done.2
  2.2 0.0 copy-start
  2.2 0.5 shard_map.50
  2.8 19.9 %all_to_all.25.got_ref.c_got_ref = f32[8,32,384]{2,1,0:T(8,128)S(1)} all-to-all(f32[8,32,384]{2,1,0:T(8,128)S(1)} %shard_map.50), channel_id=1, replica_groups=mesh['ia'=16,'ja'=8,'ka'=4] {'ja'}, dimensions={0} | all-to-all | bytes 786432 | tf_op jit(solution)/shard_map/all_to_all | solution.py:221
  22.7 0.1 shard_map.51
  22.8 20.3 %all_to_all.26.b_got_ref = f32[4,48,384]{2,1,0:T(8,128)S(1)} all-to-all(f32[4,48,384]{2,1,0:T(8,128)S(1)} %shard_map.51), channel_id=1, replica_groups=mesh['ia'=16,'ja'=8,'ka'=4] {'ka'}, dimensions={0} | all-to-all | bytes 589824 | tf_op jit(solution)/shard_map/all_to_all | solution.py:223
  43.1 0.0 copy-done
  43.1 2.1 %shard_map.52 = f32[8,24,384]{2,1,0:T(8,128)S(1)} custom-call(f32[32,128,128]{2,1,0:T(8,128)S(1)} %copy-done, f32[8,32,384]{2,1,0:T(8,128)S(1)} %all_to_all.25.got_ref.c_got_ref, f32[4,48,384]{2,1,0:T(8,128)S(1)} %all_to_all.26.b_got_ref), custom_call_target="tpu_custom_call" | custom-call | tf_op jit(solution)/shard_map/pallas_call | solution.py:34
  45.2 12.1 %all_to_all.27.got_ref = f32[8,24,384]{2,1,0:T(8,128)S(1)} all-to-all(f32[8,24,384]{2,1,0:T(8,128)S(1)} %shard_map.52), channel_id=1, replica_groups=mesh['ia'=16,'ja'=8,'ka'=4] {'ja'}, dimensions={0} | all-to-all | bytes 589824 | tf_op jit(solution)/shard_map/all_to_all | solution.py:225
  57.3 0.8 shard_map.53
  58.0 11.8 %all-to-all-start.3 = ((f32[64,4,384]{2,1,0:T(4,128)}), f32[64,4,384]{2,1,0:T(4,128)S(1)}, u32[]{:S(2)}, u32[]{:S(2)}) async-start(f32[64,4,384]{2,1,0:T(4,128)} %shard_map.53), calls=%async_computation.3 | async-start | bytes 786432 | tf_op jit(solution)/shard_map/all_to_all | solution.py:227
  69.9 7.1 %shard_map.54.inv_ref = f32[4,96,128]{2,1,0:T(8,128)S(1)} custom-call(f32[8,24,384]{2,1,0:T(8,128)S(1)} %all_to_all.27.got_ref), custom_call_target="tpu_custom_call" | custom-call | flops 10000000000 | bytes 40000000 | tf_op jit(solution)/shard_map/pallas_call | solution.py:34
  77.0 8.6 %all-to-all-done.3.got_ref = f32[64,4,384]{2,1,0:T(4,128)S(1)} async-done(((f32[64,4,384]{2,1,0:T(4,128)}), f32[64,4,384]{2,1,0:T(4,128)S(1)}, u32[]{:S(2)}, u32[]{:S(2)}) %all-to-all-start.3) | async-done | bytes 393248 | tf_op jit(solution)/shard_map/all_to_all | solution.py:227
  85.6 0.5 shard_map.55
  86.1 9.0 %all_to_all.28.got_ref = f32[8,4,128]{2,1,0:T(4,128)S(1)} all-to-all(f32[8,4,128]{2,1,0:T(4,128)S(1)} %get-tuple-element.4), channel_id=1, replica_groups=mesh['ia'=16,'ja'=8,'ka'=4] {'ja'}, dimensions={0} | all-to-all | bytes 32768 | tf_op jit(solution)/shard_map/all_to_all | solution.py:231
  95.1 0.6 shard_map.56
Async XLA Ops:
  0.6 0.8 copy-start.1
  1.5 0.8 copy-start.2
  2.2 40.9 %copy-start = (f32[32,128,128]{2,1,0:T(8,128)S(1)}, f32[32,128,128]{2,1,0:T(8,128)}, u32[]{:S(2)}) copy-start(f32[32,128,128]{2,1,0:T(8,128)} %t_ref.1) | copy-start | bytes 6291460
  58.0 27.5 %all-to-all-start.3 = ((f32[64,4,384]{2,1,0:T(4,128)}), f32[64,4,384]{2,1,0:T(4,128)S(1)}, u32[]{:S(2)}, u32[]{:S(2)}) async-start(f32[64,4,384]{2,1,0:T(4,128)} %shard_map.53), calls=%async_computation.3 | async-start | bytes 786432 | tf_op jit(solution)/shard_map/all_to_all | solution.py:227

commit v7 on v4

--- a/solution.py
+++ b/solution.py
@@ -73,44 +73,48 @@
             out_ref[p, nc : nc + third, q * 128 : (q + 1) * 128] = z_ref[at : at + third, :]
 
 
-def contract(t_hbm, c_got_ref, b_ref, out_ref, share_ref, t_ref, sems):
+def contract(t_hbm, c_got_ref, b_ref, out_ref, t_ref, m_ref, z_ref, sems):
     ni, nj, nk = t_ref.shape
     steps = sems.shape[0]
     group = ni // steps
     parts = [pl.ds(n * group, group) for n in range(steps)]
     copies = [pltpu.make_async_copy(t_hbm.at[p], t_ref.at[p], sems.at[n]) for n, p in enumerate(parts)]
-    for copy in copies:
-        copy.start()
+    copies[0].start()
+    copies[1].start()
     nc = nk // c_got_ref.shape[0]
-    share_ref[...] = jnp.sum(c_got_ref[:, nc:, :], axis=0)
+    share = jnp.sum(c_got_ref[:, nc:, :], axis=0)
+    third = share.shape[0]
+    for q in range(3):
+        z_ref[third * q : third * (q + 1), :] = share[:, q * 128 : (q + 1) * 128]
+    for p in range(ni):
+        at = 12 * (p % (third // 4))
+        out_ref[p, 0:12, :] = z_ref[at : at + 12, :]
+    out_ref[:, 15, :] = jnp.zeros((ni, 128), f32)
     c = c_got_ref[:, 0:nc, :].reshape(nk, W)
     b = b_ref[...]
     c_high = c.astype(bf16)
     c_low = (c - c_high.astype(f32)).astype(bf16)
     twice = jnp.concatenate([c_high, c_high], axis=0)
-    each = out_ref.shape[1]
     for n in range(steps):
         copies[n].wait()
+        if n + 2 < steps:
+            copies[n + 2].start()
         at = n * group
         t = t_ref[at : at + group, :, :].reshape(group * nj, nk)
         t_high = t.astype(bf16)
         t_low = (t - t_high.astype(f32)).astype(bf16)
         both = jnp.concatenate([t_high, t_low], axis=1)
         value = dot(both, twice, ((1,), (0,)), None) + dot(t_high, c_low, ((1,), (0,)), None)
-        value = jnp.sum(value.reshape(group, nj, W) * b[None], axis=1)
-        for p in range(group // each):
-            out_ref[at // each + p] = value[p * each : (p + 1) * each]
-
-
-def mix(m_ref, share_ref, out_ref):
-    depth, each = share_ref.shape[0], m_ref.shape[1]
-    out_ref[0:depth, :] = share_ref[...]
-    out_ref[depth : depth + each, :] = jnp.sum(m_ref[...], axis=0)
-    out_ref[depth + each :, :] = jnp.zeros((out_ref.shape[0] - depth - each, W), f32)
-
-
-def spread(x_ref, out_ref):
-    out_ref[...] = jnp.broadcast_to(x_ref[...][None], out_ref.shape)
+        m_ref[at : at + group, :] = jnp.sum(value.reshape(group, nj, W) * b[None], axis=1)
+    for q in range(3):
+        out_ref[:, 12 + q, :] = m_ref[:, q * 128 : (q + 1) * 128]
+
+
+def total(got_ref, out_ref):
+    ka = lax.axis_size("ka")
+    share = jnp.sum(got_ref[pl.ds(lax.axis_index("ja") * ka, ka), 0:12, :], axis=0)
+    out_ref[:, 0:12, :] = jnp.broadcast_to(share[None], (out_ref.shape[0], 12, 128))
+    out_ref[:, 12:16, :] = jnp.broadcast_to(jnp.sum(got_ref[:, 12:16, :], axis=0)[None], (out_ref.shape[0], 4, 128))
 
 
 def wide(v):
@@ -155,17 +159,13 @@
 
 
 def solve(got_ref, own_ref, out_ref, raw_ref, z_ref, m_ref):
-    peers = got_ref.shape[0]
-    third = S * R // peers // 3
-    each = m_ref.shape[0] // peers - 1
-    for p in range(peers):
-        m_ref[each * p : each * (p + 1), :] = got_ref[p, third : third + each, :]
-        for q in range(3):
-            at = (3 * p + q) * third
-            z_ref[at : at + third, :] = got_ref[p, 0:third, q * 128 : (q + 1) * 128]
-    count = each * peers
-    mine = own_ref[pl.ds(third + lax.axis_index("ka"), 1), :]
-    m_ref[count:, :] = jnp.broadcast_to(mine, (m_ref.shape[0] - count, W))
+    count = got_ref.shape[0]
+    for p in range(count):
+        z_ref[12 * p : 12 * (p + 1), :] = got_ref[p, 0:12, :]
+    for q in range(3):
+        at = slice(q * 128, (q + 1) * 128)
+        m_ref[0:count, at] = got_ref[:, 12 + q, :]
+        m_ref[count:, at] = jnp.broadcast_to(own_ref[0, 12 + q : 13 + q, :], (m_ref.shape[0] - count, 128))
     lane, row = lanes((R, 128)), rows((R, 128))
     fill = jnp.zeros((128 - R, 128), f32)
     blocks = []
@@ -209,7 +209,6 @@
     ia, ja, ka = (lax.axis_size(a) for a in ("ia", "ja", "ka"))
     nb, nc = factor_b.shape[0], factor_c.shape[0]
     third = S * R // ja // 3
-    each = ni // ja
     grams = pltpu.VMEM((S * R, 128), f32)
     slots_c, b_flat = call(
         prepare,
@@ -220,17 +219,17 @@
     )(factor_b, factor_c)
     got_c = lax.all_to_all(slots_c, "ja", 0, 0)
     b_block = lax.all_gather(b_flat, "ka", axis=0, tiled=True)
-    slots_m, share = call(
+    slots_m = call(
         contract,
-        [(ja, each, W), (third, W)],
-        scratch=[pltpu.VMEM(tensor.shape, f32), pltpu.SemaphoreType.DMA((4,))],
+        [(ja * ka, 16, 128)],
+        scratch=[pltpu.VMEM(v, f32) for v in (tensor.shape, (ni, W), (3 * third, 128))] + [pltpu.SemaphoreType.DMA((8,))],
         hbm=1,
         limit=52,
-    )(tensor, got_c, b_block)
-    got_m = lax.all_to_all(slots_m, "ja", 0, 0)
-    sums = lax.psum(call(mix, [(third + 8, W)])(got_m, share)[0], "ka")
-    got_all = lax.all_to_all(call(spread, [(ja, third + 8, W)])(sums)[0], "ja", 0, 0)
-    squares, raw = call(solve, [(ia, S, 128), (S, 128)], scratch=[grams, pltpu.VMEM((ni + ja, W), f32)])(got_all, sums)
+    )(tensor, got_c, b_block)[0]
+    got_m = lax.all_to_all(slots_m, ("ja", "ka"), 0, 0)
+    own = call(total, [(ja * ka, 16, 128)])(got_m)[0]
+    got_all = lax.all_to_all(own, ("ja", "ka"), 0, 0)
+    squares, raw = call(solve, [(ia, S, 128), (S, 128)], scratch=[grams, pltpu.VMEM((ni + 8, W), f32)])(got_all, own)
     got_s = lax.all_to_all(squares, "ia", 0, 0)
     return tuple(call(finish_of(ni * ia), [(1, S, R), (S, R)])(got_s, raw))
 

time: 105 us -> 97.5 us (0.929)
  blocking collectives: 80 us -> 71.8 us
    psum x1 -> x0, blocking collectives: 15.7 us -> none  [shards(): sums = lax.psum(call(mix, [(third + 8, W)])(got_m, share)[0], 'ka')]
    all_to_all x2, blocking collectives: 25.4 us -> 37.4 us  [the longest x1 21.5 us: shards(): got_m = lax.all_to_all(slots_m, ('ja', 'ka'), 0, 0)]
    all_to_all x1, blocking collectives: 21.5 us -> 17 us  [shards(): got_s = lax.all_to_all(squares, 'ia', 0, 0)]
    pallas_call x6 -> x5, Pallas kernels: 16 us -> 16.9 us  [run(): pl.pallas_call(body, out_shape=shapes, in_specs=[HBM] * hbm + [VMEM] * (l...]
where the time goes in v7:
time: 97.5 us; the launch traced here: 97 us
  blocking collectives  71.8 us (74%)
  Pallas kernels  16.9 us (17%)
  starting transfers between devices  7.66 us (8%)
    all_to_all x1, blocking collectives, shards(): got_m = lax.all_to_all(slots_m, ('ja', 'ka'), 0, 0)  21.5 us
    all_gather x1, blocking collectives, shards(): b_block = lax.all_gather(b_flat, 'ka', axis=0, tiled=True)  17.4 us
    all_to_all x1, blocking collectives, shards(): got_s = lax.all_to_all(squares, 'ia', 0, 0)  17 us
    pallas_call x5, Pallas kernels, run(): pl.pallas_call(body, out_shape=shapes, in_specs=[HBM] * hbm + [VMEM] * (l...  16.9 us
    all_to_all x1, blocking collectives, shards(): got_all = lax.all_to_all(own, ('ja', 'ka'), 0, 0)  15.9 us
    all_to_all x1, starting transfers between devices, shards(): got_c = lax.all_to_all(slots_c, 'ja', 0, 0)  7.66 us
  transfers between devices with their start and end apart: 1, of which 0 were waited for; matrix products, arithmetic and copies ran while one was open for 0% of the time, Pallas kernels for 0%

profile of v7, /device:TPU:1, one launch (start us, length us, event | category | flops | bytes accessed | tf_op | source)
XLA Modules:
  0.0 97.0 jit_solution(7499536625632843721)
XLA Ops:
  0.6 2.2 %shard_map.50 = (f32[8,32,384]{2,1,0:T(8,128)}, f32[32,384]{1,0:T(8,128)}) custom-call(f32[32,4,96]{2,1,0:T(4,128)} %fb_hbm.1, f32[16,4,96]{2,1,0:T(4,128)} %fc_hbm.1), custom_call_target="tpu_custom_call" | custom-call | tf_op jit(solution)/shard_map/pallas_call | solution.py:35
  2.8 7.7 %all-to-all-start = ((f32[8,32,384]{2,1,0:T(8,128)}), f32[8,32,384]{2,1,0:T(8,128)S(1)}, u32[]{:S(2)}, u32[]{:S(2)}) async-start(f32[8,32,384]{2,1,0:T(8,128)} %get-tuple-element.6), calls=%async_computation | async-start | bytes 786432 | tf_op jit(solution)/shard_map/all_to_all | solution.py:220
  10.5 17.4 %all_gather.3.b_ref = f32[128,384]{1,0:T(8,128)S(1)} all-gather(f32[32,384]{1,0:T(8,128)} %get-tuple-element.7), channel_id=1, replica_groups=mesh['ia'=16,'ja'=8,'ka'=4] {'ka'}, dimensions={0}, use_global_device_ids=true | all-gather | bytes 245760 | tf_op jit(solution)/shard_map/all_gather | solution.py:221
  27.8 0.0 all-to-all-done.c_got_ref
  27.8 4.8 %shard_map.51 = f32[32,16,128]{2,1,0:T(8,128)S(1)} custom-call(f32[32,128,128]{2,1,0:T(8,128)} %t_hbm.1, f32[8,32,384]{2,1,0:T(8,128)S(1)} %all-to-all-done.c_got_ref, f32[128,384]{1,0:T(8,128)S(1)} %all_gather.3.b_ref), custom_call_target="tpu_custom_call" | custom-call | tf_op jit(solution)/shard_map/pallas_call | solution.py:35
  32.7 21.5 %all_to_all.20.got_ref = f32[32,16,128]{2,1,0:T(8,128)S(1)} all-to-all(f32[32,16,128]{2,1,0:T(8,128)S(1)} %shard_map.51), channel_id=1, replica_groups=mesh['ia'=16,'ja'=8,'ka'=4] {'ja','ka'}, dimensions={0} | all-to-all | bytes 524288 | tf_op jit(solution)/shard_map/all_to_all | solution.py:229
  54.2 15.9 %all_to_all.21.got_ref = f32[32,16,128]{2,1,0:T(8,128)S(1)} all-to-all(f32[32,16,128]{2,1,0:T(8,128)S(1)} %shard_map.52.own_ref), channel_id=1, replica_groups=mesh['ia'=16,'ja'=8,'ka'=4] {'ja','ka'}, dimensions={0} | all-to-all | bytes 524288 | tf_op jit(solution)/shard_map/all_to_all | solution.py:231
  70.2 9.3 %shard_map.53 = (f32[16,4,128]{2,1,0:T(4,128)S(1)}, f32[4,128]{1,0:T(4,128)S(1)}) custom-call(f32[32,16,128]{2,1,0:T(8,128)S(1)} %all_to_all.21.got_ref, f32[32,16,128]{2,1,0:T(8,128)S(1)} %shard_map.52.own_ref), custom_call_target="tpu_custom_call" | custom-call | tf_op jit(solution)/shard_map/pallas_call | solution.py:35
  79.4 17.0 %all_to_all.22.got_ref = f32[16,4,128]{2,1,0:T(4,128)S(1)} all-to-all(f32[16,4,128]{2,1,0:T(4,128)S(1)} %get-tuple-element.8), channel_id=1, replica_groups=mesh['ia'=16,'ja'=8,'ka'=4] {'ia'}, dimensions={0} | all-to-all | bytes 65536 | tf_op jit(solution)/shard_map/all_to_all | solution.py:233
  96.4 0.6 shard_map.54
  (1 shorter events, 0.0 us)
Async XLA Ops:
  2.8 25.0 %all-to-all-start = ((f32[8,32,384]{2,1,0:T(8,128)}), f32[8,32,384]{2,1,0:T(8,128)S(1)}, u32[]{:S(2)}, u32[]{:S(2)}) async-start(f32[8,32,384]{2,1,0:T(8,128)} %get-tuple-element.6), calls=%async_computation | async-start | bytes 786432 | tf_op jit(solution)/shard_map/all_to_all | solution.py:220

commit v8 on v4

--- a/solution.py
+++ b/solution.py
@@ -73,44 +73,46 @@
             out_ref[p, nc : nc + third, q * 128 : (q + 1) * 128] = z_ref[at : at + third, :]
 
 
-def contract(t_hbm, c_got_ref, b_ref, out_ref, share_ref, t_ref, sems):
+def middle(got_ref, out_ref):
+    depth = out_ref.shape[1]
+    share = jnp.sum(got_ref[:, got_ref.shape[1] - depth :, :], axis=0)
+    out_ref[...] = jnp.broadcast_to(share[None], out_ref.shape)
+
+
+def contract(t_ref, c_got_ref, b_ref, out_ref):
     ni, nj, nk = t_ref.shape
-    steps = sems.shape[0]
-    group = ni // steps
-    parts = [pl.ds(n * group, group) for n in range(steps)]
-    copies = [pltpu.make_async_copy(t_hbm.at[p], t_ref.at[p], sems.at[n]) for n, p in enumerate(parts)]
-    for copy in copies:
-        copy.start()
-    nc = nk // c_got_ref.shape[0]
-    share_ref[...] = jnp.sum(c_got_ref[:, nc:, :], axis=0)
-    c = c_got_ref[:, 0:nc, :].reshape(nk, W)
+    c = c_got_ref[:, 0 : nk // c_got_ref.shape[0], :].reshape(nk, W)
     b = b_ref[...]
     c_high = c.astype(bf16)
     c_low = (c - c_high.astype(f32)).astype(bf16)
     twice = jnp.concatenate([c_high, c_high], axis=0)
-    each = out_ref.shape[1]
-    for n in range(steps):
-        copies[n].wait()
-        at = n * group
+    group = 8
+    for at in range(0, ni, group):
         t = t_ref[at : at + group, :, :].reshape(group * nj, nk)
         t_high = t.astype(bf16)
         t_low = (t - t_high.astype(f32)).astype(bf16)
         both = jnp.concatenate([t_high, t_low], axis=1)
         value = dot(both, twice, ((1,), (0,)), None) + dot(t_high, c_low, ((1,), (0,)), None)
-        value = jnp.sum(value.reshape(group, nj, W) * b[None], axis=1)
-        for p in range(group // each):
-            out_ref[at // each + p] = value[p * each : (p + 1) * each]
-
-
-def mix(m_ref, share_ref, out_ref):
-    depth, each = share_ref.shape[0], m_ref.shape[1]
-    out_ref[0:depth, :] = share_ref[...]
-    out_ref[depth : depth + each, :] = jnp.sum(m_ref[...], axis=0)
-    out_ref[depth + each :, :] = jnp.zeros((out_ref.shape[0] - depth - each, W), f32)
-
-
-def spread(x_ref, out_ref):
-    out_ref[...] = jnp.broadcast_to(x_ref[...][None], out_ref.shape)
+        out_ref[at : at + group, :] = jnp.sum(value.reshape(group, nj, W) * b[None], axis=1)
+
+
+def pack(m_ref, z_got_ref, out_ref):
+    share = jnp.sum(z_got_ref[...], axis=0)
+    depth = share.shape[0]
+    each = m_ref.shape[0] // out_ref.shape[0]
+    pad = jnp.zeros((out_ref.shape[1] - depth - each, W), f32)
+    for p in range(out_ref.shape[0]):
+        out_ref[p, 0:depth, :] = share
+        out_ref[p, depth : depth + each, :] = m_ref[each * p : each * (p + 1), :]
+        out_ref[p, depth + each :, :] = pad
+
+
+def rows_of(first):
+    def sum_rows(got_ref, out_ref):
+        each = out_ref.shape[1]
+        out_ref[...] = jnp.broadcast_to(jnp.sum(got_ref[:, first : first + each, :], axis=0)[None], out_ref.shape)
+
+    return sum_rows
 
 
 def wide(v):
@@ -154,18 +156,12 @@
     return scale
 
 
-def solve(got_ref, own_ref, out_ref, raw_ref, z_ref, m_ref):
-    peers = got_ref.shape[0]
-    third = S * R // peers // 3
-    each = m_ref.shape[0] // peers - 1
-    for p in range(peers):
-        m_ref[each * p : each * (p + 1), :] = got_ref[p, third : third + each, :]
+def invert(got_ref, out_ref, z_ref):
+    third = S * R // got_ref.shape[0] // 3
+    for p in range(got_ref.shape[0]):
         for q in range(3):
             at = (3 * p + q) * third
             z_ref[at : at + third, :] = got_ref[p, 0:third, q * 128 : (q + 1) * 128]
-    count = each * peers
-    mine = own_ref[pl.ds(third + lax.axis_index("ka"), 1), :]
-    m_ref[count:, :] = jnp.broadcast_to(mine, (m_ref.shape[0] - count, W))
     lane, row = lanes((R, 128)), rows((R, 128))
     fill = jnp.zeros((128 - R, 128), f32)
     blocks = []
@@ -183,12 +179,23 @@
     for k in range(0, R, 4):
         for s in range(S):
             scale[s] = eliminate(blocks[s], scale[s], k, 4, lane8, row8)
-    squares = []
     for s in range(S):
         w = jnp.concatenate(blocks[s], axis=0)
         w = jnp.where(lane == row, 1.0, jnp.where(lane < row, w, 0.0))
-        half = dot(m_ref[:, s * R : (s + 1) * R], w[:, 0:R], ((1,), (1,))) * scale[s][0:1, 0:R]
-        raw = dot(half, w, ((1,), (0,)))
+        inv = jnp.sum(jnp.where(lane == row, scale[s][0:1], 0.0), axis=1, keepdims=True)
+        out_ref[s] = dot(w[:, 0:R], w * inv, ((0,), (0,)))
+
+
+def solve(got_ref, own_ref, inv_ref, out_ref, raw_ref, m_ref):
+    each = got_ref.shape[1]
+    count = m_ref.shape[0] - 8
+    for p in range(got_ref.shape[0]):
+        m_ref[each * p : each * (p + 1), :] = got_ref[p]
+    mine = own_ref[0, pl.ds(lax.axis_index("ka"), 1), :]
+    m_ref[count:, :] = jnp.broadcast_to(mine, (8, W))
+    squares = []
+    for s in range(S):
+        raw = dot(m_ref[:, s * R : (s + 1) * R], inv_ref[s], ((1,), (0,)))
         squares.append(jnp.sum(raw[0:count] * raw[0:count], axis=0, keepdims=True))
         raw_ref[s : s + 1, :] = raw[count : count + 1]
     out_ref[...] = jnp.broadcast_to(jnp.concatenate(squares, axis=0)[None], out_ref.shape)
@@ -202,6 +209,10 @@
         fa_ref[0] = (raw_ref[...] / weights)[:, 0:R]
 
     return finish
+
+
+def work(flops, nbytes):
+    return pl.CostEstimate(flops=int(flops), bytes_accessed=int(nbytes), transcendentals=0)
 
 
 def shards(tensor, factor_b, factor_c):
@@ -220,17 +231,14 @@
     )(factor_b, factor_c)
     got_c = lax.all_to_all(slots_c, "ja", 0, 0)
     b_block = lax.all_gather(b_flat, "ka", axis=0, tiled=True)
-    slots_m, share = call(
-        contract,
-        [(ja, each, W), (third, W)],
-        scratch=[pltpu.VMEM(tensor.shape, f32), pltpu.SemaphoreType.DMA((4,))],
-        hbm=1,
-        limit=52,
-    )(tensor, got_c, b_block)
-    got_m = lax.all_to_all(slots_m, "ja", 0, 0)
-    sums = lax.psum(call(mix, [(third + 8, W)])(got_m, share)[0], "ka")
-    got_all = lax.all_to_all(call(spread, [(ja, third + 8, W)])(sums)[0], "ja", 0, 0)
-    squares, raw = call(solve, [(ia, S, 128), (S, 128)], scratch=[grams, pltpu.VMEM((ni + ja, W), f32)])(got_all, sums)
+    got_z = lax.all_to_all(call(middle, [(ka, third, W)])(got_c)[0], "ka", 0, 0)
+    m_part = call(contract, [(ni, W)], cost=work(2e9, 4e6))(tensor, got_c, b_block)[0]
+    got_m = lax.all_to_all(call(pack, [(ja, third + 8, W)])(m_part, got_z)[0], "ja", 0, 0)
+    got_k = lax.all_to_all(call(rows_of(third), [(ka, each, W)])(got_m)[0], "ka", 0, 0)
+    own = call(rows_of(0), [(ja, each, W)])(got_k)[0]
+    got_j = lax.all_to_all(own, "ja", 0, 0)
+    inverse = call(invert, [(S, R, 128)], cost=work(1e10, 4e7), scratch=[grams])(got_m)[0]
+    squares, raw = call(solve, [(ia, S, 128), (S, 128)], scratch=[pltpu.VMEM((ni + 8, W), f32)])(got_j, own, inverse)
     got_s = lax.all_to_all(squares, "ia", 0, 0)
     return tuple(call(finish_of(ni * ia), [(1, S, R), (S, R)])(got_s, raw))
 

time: 105 us -> 98.6 us (0.939)
  blocking collectives: 80 us -> 59.8 us
  starting transfers between devices: 7.66 us -> 17.8 us
  waiting for transfers between devices: 0.01 us -> 3.66 us
  Pallas kernels: 16 us -> 14.4 us
  local copies, waits for them, and re-layouts: 0 us -> 1.59 us
    psum x1 -> x0, blocking collectives: 15.7 us -> none  [shards(): sums = lax.psum(call(mix, [(third + 8, W)])(got_m, share)[0], 'ka')]
    all_to_all x0 -> x2, starting transfers between devices: none -> 10.2 us  [the longest x1 6.84 us: shards(): got_z = lax.all_to_all(call(middle, [(ka, third, W)])(got_c)[0], 'ka', 0, 0)]
    all_to_all x0 -> x2, waiting for transfers between devices: none -> 3.66 us  [the longest x1 3.66 us: shards(): got_z = lax.all_to_all(call(middle, [(ka, third, W)])(got_c)[0], 'ka', 0, 0)]
    all_to_all x1, blocking collectives: 21.5 us -> 19 us  [shards(): got_s = lax.all_to_all(squares, 'ia', 0, 0)]
    all_to_all x2, blocking collectives: 25.4 us -> 23.4 us  [the longest x1 13.9 us: shards(): lax.all_to_all(call(pack, [(ja, third + 8, W)])(m_part, got_z)[0], 'ja',...]
    unnamed x0 -> x2, local copies, waits for them, and re-layouts: none -> 1.59 us
    pallas_call x6 -> x9, Pallas kernels: 16 us -> 14.4 us  [run(): pl.pallas_call(body, out_shape=shapes, in_specs=[HBM] * hbm + [VMEM] * (l...]
  transfers between devices with their start and end apart: 1 -> 3, of which waited for: 0 -> 1; matrix products, arithmetic and copies ran while one was open for 0% -> 0% of each run, Pallas kernels for 0% -> 9%
where the time goes in v8:
time: 98.6 us; the launch traced here: 98 us
  blocking collectives  59.8 us (61%)
  starting transfers between devices  17.8 us (18%)
  Pallas kernels  14.4 us (15%)
  waiting for transfers between devices  3.66 us (4%)
  local copies, waits for them, and re-layouts  1.59 us (2%)
    all_to_all x1, blocking collectives, shards(): got_s = lax.all_to_all(squares, 'ia', 0, 0)  19 us
    all_gather x1, blocking collectives, shards(): b_block = lax.all_gather(b_flat, 'ka', axis=0, tiled=True)  17.4 us
    pallas_call x9, Pallas kernels, run(): pl.pallas_call(body, out_shape=shapes, in_specs=[HBM] * hbm + [VMEM] * (l...  14.4 us
    all_to_all x1, blocking collectives, shards(): lax.all_to_all(call(pack, [(ja, third + 8, W)])(m_part, got_z)[0], 'ja',...  13.9 us
    all_to_all x1, blocking collectives, shards(): lax.all_to_all(call(rows_of(third), [(ka, each, W)])(got_m)[0], 'ka', 0, 0)  9.51 us
    all_to_all x1, starting transfers between devices, shards(): got_c = lax.all_to_all(slots_c, 'ja', 0, 0)  7.66 us
    all_to_all x1, starting transfers between devices, shards(): got_z = lax.all_to_all(call(middle, [(ka, third, W)])(got_c)[0], 'ka', 0, 0)  6.84 us
    all_to_all x1, waiting for transfers between devices, shards(): got_z = lax.all_to_all(call(middle, [(ka, third, W)])(got_c)[0], 'ka', 0, 0)  3.66 us
  transfers between devices with their start and end apart: 3, of which 1 were waited for; matrix products, arithmetic and copies ran while one was open for 0% of the time, Pallas kernels for 9%

profile of v8, /device:TPU:1, one launch (start us, length us, event | category | flops | bytes accessed | tf_op | source)
XLA Modules:
  0.0 98.0 jit_solution(17419142257767257722)
XLA Ops:
  0.6 2.2 %shard_map.50 = (f32[8,32,384]{2,1,0:T(8,128)}, f32[32,384]{1,0:T(8,128)}) custom-call(f32[32,4,96]{2,1,0:T(4,128)} %fb_hbm.1, f32[16,4,96]{2,1,0:T(4,128)} %fc_hbm.1), custom_call_target="tpu_custom_call" | custom-call | tf_op jit(solution)/shard_map/pallas_call | solution.py:35
  2.8 7.7 %all-to-all-start = ((f32[8,32,384]{2,1,0:T(8,128)}), f32[8,32,384]{2,1,0:T(8,128)S(1)}, u32[]{:S(2)}, u32[]{:S(2)}) async-start(f32[8,32,384]{2,1,0:T(8,128)} %get-tuple-element.6), calls=%async_computation | async-start | bytes 786432 | tf_op jit(solution)/shard_map/all_to_all | solution.py:232
  10.5 17.4 %all_gather.3.b_ref = f32[128,384]{1,0:T(8,128)S(1)} all-gather(f32[32,384]{1,0:T(8,128)} %get-tuple-element.7), channel_id=1, replica_groups=mesh['ia'=16,'ja'=8,'ka'=4] {'ka'}, dimensions={0}, use_global_device_ids=true | all-gather | bytes 245760 | tf_op jit(solution)/shard_map/all_gather | solution.py:233
  27.8 0.0 all-to-all-done.c_got_ref.got_ref
  27.8 0.6 shard_map.52
  28.5 6.8 %all-to-all-start.1 = ((f32[4,16,384]{2,1,0:T(8,128)}), f32[4,16,384]{2,1,0:T(8,128)S(1)}, u32[]{:S(2)}, u32[]{:S(2)}) async-start(f32[4,16,384]{2,1,0:T(8,128)} %shard_map.52), calls=%async_computation.1 | async-start | bytes 196608 | tf_op jit(solution)/shard_map/all_to_all | solution.py:234
  35.3 0.0 copy-start
  35.3 1.6 %copy-done = f32[32,128,128]{2,1,0:T(8,128)S(1)} copy-done((f32[32,128,128]{2,1,0:T(8,128)S(1)}, f32[32,128,128]{2,1,0:T(8,128)}, u32[]{:S(2)}) %copy-start) | copy-done | bytes 2097176
  36.9 2.1 %shard_map.51.m_ref = f32[32,384]{1,0:T(8,128)S(1)} custom-call(f32[32,128,128]{2,1,0:T(8,128)S(1)} %copy-done, f32[8,32,384]{2,1,0:T(8,128)S(1)} %all-to-all-done.c_got_ref.got_ref, f32[128,384]{1,0:T(8,128)S(1)} %all_gather.3.b_ref), custom_call_target="tpu_custom_call" | custom-call | flops 2000000000 | bytes 4000000 | tf_op jit(solution)/shard_map/pallas_call | solution.py:35
  39.0 3.7 %all-to-all-done.1.z_got_ref = f32[4,16,384]{2,1,0:T(8,128)S(1)} async-done(((f32[4,16,384]{2,1,0:T(8,128)}), f32[4,16,384]{2,1,0:T(8,128)S(1)}, u32[]{:S(2)}, u32[]{:S(2)}) %all-to-all-start.1) | async-done | bytes 98336 | tf_op jit(solution)/shard_map/all_to_all | solution.py:234
  42.7 13.9 %all_to_all.30.got_ref = f32[8,24,384]{2,1,0:T(8,128)S(1)} all-to-all(f32[8,24,384]{2,1,0:T(8,128)S(1)} %shard_map.53), channel_id=1, replica_groups=mesh['ia'=16,'ja'=8,'ka'=4] {'ja'}, dimensions={0} | all-to-all | bytes 589824 | tf_op jit(solution)/shard_map/all_to_all | solution.py:236
  56.6 9.5 %all_to_all.31.got_ref = f32[4,4,384]{2,1,0:T(4,128)S(1)} all-to-all(f32[4,4,384]{2,1,0:T(4,128)S(1)} %shard_map.54), channel_id=1, replica_groups=mesh['ia'=16,'ja'=8,'ka'=4] {'ka'}, dimensions={0} | all-to-all | bytes 49152 | tf_op jit(solution)/shard_map/all_to_all | solution.py:237
  66.2 0.6 shard_map.55.own_ref
  66.8 3.3 %all-to-all-start.4 = ((f32[8,4,384]{2,1,0:T(4,128)}), f32[8,4,384]{2,1,0:T(4,128)S(1)}, u32[]{:S(2)}, u32[]{:S(2)}) async-start(f32[8,4,384]{2,1,0:T(4,128)} %shard_map.55.own_ref), calls=%async_computation.4 | async-start | bytes 98304 | tf_op jit(solution)/shard_map/all_to_all | solution.py:239
  70.1 7.1 %shard_map.56.inv_ref = f32[4,96,128]{2,1,0:T(8,128)S(1)} custom-call(f32[8,24,384]{2,1,0:T(8,128)S(1)} %all_to_all.30.got_ref), custom_call_target="tpu_custom_call" | custom-call | flops 10000000000 | bytes 40000000 | tf_op jit(solution)/shard_map/pallas_call | solution.py:35
  77.2 0.0 all-to-all-done.4.got_ref
  77.3 1.2 %shard_map.57 = (f32[16,4,128]{2,1,0:T(4,128)S(1)}, f32[4,128]{1,0:T(4,128)S(1)}) custom-call(f32[8,4,384]{2,1,0:T(4,128)S(1)} %all-to-all-done.4.got_ref, f32[8,4,384]{2,1,0:T(4,128)} %shard_map.55.own_ref, f32[4,96,128]{2,1,0:T(8,128)S(1)} %shard_map.56.inv_ref), custom_call_target="tpu_custom_call" | custom-call | tf_op jit(solution)/shard_map/pallas_call | solution.py:35
  78.4 19.0 %all_to_all.32.got_ref = f32[16,4,128]{2,1,0:T(4,128)S(1)} all-to-all(f32[16,4,128]{2,1,0:T(4,128)S(1)} %get-tuple-element.8), channel_id=1, replica_groups=mesh['ia'=16,'ja'=8,'ka'=4] {'ia'}, dimensions={0} | all-to-all | bytes 65536 | tf_op jit(solution)/shard_map/all_to_all | solution.py:242
  97.4 0.6 shard_map.58
  (2 shorter events, 0.0 us)
Async XLA Ops:
  2.8 25.0 %all-to-all-start = ((f32[8,32,384]{2,1,0:T(8,128)}), f32[8,32,384]{2,1,0:T(8,128)S(1)}, u32[]{:S(2)}, u32[]{:S(2)}) async-start(f32[8,32,384]{2,1,0:T(8,128)} %get-tuple-element.6), calls=%async_computation | async-start | bytes 786432 | tf_op jit(solution)/shard_map/all_to_all | solution.py:232
  28.5 14.2 %all-to-all-start.1 = ((f32[4,16,384]{2,1,0:T(8,128)}), f32[4,16,384]{2,1,0:T(8,128)S(1)}, u32[]{:S(2)}, u32[]{:S(2)}) async-start(f32[4,16,384]{2,1,0:T(8,128)} %shard_map.52), calls=%async_computation.1 | async-start | bytes 196608 | tf_op jit(solution)/shard_map/all_to_all | solution.py:234
  35.3 1.6 %copy-start = (f32[32,128,128]{2,1,0:T(8,128)S(1)}, f32[32,128,128]{2,1,0:T(8,128)}, u32[]{:S(2)}) copy-start(f32[32,128,128]{2,1,0:T(8,128)} %t_ref.1) | copy-start | bytes 6291460
  66.8 10.5 %all-to-all-start.4 = ((f32[8,4,384]{2,1,0:T(4,128)}), f32[8,4,384]{2,1,0:T(4,128)S(1)}, u32[]{:S(2)}, u32[]{:S(2)}) async-start(f32[8,4,384]{2,1,0:T(4,128)} %shard_map.55.own_ref), calls=%async_computation.4 | async-start | bytes 98304 | tf_op jit(solution)/shard_map/all_to_all | solution.py:239

commit v9 on v5

--- a/solution.py
+++ b/solution.py
@@ -11,6 +11,7 @@
 
 R = 96
 S = 4
+HALF = 2
 W = S * R
 VMEM = pl.BlockSpec(memory_space=pltpu.VMEM)
 
@@ -44,9 +45,13 @@
     return run
 
 
+def half():
+    return lax.rem(lax.axis_index("ia"), 2)
+
+
 def prepare(fb_ref, fc_ref, out_ref, z_ref):
     nc = fc_ref.shape[0]
-    parts, depth = out_ref.shape[0], z_ref.shape[0] // out_ref.shape[0]
+    parts, depth = out_ref.shape[0], HALF * R // out_ref.shape[0]
     low = lanes((R, 128)) <= rows((R, 128))
     flat = []
     for s in range(S):
@@ -63,8 +68,8 @@
     for p in range(parts):
         out_ref[p, 0:nc, :] = c_flat
         for q in range(3):
-            at = p * depth + q * third
-            out_ref[p, nc : nc + third, q * 128 : (q + 1) * 128] = z_ref[at : at + third, :]
+            at = pl.multiple_of(half() * HALF * R + p * depth + q * third, 8)
+            out_ref[p, nc : nc + third, q * 128 : (q + 1) * 128] = z_ref[pl.ds(at, third), :]
 
 
 def middle(got_ref, fb_ref, out_ref, z_ref):
@@ -109,14 +114,15 @@
     share = b_got_ref[0, nb : nb + 8, :]
     for p in range(1, b_got_ref.shape[0]):
         share = share + b_got_ref[p, nb : nb + 8, :]
-    step = 4
+    step = HALF
     z = jnp.concatenate([share[0:step, q * 128 : (q + 1) * 128] for q in range(3)], axis=0)
     for p in range(out_ref.shape[0]):
         out_ref[p, 0 : 3 * step, :] = z
+        out_ref[p, 3 * step : 12, :] = jnp.zeros((12 - 3 * step, 128), f32)
     pad = jnp.zeros((ni, 128 - R), f32)
     for s in range(S):
         one = jnp.concatenate([m_ref[:, s * R : (s + 1) * R], pad], axis=1)
-        out_ref[:, 3 * step + s, :] = one
+        out_ref[:, 12 + s, :] = one
 
 
 def own_row(got_ref, out_ref):
@@ -167,11 +173,11 @@
 
 def invert(got_ref, out_ref, z_ref):
     for p in range(got_ref.shape[0]):
-        z_ref[12 * p : 12 * (p + 1), :] = got_ref[p, 0:12, :]
+        z_ref[6 * p : 6 * (p + 1), :] = got_ref[p, 0:6, :]
     lane, row = lanes((R, 128)), rows((R, 128))
     fill = jnp.zeros((128 - R, 128), f32)
     blocks = []
-    for s in range(S):
+    for s in range(HALF):
         z = z_ref[s * R : (s + 1) * R, :]
         low = jnp.where(lane <= row, z, 0.0)
         b_up = jnp.concatenate([low, fill], axis=0).T[0:R]
@@ -181,21 +187,21 @@
         full = up + jnp.concatenate([strict, fill], axis=0).T[0:R]
         blocks.append([full[8 * i : 8 * i + 8] for i in range(R // 8)])
     lane8, row8 = lanes((8, 128)), rows((8, 1))
-    scale = [jnp.zeros((8, 128), f32)] * S
+    scale = [jnp.zeros((8, 128), f32)] * HALF
     for k in range(0, R, 4):
-        for s in range(S):
+        for s in range(HALF):
             scale[s] = eliminate(blocks[s], scale[s], k, 4, lane8, row8)
-    for s in range(S):
+    for s in range(HALF):
         w = jnp.concatenate(blocks[s], axis=0)
         w = jnp.where(lane == row, 1.0, jnp.where(lane < row, w, 0.0))
         inv = jnp.sum(jnp.where(lane == row, scale[s][0:1], 0.0), axis=1, keepdims=True)
         out_ref[s] = dot(w[:, 0:R], w * inv, ((0,), (0,)))
 
 
-def solve(m_ref, own_ref, inv_ref, out_ref, raw_ref):
+def solve(m_ref, own_ref, mine_ref, other_ref, out_ref, raw_ref):
     squares = []
     for s in range(S):
-        inv = inv_ref[s]
+        inv = jnp.where(half() == s // HALF, mine_ref[s % HALF], other_ref[s % HALF])
         raw = dot(m_ref[:, s, 0:R], inv, ((1,), (0,)))
         squares.append(jnp.sum(raw * raw, axis=0, keepdims=True))
         raw_ref[s : s + 1, :] = dot(own_ref[0, :, 0:R], inv, ((1,), (0,)))[s : s + 1]
@@ -216,19 +222,20 @@
 def shards(tensor, factor_b, factor_c):
     ni = tensor.shape[0]
     ia, ja, ka = (lax.axis_size(a) for a in ("ia", "ja", "ka"))
-    depth = S * R // ja
+    depth = HALF * R // ja
+    cost = pl.CostEstimate(flops=int(1e10), bytes_accessed=int(4e7), transcendentals=0)
     grams = pltpu.VMEM((S * R, 128), f32)
     slots_c = call(prepare, [(ja, factor_c.shape[0] + depth // 3, W)], scratch=[grams])(factor_b, factor_c)[0]
     got_c = lax.all_to_all(slots_c, "ja", 0, 0)
-    slots_b = call(middle, [(ka, factor_b.shape[0] + 8, W)], scratch=[pltpu.VMEM((depth, 128), f32)])(got_c, factor_b)[0]
+    slots_b = call(middle, [(ka, factor_b.shape[0] + 8, W)], cost=cost, scratch=[pltpu.VMEM((depth, 128), f32)])(got_c, factor_b)[0]
     got_b = lax.all_to_all(slots_b, "ka", 0, 0)
     slots_m = call(contract, [(ja * ka, 16, 128)], scratch=[pltpu.VMEM((ni, W), f32)])(tensor, got_c, got_b)[0]
     got_m = lax.all_to_all(slots_m, ("ja", "ka"), 0, 0)
     own = call(own_row, [(ja * ka, S, 128)])(got_m)[0]
     all_rows = lax.all_to_all(own, ("ja", "ka"), 0, 0)
-    cost = pl.CostEstimate(flops=int(1e10), bytes_accessed=int(4e7), transcendentals=0)
-    inverse = call(invert, [(S, R, 128)], cost=cost, scratch=[grams])(got_m)[0]
-    squares, raw = call(solve, [(ia, S, 128), (S, 128)])(all_rows, own, inverse)
+    inverse = call(invert, [(HALF, R, 128)], cost=cost, scratch=[grams])(got_m)[0]
+    other = lax.ppermute(inverse, "ia", [(n, n ^ 1) for n in range(ia)])
+    squares, raw = call(solve, [(ia, S, 128), (S, 128)])(all_rows, own, inverse, other)
     got_s = lax.all_to_all(squares, "ia", 0, 0)
     return tuple(call(finish_of(ni * ia), [(1, S, R), (S, R)])(got_s, raw))
 

time: 95.1 us -> 93.5 us (0.983)
  starting transfers between devices: 6.51 us -> 9.89 us
  waiting for transfers between devices: 4.06 us -> 1.85 us
  blocking collectives: 69.4 us -> 67.9 us
  Pallas kernels: 12.4 us -> 11 us
    ppermute x0 -> x1, starting transfers between devices: none -> 3.62 us  [shards(): other = lax.ppermute(inverse, 'ia', [(n, n ^ 1) for n in range(ia)])]
    all_to_all x1, waiting for transfers between devices: 4.06 us -> 0.93 us  [shards(): all_rows = lax.all_to_all(own, ('ja', 'ka'), 0, 0)]
    all_to_all x1, blocking collectives: 19.9 us -> 17.6 us  [shards(): got_c = lax.all_to_all(slots_c, 'ja', 0, 0)]
    pallas_call x7, Pallas kernels: 12.4 us -> 11 us  [run(): pl.pallas_call(body, out_shape=shapes, in_specs=[VMEM] * len(args), out_s...]
  transfers between devices with their start and end apart: 1 -> 2, of which waited for: 1 -> 2; matrix products, arithmetic and copies ran while one was open for 0% -> 0% of each run, Pallas kernels for 8% -> 6%
where the time goes in v9:
time: 93.5 us; the launch traced here: 93 us
  blocking collectives  67.9 us (73%)
  Pallas kernels  11 us (12%)
  starting transfers between devices  9.89 us (11%)
  waiting for transfers between devices  1.85 us (2%)
  local copies, waits for them, and re-layouts  1.59 us (2%)
    all_to_all x1, blocking collectives, shards(): got_b = lax.all_to_all(slots_b, 'ka', 0, 0)  19.5 us
    all_to_all x1, blocking collectives, shards(): got_c = lax.all_to_all(slots_c, 'ja', 0, 0)  17.6 us
    all_to_all x1, blocking collectives, shards(): got_m = lax.all_to_all(slots_m, ('ja', 'ka'), 0, 0)  17.4 us
    all_to_all x1, blocking collectives, shards(): got_s = lax.all_to_all(squares, 'ia', 0, 0)  13.4 us
    pallas_call x7, Pallas kernels, run(): pl.pallas_call(body, out_shape=shapes, in_specs=[VMEM] * len(args), out_s...  11 us
    all_to_all x1, starting transfers between devices, shards(): all_rows = lax.all_to_all(own, ('ja', 'ka'), 0, 0)  6.26 us
    ppermute x1, starting transfers between devices, shards(): other = lax.ppermute(inverse, 'ia', [(n, n ^ 1) for n in range(ia)])  3.62 us
  transfers between devices with their start and end apart: 2, of which 2 were waited for; matrix products, arithmetic and copies ran while one was open for 0% of the time, Pallas kernels for 6%

profile of v9, /device:TPU:1, one launch (start us, length us, event | category | flops | bytes accessed | tf_op | source)
XLA Modules:
  0.0 93.0 jit_solution(10257239131736308498)
XLA Ops:
  0.6 0.0 copy-start.1
  0.6 0.8 copy-done.1
  1.5 0.0 copy-start.2
  1.5 0.8 copy-done.2
  2.2 0.5 shard_map.50
  2.8 17.6 %all_to_all.25.got_ref.c_got_ref = f32[8,24,384]{2,1,0:T(8,128)S(1)} all-to-all(f32[8,24,384]{2,1,0:T(8,128)S(1)} %shard_map.50), channel_id=1, replica_groups=mesh['ia'=16,'ja'=8,'ka'=4] {'ja'}, dimensions={0} | all-to-all | bytes 589824 | tf_op jit(solution)/shard_map/all_to_all | solution.py:229
  20.4 0.0 copy-start
  20.4 0.1 shard_map.51
  20.5 19.5 %all_to_all.26.b_got_ref = f32[4,40,384]{2,1,0:T(8,128)S(1)} all-to-all(f32[4,40,384]{2,1,0:T(8,128)S(1)} %shard_map.51), channel_id=1, replica_groups=mesh['ia'=16,'ja'=8,'ka'=4] {'ka'}, dimensions={0} | all-to-all | bytes 491520 | tf_op jit(solution)/shard_map/all_to_all | solution.py:231
  40.0 0.0 copy-done
  40.0 2.2 %shard_map.52 = f32[32,16,128]{2,1,0:T(8,128)S(1)} custom-call(f32[32,128,128]{2,1,0:T(8,128)S(1)} %copy-done, f32[8,24,384]{2,1,0:T(8,128)S(1)} %all_to_all.25.got_ref.c_got_ref, f32[4,40,384]{2,1,0:T(8,128)S(1)} %all_to_all.26.b_got_ref), custom_call_target="tpu_custom_call" | custom-call | tf_op jit(solution)/shard_map/pallas_call | solution.py:35
  42.1 17.4 %all_to_all.27.got_ref = f32[32,16,128]{2,1,0:T(8,128)S(1)} all-to-all(f32[32,16,128]{2,1,0:T(8,128)S(1)} %shard_map.52), channel_id=1, replica_groups=mesh['ia'=16,'ja'=8,'ka'=4] {'ja','ka'}, dimensions={0} | all-to-all | bytes 524288 | tf_op jit(solution)/shard_map/all_to_all | solution.py:233
  59.6 0.7 shard_map.53.own_ref
  60.2 6.3 %all-to-all-start.3 = ((f32[32,4,128]{2,1,0:T(4,128)}), f32[32,4,128]{2,1,0:T(4,128)S(1)}, u32[]{:S(2)}, u32[]{:S(2)}) async-start(f32[32,4,128]{2,1,0:T(4,128)} %shard_map.53.own_ref), calls=%async_computation.3 | async-start | bytes 131072 | tf_op jit(solution)/shard_map/all_to_all | solution.py:235
  66.5 5.7 %shard_map.54.mine_ref = f32[2,96,128]{2,1,0:T(8,128)S(1)} custom-call(f32[32,16,128]{2,1,0:T(8,128)S(1)} %all_to_all.27.got_ref), custom_call_target="tpu_custom_call" | custom-call | flops 10000000000 | bytes 40000000 | tf_op jit(solution)/shard_map/pallas_call | solution.py:35
  72.2 3.6 %collective-permute-start = (f32[2,96,128]{2,1,0:T(8,128)S(1)}, f32[2,96,128]{2,1,0:T(8,128)S(1)}, u32[]{:S(2)}, u32[]{:S(2)}) collective-permute-start(f32[2,96,128]{2,1,0:T(8,128)S(1)} %shard_map.54.mine_ref), channel_id=1, source_target_pairs={{0,32},{32,0},{64,96},{96,64},{128,160},{160,128},{192,224},{224,1... | collective-permute-start | bytes 294920 | tf_op jit(solution)/shard_map/ppermute | solution.py:237
  75.8 0.9 collective-permute-done.other_ref
  76.7 0.9 all-to-all-done.3.m_ref
  77.7 1.3 %shard_map.55 = (f32[16,4,128]{2,1,0:T(4,128)S(1)}, f32[4,128]{1,0:T(4,128)S(1)}) custom-call(f32[32,4,128]{2,1,0:T(4,128)S(1)} %all-to-all-done.3.m_ref, f32[32,4,128]{2,1,0:T(4,128)} %shard_map.53.own_ref, f32[2,96,128]{2,1,0:T(8,128)S(1)} %shard_map.54.mine_ref, f32[2,96,128]{2,1,0:T(8,128)S(1)} %collective-permute-done.other_ref), custom_call_target="tpu_custom_call" | custom-call | tf_op jit(solution)/shard_map/pallas_call | solution.py:35
  79.0 13.4 %all_to_all.28.got_ref = f32[16,4,128]{2,1,0:T(4,128)S(1)} all-to-all(f32[16,4,128]{2,1,0:T(4,128)S(1)} %get-tuple-element.4), channel_id=1, replica_groups=mesh['ia'=16,'ja'=8,'ka'=4] {'ia'}, dimensions={0} | all-to-all | bytes 65536 | tf_op jit(solution)/shard_map/all_to_all | solution.py:239
  92.3 0.6 shard_map.56
Async XLA Ops:
  0.6 0.8 copy-start.1
  1.5 0.8 copy-start.2
  20.4 19.6 %copy-start = (f32[32,128,128]{2,1,0:T(8,128)S(1)}, f32[32,128,128]{2,1,0:T(8,128)}, u32[]{:S(2)}) copy-start(f32[32,128,128]{2,1,0:T(8,128)} %t_ref.1) | copy-start | bytes 6291460
  60.2 17.4 %all-to-all-start.3 = ((f32[32,4,128]{2,1,0:T(4,128)}), f32[32,4,128]{2,1,0:T(4,128)S(1)}, u32[]{:S(2)}, u32[]{:S(2)}) async-start(f32[32,4,128]{2,1,0:T(4,128)} %shard_map.53.own_ref), calls=%async_computation.3 | async-start | bytes 131072 | tf_op jit(solution)/shard_map/all_to_all | solution.py:235
  72.2 4.6 %collective-permute-start = (f32[2,96,128]{2,1,0:T(8,128)S(1)}, f32[2,96,128]{2,1,0:T(8,128)S(1)}, u32[]{:S(2)}, u32[]{:S(2)}) collective-permute-start(f32[2,96,128]{2,1,0:T(8,128)S(1)} %shard_map.54.mine_ref), channel_id=1, source_target_pairs={{0,32},{32,0},{64,96},{96,64},{128,160},{160,128},{192,224},{224,1... | collective-permute-start | bytes 294920 | tf_op jit(solution)/shard_map/ppermute | solution.py:237

commit v10 on v5

v10 whole, which is shorter than its diff:
```python
import jax
import jax.numpy as jnp
from jax import lax
from jax.experimental import pallas as pl
from jax.experimental.pallas import tpu as pltpu
from jax.sharding import PartitionSpec as P

highest = lax.Precision.HIGHEST
f32 = jnp.float32
bf16 = jnp.bfloat16

R = 96
S = 4
W = S * R
VMEM = pl.BlockSpec(memory_space=pltpu.VMEM)


def dot(a, b, dims, precision=highest):
    return lax.dot_general(a, b, (dims, ((), ())), precision=precision, preferred_element_type=f32)


def lanes(shape):
    return lax.broadcasted_iota(jnp.int32, shape, 1)


def rows(shape):
    return lax.broadcasted_iota(jnp.int32, shape, 0)


def call(body, out, cost=None, scratch=()):
    shapes = [jax.ShapeDtypeStruct(o, f32) for o in out]

    def run(*args):
        return pl.pallas_call(
            body,
            out_shape=shapes,
            in_specs=[VMEM] * len(args),
            out_specs=[VMEM] * len(shapes),
            scratch_shapes=list(scratch),
            compiler_params=pltpu.CompilerParams(vmem_limit_bytes=32 * 1024 * 1024),
            cost_estimate=cost,
        )(*args)

    return run


def start_of():
    return lax.rem(lax.axis_index("ia"), S)


def pick(which, choices):
    out = choices[0]
    for n in range(1, len(choices)):
        out = jnp.where(which == n, choices[n], out)
    return out


def prepare(fb_ref, fc_ref, out_ref):
    peers, nc = out_ref.shape[0], fc_ref.shape[0]
    b = pick(start_of(), [fb_ref[:, s, :] for s in range(S)])
    c = pick(start_of(), [fc_ref[:, s, :] for s in range(S)])
    wide_b = jnp.concatenate([b, jnp.zeros((b.shape[0], 128 - R), f32)], axis=1)
    wide_c = jnp.concatenate([c, jnp.zeros((c.shape[0], 128 - R), f32)], axis=1)
    gram_b = dot(b, wide_b, ((0,), (0,)))
    gram_c = dot(c, pltpu.roll(wide_c, 1, 1), ((0,), (0,)))
    z = jnp.where(lanes((R, 128)) <= rows((R, 128)), gram_b, gram_c)
    c_flat = jnp.concatenate([fc_ref[:, s, :] for s in range(S)], axis=1)
    depth = R // peers
    fill = jnp.zeros((out_ref.shape[1] - 3 * nc - depth, 128), f32)
    for p in range(peers):
        for q in range(3):
            out_ref[p, q * nc : (q + 1) * nc, :] = c_flat[:, q * 128 : (q + 1) * 128]
        out_ref[p, 3 * nc :, :] = jnp.concatenate([z[p * depth : (p + 1) * depth], fill], axis=0)


def middle(got_ref, fb_ref, out_ref):
    parts, nb = out_ref.shape[0], fb_ref.shape[0]
    depth = R // got_ref.shape[0]
    share = jnp.sum(got_ref[:, got_ref.shape[1] - 16 :, :], axis=0)
    b_flat = jnp.concatenate([fb_ref[:, s, :] for s in range(S)], axis=1)
    step = depth // parts
    fill = jnp.zeros((8 - step, 128), f32)
    for p in range(parts):
        for q in range(3):
            out_ref[p, q * nb : (q + 1) * nb, :] = b_flat[:, q * 128 : (q + 1) * 128]
        out_ref[p, 3 * nb :, :] = jnp.concatenate([share[p * step : (p + 1) * step], fill], axis=0)


def gathered(ref, count):
    pieces = [ref[:, q * count : (q + 1) * count, :].reshape(ref.shape[0] * count, 128) for q in range(3)]
    return jnp.concatenate(pieces, axis=1)


def contract(t_ref, c_got_ref, b_got_ref, out_ref, m_ref):
    ni, nj, nk = t_ref.shape
    nb = nj // b_got_ref.shape[0]
    c = gathered(c_got_ref, nk // c_got_ref.shape[0])
    b = gathered(b_got_ref, nb)
    c_high = c.astype(bf16)
    c_low = (c - c_high.astype(f32)).astype(bf16)
    twice = jnp.concatenate([c_high, c_high], axis=0)
    group = 8
    for at in range(0, ni, group):
        t = t_ref[at : at + group, :, :].reshape(group * nj, nk)
        t_high = t.astype(bf16)
        t_low = (t - t_high.astype(f32)).astype(bf16)
        both = jnp.concatenate([t_high, t_low], axis=1)
        value = dot(both, twice, ((1,), (0,)), None) + dot(t_high, c_low, ((1,), (0,)), None)
        m_ref[at : at + group, :] = jnp.sum(value.reshape(group, nj, W) * b[None], axis=1)
    share = jnp.sum(b_got_ref[:, 3 * nb :, :], axis=0)
    out_ref[...] = jnp.broadcast_to(share[None], out_ref.shape)
    for q in range(3):
        out_ref[:, 3 + q, :] = m_ref[:, q * 128 : (q + 1) * 128]


def own_row(got_ref, out_ref):
    total = jnp.sum(got_ref[...], axis=0)
    flat = jnp.concatenate([total[3 + q : 4 + q] for q in range(3)], axis=1)
    pad = jnp.zeros((1, 128 - R), f32)
    row = [jnp.concatenate([flat[:, s * R : (s + 1) * R], pad], axis=1) for s in range(S)]
    out_ref[...] = jnp.broadcast_to(jnp.concatenate(row, axis=0)[None], out_ref.shape)


def wide(v):
    return jnp.broadcast_to(v, (8, 128))


def eliminate(blocks, scale, k, q, lane8, row8):
    own, m = divmod(k, 8)
    hit = (lane8 >= k) & (lane8 < k + q)
    mine = blocks[own]
    row = [wide(mine[m + p : m + p + 1]) for p in range(q)]
    cols = [wide(mine[:, k + j : k + j + 1]) for j in range(q)]
    a = {(p, j): wide(cols[j][m + p : m + p + 1]) for p in range(q) for j in range(p, q)}
    inv, u, unit = [], {}, []
    for p in range(q):
        inv.append(1.0 / a[p, p])
        unit.append(jnp.where(lane8 == k + p, 1.0, row[p]))
        scale = jnp.where(lane8 == k + p, inv[p], scale)
        for i in range(p + 1, q):
            u[i, p] = a[p, i] * inv[p]
            for j in range(i, q):
                a[i, j] = a[i, j] - u[i, p] * a[p, j]
        for i in range(p + 1, q):
            row[i] = jnp.where(lane8 == k + p, 0.0, row[i]) - u[i, p] * unit[p]
    steps = [None] * q
    for p in reversed(range(q)):
        step = jnp.where((lane8 > k + p) & hit, 0.0, unit[p]) * inv[p]
        for j in range(p + 1, q):
            step = step - u[j, p] * steps[j]
        steps[p] = step
    for i in range(own, len(blocks)):
        old = blocks[i]
        new = jnp.where(hit, 0.0, old)
        for p in range(q):
            new = new - wide(old[:, k + p : k + p + 1]) * steps[p]
        if i == own:
            new = jnp.where(row8 >= m + q, new, old)
            for p in range(1, q):
                new = jnp.where(row8 == m + p, row[p], new)
        blocks[i] = new
    return scale


def invert(got_ref, out_ref, z_ref):
    for p in range(got_ref.shape[0]):
        z_ref[3 * p : 3 * (p + 1), :] = got_ref[p, 0:3, :]
    lane, row = lanes((R, 128)), rows((R, 128))
    fill = jnp.zeros((128 - R, 128), f32)
    blocks = []
    for s in range(1):
        z = z_ref[s * R : (s + 1) * R, :]
        low = jnp.where(lane <= row, z, 0.0)
        b_up = jnp.concatenate([low, fill], axis=0).T[0:R]
        c_up = pltpu.roll(z, 127, 1)
        up = jnp.where((lane >= row) & (lane < R), b_up * c_up, 0.0)
        strict = jnp.where(lane > row, up, 0.0)
        full = up + jnp.concatenate([strict, fill], axis=0).T[0:R]
        blocks.append([full[8 * i : 8 * i + 8] for i in range(R // 8)])
    lane8, row8 = lanes((8, 128)), rows((8, 1))
    scale = [jnp.zeros((8, 128), f32)]
    for k in range(0, R, 4):
        for s in range(1):
            scale[s] = eliminate(blocks[s], scale[s], k, 4, lane8, row8)
    for s in range(1):
        w = jnp.concatenate(blocks[s], axis=0)
        w = jnp.where(lane == row, 1.0, jnp.where(lane < row, w, 0.0))
        inv = jnp.sum(jnp.where(lane == row, scale[s][0:1], 0.0), axis=1, keepdims=True)
        out_ref[s] = dot(w[:, 0:R], w * inv, ((0,), (0,)))


def solve(m_ref, own_ref, *refs):
    inverses, (out_ref, raw_ref) = [ref[0] for ref in refs[:S]], refs[S:]
    squares = []
    for s in range(S):
        inv = pick(start_of() ^ s, inverses)
        raw = dot(m_ref[:, s, 0:R], inv, ((1,), (0,)))
        squares.append(jnp.sum(raw * raw, axis=0, keepdims=True))
        raw_ref[s : s + 1, :] = dot(own_ref[0, :, 0:R], inv, ((1,), (0,)))[s : s + 1]
    total = jnp.concatenate(squares, axis=0)
    out_ref[...] = jnp.broadcast_to(total[None], out_ref.shape)


def finish_of(row_total):
    def finish(got_ref, raw_ref, fa_ref, w_ref):
        total = jnp.sum(got_ref[...], axis=0)
        weights = jnp.sqrt(total / row_total + 1e-06)
        w_ref[...] = weights[:, 0:R]
        fa_ref[0] = (raw_ref[...] / weights)[:, 0:R]

    return finish


def shards(tensor, factor_b, factor_c):
    ni = tensor.shape[0]
    ia, ja, ka = (lax.axis_size(a) for a in ("ia", "ja", "ka"))
    nb, nc = factor_b.shape[0], factor_c.shape[0]
    cost = pl.CostEstimate(flops=int(1e10), bytes_accessed=int(4e7), transcendentals=0)
    slots_c = call(prepare, [(ja, 3 * nc + 16, 128)])(factor_b, factor_c)[0]
    got_c = lax.all_to_all(slots_c, "ja", 0, 0)
    slots_b = call(middle, [(ka, 3 * nb + 8, 128)], cost=cost)(got_c, factor_b)[0]
    got_b = lax.all_to_all(slots_b, "ka", 0, 0)
    slots_m = call(contract, [(ja * ka, 8, 128)], scratch=[pltpu.VMEM((ni, W), f32)])(tensor, got_c, got_b)[0]
    got_m = lax.all_to_all(slots_m, ("ja", "ka"), 0, 0)
    own = call(own_row, [(ja * ka, S, 128)])(got_m)[0]
    all_rows = lax.all_to_all(own, ("ja", "ka"), 0, 0)
    inverse = call(invert, [(1, R, 128)], cost=cost, scratch=[pltpu.VMEM((R, 128), f32)])(got_m)[0]
    others = [lax.ppermute(inverse, "ia", [(n, n ^ d) for n in range(ia)]) for d in range(1, S)]
    squares, raw = call(solve, [(ia, S, 128), (S, 128)])(all_rows, own, inverse, *others)
    got_s = lax.all_to_all(squares, "ia", 0, 0)
    return tuple(call(finish_of(ni * ia), [(1, S, R), (S, R)])(got_s, raw))


def solution(mesh):
    in_specs = (P("ia", "ja", "ka"), P(("ja", "ka"), None, None), P(("ka", "ja"), None, None))
    out_specs = (P(("ia", "ja", "ka"), None, None), P())
    return jax.shard_map(shards, mesh=mesh, in_specs=in_specs, out_specs=out_specs, check_vma=False)
```

time: 95.1 us -> 91.8 us (0.965)
  starting transfers between devices: 6.51 us -> 14.1 us
  blocking collectives: 69.4 us -> 63.4 us
  waiting for transfers between devices: 4.06 us -> 1.05 us
  Pallas kernels: 12.4 us -> 10.4 us
    ppermute x0 -> x3, starting transfers between devices: none -> 10.2 us  [shards(): lax.ppermute(inverse, 'ia', [(n, n ^ d) for n in range(ia)])]
    all_to_all x1, waiting for transfers between devices: 4.06 us -> 0.01 us  [shards(): all_rows = lax.all_to_all(own, ('ja', 'ka'), 0, 0)]
    all_to_all x1, blocking collectives: 19.9 us -> 16.7 us  [shards(): got_c = lax.all_to_all(slots_c, 'ja', 0, 0)]
    all_to_all x1, starting transfers between devices: 6.51 us -> 3.86 us  [shards(): all_rows = lax.all_to_all(own, ('ja', 'ka'), 0, 0)]
    all_to_all x1, blocking collectives: 12.8 us -> 10.7 us  [shards(): got_s = lax.all_to_all(squares, 'ia', 0, 0)]
    pallas_call x7, Pallas kernels: 12.4 us -> 10.4 us  [run(): pl.pallas_call(body, out_shape=shapes, in_specs=[VMEM] * len(args), out_s...]
    ppermute x0 -> x3, waiting for transfers between devices: none -> 1.05 us  [shards(): lax.ppermute(inverse, 'ia', [(n, n ^ d) for n in range(ia)])]
  transfers between devices with their start and end apart: 1 -> 4, of which waited for: 1 -> 2; matrix products, arithmetic and copies ran while one was open for 0% -> 0% of each run, Pallas kernels for 8% -> 6%
where the time goes in v10:
time: 91.8 us; the launch traced here: 91.2 us
  blocking collectives  63.4 us (69%)
  starting transfers between devices  14.1 us (15%)
  Pallas kernels  10.4 us (11%)
  local copies, waits for them, and re-layouts  1.59 us (2%)
  waiting for transfers between devices  1.05 us (1%)
    all_to_all x1, blocking collectives, shards(): got_b = lax.all_to_all(slots_b, 'ka', 0, 0)  19.6 us
    all_to_all x1, blocking collectives, shards(): got_c = lax.all_to_all(slots_c, 'ja', 0, 0)  16.7 us
    all_to_all x1, blocking collectives, shards(): got_m = lax.all_to_all(slots_m, ('ja', 'ka'), 0, 0)  16.4 us
    all_to_all x1, blocking collectives, shards(): got_s = lax.all_to_all(squares, 'ia', 0, 0)  10.7 us
    pallas_call x7, Pallas kernels, run(): pl.pallas_call(body, out_shape=shapes, in_specs=[VMEM] * len(args), out_s...  10.4 us
    ppermute x3, starting transfers between devices, shards(): lax.ppermute(inverse, 'ia', [(n, n ^ d) for n in range(ia)])  10.2 us
    all_to_all x1, starting transfers between devices, shards(): all_rows = lax.all_to_all(own, ('ja', 'ka'), 0, 0)  3.86 us
  transfers between devices with their start and end apart: 4, of which 2 were waited for; matrix products, arithmetic and copies ran while one was open for 0% of the time, Pallas kernels for 6%

profile of v10, /device:TPU:1, one launch (start us, length us, event | category | flops | bytes accessed | tf_op | source)
XLA Modules:
  0.0 91.2 jit_solution(1606975915710069015)
XLA Ops:
  0.6 0.0 copy-start.1
  0.6 0.8 copy-done.1
  1.5 0.0 copy-start.2
  1.5 0.8 copy-done.2
  2.2 0.3 shard_map.50
  2.6 16.7 %all_to_all.25.got_ref.c_got_ref = f32[8,64,128]{2,1,0:T(8,128)S(1)} all-to-all(f32[8,64,128]{2,1,0:T(8,128)S(1)} %shard_map.50), channel_id=1, replica_groups=mesh['ia'=16,'ja'=8,'ka'=4] {'ja'}, dimensions={0} | all-to-all | bytes 524288 | tf_op jit(solution)/shard_map/all_to_all | solution.py:220
  19.3 0.1 shard_map.51
  19.4 19.6 %all_to_all.26.b_got_ref = f32[4,104,128]{2,1,0:T(8,128)S(1)} all-to-all(f32[4,104,128]{2,1,0:T(8,128)S(1)} %shard_map.51), channel_id=1, replica_groups=mesh['ia'=16,'ja'=8,'ka'=4] {'ka'}, dimensions={0} | all-to-all | bytes 425984 | tf_op jit(solution)/shard_map/all_to_all | solution.py:222
  39.0 0.0 copy-done
  39.0 2.1 %shard_map.52 = f32[32,8,128]{2,1,0:T(8,128)S(1)} custom-call(f32[32,128,128]{2,1,0:T(8,128)S(1)} %copy-done, f32[8,64,128]{2,1,0:T(8,128)S(1)} %all_to_all.25.got_ref.c_got_ref, f32[4,104,128]{2,1,0:T(8,128)S(1)} %all_to_all.26.b_got_ref), custom_call_target="tpu_custom_call" | custom-call | tf_op jit(solution)/shard_map/pallas_call | solution.py:34
  41.1 16.4 %all_to_all.27.got_ref = f32[32,8,128]{2,1,0:T(8,128)S(1)} all-to-all(f32[32,8,128]{2,1,0:T(8,128)S(1)} %shard_map.52), channel_id=1, replica_groups=mesh['ia'=16,'ja'=8,'ka'=4] {'ja','ka'}, dimensions={0} | all-to-all | bytes 262144 | tf_op jit(solution)/shard_map/all_to_all | solution.py:224
  57.5 0.7 shard_map.53.own_ref
  58.3 3.9 %all-to-all-start.3 = ((f32[32,4,128]{2,1,0:T(4,128)}), f32[32,4,128]{2,1,0:T(4,128)S(1)}, u32[]{:S(2)}, u32[]{:S(2)}) async-start(f32[32,4,128]{2,1,0:T(4,128)} %shard_map.53.own_ref), calls=%async_computation.3 | async-start | bytes 131072 | tf_op jit(solution)/shard_map/all_to_all | solution.py:226
  62.1 5.2 %shard_map.54.refs_0_ = f32[1,96,128]{2,1,0:T(8,128)S(1)} custom-call(f32[32,8,128]{2,1,0:T(8,128)S(1)} %all_to_all.27.got_ref), custom_call_target="tpu_custom_call" | custom-call | flops 10000000000 | bytes 40000000 | tf_op jit(solution)/shard_map/pallas_call | solution.py:34
  67.3 6.0 %collective-permute-start.2 = (f32[1,96,128]{2,1,0:T(8,128)S(1)}, f32[1,96,128]{2,1,0:T(8,128)S(1)}, u32[]{:S(2)}, u32[]{:S(2)}) collective-permute-start(f32[1,96,128]{2,1,0:T(8,128)S(1)} %shard_map.54.refs_0_), channel_id=1, source_target_pairs={{0,96},{32,64},{64,32},{96,0},{128,224},{160,192},{192,160},{224,1... | collective-permute-start | bytes 147464 | tf_op jit(solution)/shard_map/ppermute | solution.py:228
  73.3 2.2 %collective-permute-start.1 = (f32[1,96,128]{2,1,0:T(8,128)S(1)}, f32[1,96,128]{2,1,0:T(8,128)S(1)}, u32[]{:S(2)}, u32[]{:S(2)}) collective-permute-start(f32[1,96,128]{2,1,0:T(8,128)S(1)} %shard_map.54.refs_0_), channel_id=1, source_target_pairs={{0,64},{32,96},{64,0},{96,32},{128,192},{160,224},{192,128},{224,1... | collective-permute-start | bytes 147464 | tf_op jit(solution)/shard_map/ppermute | solution.py:228
  75.5 2.1 %collective-permute-start = (f32[1,96,128]{2,1,0:T(8,128)S(1)}, f32[1,96,128]{2,1,0:T(8,128)S(1)}, u32[]{:S(2)}, u32[]{:S(2)}) collective-permute-start(f32[1,96,128]{2,1,0:T(8,128)S(1)} %shard_map.54.refs_0_), channel_id=1, source_target_pairs={{0,32},{32,0},{64,96},{96,64},{128,160},{160,128},{192,224},{224,1... | collective-permute-start | bytes 147464 | tf_op jit(solution)/shard_map/ppermute | solution.py:228
  77.6 0.0 collective-permute-done.2.refs_3_
  77.6 0.6 collective-permute-done.1.refs_2_
  78.2 0.5 collective-permute-done.refs_1_
  78.6 0.0 all-to-all-done.3.m_ref
  78.6 1.3 %shard_map.55 = (f32[16,4,128]{2,1,0:T(4,128)S(1)}, f32[4,128]{1,0:T(4,128)S(1)}) custom-call(f32[32,4,128]{2,1,0:T(4,128)S(1)} %all-to-all-done.3.m_ref, f32[32,4,128]{2,1,0:T(4,128)} %shard_map.53.own_ref, f32[1,96,128]{2,1,0:T(8,128)S(1)} %shard_map.54.refs_0_, f32[1,96,128]{2,1,0:T(8,128)S(1)} %collective-permute-done.refs_1_, ...), custom_call_target="tpu_custom_call" | custom-call | tf_op jit(solution)/shard_map/pallas_call | solution.py:34
  79.9 10.7 %all_to_all.28.got_ref = f32[16,4,128]{2,1,0:T(4,128)S(1)} all-to-all(f32[16,4,128]{2,1,0:T(4,128)S(1)} %get-tuple-element.4), channel_id=1, replica_groups=mesh['ia'=16,'ja'=8,'ka'=4] {'ia'}, dimensions={0} | all-to-all | bytes 65536 | tf_op jit(solution)/shard_map/all_to_all | solution.py:230
  90.6 0.6 shard_map.56
  (1 shorter events, 0.0 us)
Async XLA Ops:
  0.6 0.8 copy-start.1
  1.5 0.8 copy-start.2
  19.3 19.7 %copy-start = (f32[32,128,128]{2,1,0:T(8,128)S(1)}, f32[32,128,128]{2,1,0:T(8,128)}, u32[]{:S(2)}) copy-start(f32[32,128,128]{2,1,0:T(8,128)} %t_ref.1) | copy-start | bytes 6291460
  58.3 20.4 %all-to-all-start.3 = ((f32[32,4,128]{2,1,0:T(4,128)}), f32[32,4,128]{2,1,0:T(4,128)S(1)}, u32[]{:S(2)}, u32[]{:S(2)}) async-start(f32[32,4,128]{2,1,0:T(4,128)} %shard_map.53.own_ref), calls=%async_computation.3 | async-start | bytes 131072 | tf_op jit(solution)/shard_map/all_to_all | solution.py:226
  67.3 10.2 %collective-permute-start.2 = (f32[1,96,128]{2,1,0:T(8,128)S(1)}, f32[1,96,128]{2,1,0:T(8,128)S(1)}, u32[]{:S(2)}, u32[]{:S(2)}) collective-permute-start(f32[1,96,128]{2,1,0:T(8,128)S(1)} %shard_map.54.refs_0_), channel_id=1, source_target_pairs={{0,96},{32,64},{64,32},{96,0},{128,224},{160,192},{192,160},{224,1... | collective-permute-start | bytes 147464 | tf_op jit(solution)/shard_map/ppermute | solution.py:228
  73.3 4.8 %collective-permute-start.1 = (f32[1,96,128]{2,1,0:T(8,128)S(1)}, f32[1,96,128]{2,1,0:T(8,128)S(1)}, u32[]{:S(2)}, u32[]{:S(2)}) collective-permute-start(f32[1,96,128]{2,1,0:T(8,128)S(1)} %shard_map.54.refs_0_), channel_id=1, source_target_pairs={{0,64},{32,96},{64,0},{96,32},{128,192},{160,224},{192,128},{224,1... | collective-permute-start | bytes 147464 | tf_op jit(solution)/shard_map/ppermute | solution.py:228
  75.5 3.1 %collective-permute-start = (f32[1,96,128]{2,1,0:T(8,128)S(1)}, f32[1,96,128]{2,1,0:T(8,128)S(1)}, u32[]{:S(2)}, u32[]{:S(2)}) collective-permute-start(f32[1,96,128]{2,1,0:T(8,128)S(1)} %shard_map.54.refs_0_), channel_id=1, source_target_pairs={{0,32},{32,0},{64,96},{96,64},{128,160},{160,128},{192,224},{224,1... | collective-permute-start | bytes 147464 | tf_op jit(solution)/shard_map/ppermute | solution.py:228

commit v11 on v10

--- a/solution.py
+++ b/solution.py
@@ -179,9 +179,9 @@
         blocks.append([full[8 * i : 8 * i + 8] for i in range(R // 8)])
     lane8, row8 = lanes((8, 128)), rows((8, 1))
     scale = [jnp.zeros((8, 128), f32)]
-    for k in range(0, R, 4):
+    for k in range(0, R, 8):
         for s in range(1):
-            scale[s] = eliminate(blocks[s], scale[s], k, 4, lane8, row8)
+            scale[s] = eliminate(blocks[s], scale[s], k, 8, lane8, row8)
     for s in range(1):
         w = jnp.concatenate(blocks[s], axis=0)
         w = jnp.where(lane == row, 1.0, jnp.where(lane < row, w, 0.0))
@@ -191,12 +191,14 @@
 
 def solve(m_ref, own_ref, *refs):
     inverses, (out_ref, raw_ref) = [ref[0] for ref in refs[:S]], refs[S:]
+    count = m_ref.shape[0]
     squares = []
     for s in range(S):
         inv = pick(start_of() ^ s, inverses)
-        raw = dot(m_ref[:, s, 0:R], inv, ((1,), (0,)))
-        squares.append(jnp.sum(raw * raw, axis=0, keepdims=True))
-        raw_ref[s : s + 1, :] = dot(own_ref[0, :, 0:R], inv, ((1,), (0,)))[s : s + 1]
+        both = jnp.concatenate([m_ref[:, s, 0:R], own_ref[0:8, s, 0:R]], axis=0)
+        raw = dot(both, inv, ((1,), (0,)))
+        squares.append(jnp.sum(raw[0:count] * raw[0:count], axis=0, keepdims=True))
+        raw_ref[s : s + 1, :] = raw[count : count + 1]
     total = jnp.concatenate(squares, axis=0)
     out_ref[...] = jnp.broadcast_to(total[None], out_ref.shape)
 

time: 91.8 us -> 91 us (level)
  transfers between devices with their start and end apart: 4 -> 4, of which waited for: 2 -> 2; matrix products, arithmetic and copies ran while one was open for 0% -> 0% of each run, Pallas kernels for 6% -> 5%
where the time goes in v11:
time: 91 us; the launch traced here: 90.5 us
  blocking collectives  63.4 us (70%)
  starting transfers between devices  14.1 us (15%)
  Pallas kernels  9.65 us (11%)
  local copies, waits for them, and re-layouts  1.59 us (2%)
  waiting for transfers between devices  1.05 us (1%)
    all_to_all x1, blocking collectives, shards(): got_b = lax.all_to_all(slots_b, 'ka', 0, 0)  19.6 us
    all_to_all x1, blocking collectives, shards(): got_c = lax.all_to_all(slots_c, 'ja', 0, 0)  16.7 us
    all_to_all x1, blocking collectives, shards(): got_m = lax.all_to_all(slots_m, ('ja', 'ka'), 0, 0)  16.4 us
    all_to_all x1, blocking collectives, shards(): got_s = lax.all_to_all(squares, 'ia', 0, 0)  10.7 us
    ppermute x3, starting transfers between devices, shards(): lax.ppermute(inverse, 'ia', [(n, n ^ d) for n in range(ia)])  10.2 us
    pallas_call x7, Pallas kernels, run(): pl.pallas_call(body, out_shape=shapes, in_specs=[VMEM] * len(args), out_s...  9.65 us
    all_to_all x1, starting transfers between devices, shards(): all_rows = lax.all_to_all(own, ('ja', 'ka'), 0, 0)  3.86 us
  transfers between devices with their start and end apart: 4, of which 2 were waited for; matrix products, arithmetic and copies ran while one was open for 0% of the time, Pallas kernels for 5%

profile of v11, /device:TPU:1, one launch (start us, length us, event | category | flops | bytes accessed | tf_op | source)
XLA Modules:
  0.0 90.5 jit_solution(6625198540361749436)
XLA Ops:
  0.6 0.0 copy-start.1
  0.6 0.8 copy-done.1
  1.5 0.0 copy-start.2
  1.5 0.8 copy-done.2
  2.2 0.3 shard_map.50
  2.6 16.7 %all_to_all.25.got_ref.c_got_ref = f32[8,64,128]{2,1,0:T(8,128)S(1)} all-to-all(f32[8,64,128]{2,1,0:T(8,128)S(1)} %shard_map.50), channel_id=1, replica_groups=mesh['ia'=16,'ja'=8,'ka'=4] {'ja'}, dimensions={0} | all-to-all | bytes 524288 | tf_op jit(solution)/shard_map/all_to_all | solution.py:222
  19.3 0.1 shard_map.51
  19.4 19.6 %all_to_all.26.b_got_ref = f32[4,104,128]{2,1,0:T(8,128)S(1)} all-to-all(f32[4,104,128]{2,1,0:T(8,128)S(1)} %shard_map.51), channel_id=1, replica_groups=mesh['ia'=16,'ja'=8,'ka'=4] {'ka'}, dimensions={0} | all-to-all | bytes 425984 | tf_op jit(solution)/shard_map/all_to_all | solution.py:224
  39.0 0.0 copy-done
  39.0 2.1 %shard_map.52 = f32[32,8,128]{2,1,0:T(8,128)S(1)} custom-call(f32[32,128,128]{2,1,0:T(8,128)S(1)} %copy-done, f32[8,64,128]{2,1,0:T(8,128)S(1)} %all_to_all.25.got_ref.c_got_ref, f32[4,104,128]{2,1,0:T(8,128)S(1)} %all_to_all.26.b_got_ref), custom_call_target="tpu_custom_call" | custom-call | tf_op jit(solution)/shard_map/pallas_call | solution.py:34
  41.1 16.4 %all_to_all.27.got_ref = f32[32,8,128]{2,1,0:T(8,128)S(1)} all-to-all(f32[32,8,128]{2,1,0:T(8,128)S(1)} %shard_map.52), channel_id=1, replica_groups=mesh['ia'=16,'ja'=8,'ka'=4] {'ja','ka'}, dimensions={0} | all-to-all | bytes 262144 | tf_op jit(solution)/shard_map/all_to_all | solution.py:226
  57.5 0.7 shard_map.53.own_ref
  58.3 3.9 %all-to-all-start.3 = ((f32[32,4,128]{2,1,0:T(4,128)}), f32[32,4,128]{2,1,0:T(4,128)S(1)}, u32[]{:S(2)}, u32[]{:S(2)}) async-start(f32[32,4,128]{2,1,0:T(4,128)} %shard_map.53.own_ref), calls=%async_computation.3 | async-start | bytes 131072 | tf_op jit(solution)/shard_map/all_to_all | solution.py:228
  62.1 4.6 %shard_map.54.refs_0_ = f32[1,96,128]{2,1,0:T(8,128)S(1)} custom-call(f32[32,8,128]{2,1,0:T(8,128)S(1)} %all_to_all.27.got_ref), custom_call_target="tpu_custom_call" | custom-call | flops 10000000000 | bytes 40000000 | tf_op jit(solution)/shard_map/pallas_call | solution.py:34
  66.8 6.0 %collective-permute-start.2 = (f32[1,96,128]{2,1,0:T(8,128)S(1)}, f32[1,96,128]{2,1,0:T(8,128)S(1)}, u32[]{:S(2)}, u32[]{:S(2)}) collective-permute-start(f32[1,96,128]{2,1,0:T(8,128)S(1)} %shard_map.54.refs_0_), channel_id=1, source_target_pairs={{0,96},{32,64},{64,32},{96,0},{128,224},{160,192},{192,160},{224,1... | collective-permute-start | bytes 147464 | tf_op jit(solution)/shard_map/ppermute | solution.py:230
  72.7 2.2 %collective-permute-start.1 = (f32[1,96,128]{2,1,0:T(8,128)S(1)}, f32[1,96,128]{2,1,0:T(8,128)S(1)}, u32[]{:S(2)}, u32[]{:S(2)}) collective-permute-start(f32[1,96,128]{2,1,0:T(8,128)S(1)} %shard_map.54.refs_0_), channel_id=1, source_target_pairs={{0,64},{32,96},{64,0},{96,32},{128,192},{160,224},{192,128},{224,1... | collective-permute-start | bytes 147464 | tf_op jit(solution)/shard_map/ppermute | solution.py:230
  74.9 2.1 %collective-permute-start = (f32[1,96,128]{2,1,0:T(8,128)S(1)}, f32[1,96,128]{2,1,0:T(8,128)S(1)}, u32[]{:S(2)}, u32[]{:S(2)}) collective-permute-start(f32[1,96,128]{2,1,0:T(8,128)S(1)} %shard_map.54.refs_0_), channel_id=1, source_target_pairs={{0,32},{32,0},{64,96},{96,64},{128,160},{160,128},{192,224},{224,1... | collective-permute-start | bytes 147464 | tf_op jit(solution)/shard_map/ppermute | solution.py:230
  77.0 0.0 collective-permute-done.2.refs_3_
  77.0 0.6 collective-permute-done.1.refs_2_
  77.6 0.5 collective-permute-done.refs_1_
  78.0 0.0 all-to-all-done.3.m_ref
  78.0 1.2 %shard_map.55 = (f32[16,4,128]{2,1,0:T(4,128)S(1)}, f32[4,128]{1,0:T(4,128)S(1)}) custom-call(f32[32,4,128]{2,1,0:T(4,128)S(1)} %all-to-all-done.3.m_ref, f32[32,4,128]{2,1,0:T(4,128)} %shard_map.53.own_ref, f32[1,96,128]{2,1,0:T(8,128)S(1)} %shard_map.54.refs_0_, f32[1,96,128]{2,1,0:T(8,128)S(1)} %collective-permute-done.refs_1_, ...), custom_call_target="tpu_custom_call" | custom-call | tf_op jit(solution)/shard_map/pallas_call | solution.py:34
  79.2 10.7 %all_to_all.28.got_ref = f32[16,4,128]{2,1,0:T(4,128)S(1)} all-to-all(f32[16,4,128]{2,1,0:T(4,128)S(1)} %get-tuple-element.4), channel_id=1, replica_groups=mesh['ia'=16,'ja'=8,'ka'=4] {'ia'}, dimensions={0} | all-to-all | bytes 65536 | tf_op jit(solution)/shard_map/all_to_all | solution.py:232
  89.9 0.6 shard_map.56
  (1 shorter events, 0.0 us)
Async XLA Ops:
  0.6 0.8 copy-start.1
  1.5 0.8 copy-start.2
  19.3 19.7 %copy-start = (f32[32,128,128]{2,1,0:T(8,128)S(1)}, f32[32,128,128]{2,1,0:T(8,128)}, u32[]{:S(2)}) copy-start(f32[32,128,128]{2,1,0:T(8,128)} %t_ref.1) | copy-start | bytes 6291460
  58.3 19.8 %all-to-all-start.3 = ((f32[32,4,128]{2,1,0:T(4,128)}), f32[32,4,128]{2,1,0:T(4,128)S(1)}, u32[]{:S(2)}, u32[]{:S(2)}) async-start(f32[32,4,128]{2,1,0:T(4,128)} %shard_map.53.own_ref), calls=%async_computation.3 | async-start | bytes 131072 | tf_op jit(solution)/shard_map/all_to_all | solution.py:228
  66.8 10.2 %collective-permute-start.2 = (f32[1,96,128]{2,1,0:T(8,128)S(1)}, f32[1,96,128]{2,1,0:T(8,128)S(1)}, u32[]{:S(2)}, u32[]{:S(2)}) collective-permute-start(f32[1,96,128]{2,1,0:T(8,128)S(1)} %shard_map.54.refs_0_), channel_id=1, source_target_pairs={{0,96},{32,64},{64,32},{96,0},{128,224},{160,192},{192,160},{224,1... | collective-permute-start | bytes 147464 | tf_op jit(solution)/shard_map/ppermute | solution.py:230
  72.7 4.8 %collective-permute-start.1 = (f32[1,96,128]{2,1,0:T(8,128)S(1)}, f32[1,96,128]{2,1,0:T(8,128)S(1)}, u32[]{:S(2)}, u32[]{:S(2)}) collective-permute-start(f32[1,96,128]{2,1,0:T(8,128)S(1)} %shard_map.54.refs_0_), channel_id=1, source_target_pairs={{0,64},{32,96},{64,0},{96,32},{128,192},{160,224},{192,128},{224,1... | collective-permute-start | bytes 147464 | tf_op jit(solution)/shard_map/ppermute | solution.py:230
  74.9 3.1 %collective-permute-start = (f32[1,96,128]{2,1,0:T(8,128)S(1)}, f32[1,96,128]{2,1,0:T(8,128)S(1)}, u32[]{:S(2)}, u32[]{:S(2)}) collective-permute-start(f32[1,96,128]{2,1,0:T(8,128)S(1)} %shard_map.54.refs_0_), channel_id=1, source_target_pairs={{0,32},{32,0},{64,96},{96,64},{128,160},{160,128},{192,224},{224,1... | collective-permute-start | bytes 147464 | tf_op jit(solution)/shard_map/ppermute | solution.py:230

commit v12 on v11

--- a/solution.py
+++ b/solution.py
@@ -55,7 +55,7 @@
     return out
 
 
-def prepare(fb_ref, fc_ref, out_ref):
+def prepare(fb_ref, fc_ref, out_ref, b_ref):
     peers, nc = out_ref.shape[0], fc_ref.shape[0]
     b = pick(start_of(), [fb_ref[:, s, :] for s in range(S)])
     c = pick(start_of(), [fc_ref[:, s, :] for s in range(S)])
@@ -65,6 +65,7 @@
     gram_c = dot(c, pltpu.roll(wide_c, 1, 1), ((0,), (0,)))
     z = jnp.where(lanes((R, 128)) <= rows((R, 128)), gram_b, gram_c)
     c_flat = jnp.concatenate([fc_ref[:, s, :] for s in range(S)], axis=1)
+    b_ref[...] = jnp.concatenate([fb_ref[:, s, :] for s in range(S)], axis=1)
     depth = R // peers
     fill = jnp.zeros((out_ref.shape[1] - 3 * nc - depth, 128), f32)
     for p in range(peers):
@@ -73,29 +74,16 @@
         out_ref[p, 3 * nc :, :] = jnp.concatenate([z[p * depth : (p + 1) * depth], fill], axis=0)
 
 
-def middle(got_ref, fb_ref, out_ref):
-    parts, nb = out_ref.shape[0], fb_ref.shape[0]
-    depth = R // got_ref.shape[0]
-    share = jnp.sum(got_ref[:, got_ref.shape[1] - 16 :, :], axis=0)
-    b_flat = jnp.concatenate([fb_ref[:, s, :] for s in range(S)], axis=1)
-    step = depth // parts
-    fill = jnp.zeros((8 - step, 128), f32)
-    for p in range(parts):
-        for q in range(3):
-            out_ref[p, q * nb : (q + 1) * nb, :] = b_flat[:, q * 128 : (q + 1) * 128]
-        out_ref[p, 3 * nb :, :] = jnp.concatenate([share[p * step : (p + 1) * step], fill], axis=0)
-
-
 def gathered(ref, count):
     pieces = [ref[:, q * count : (q + 1) * count, :].reshape(ref.shape[0] * count, 128) for q in range(3)]
     return jnp.concatenate(pieces, axis=1)
 
 
-def contract(t_ref, c_got_ref, b_got_ref, out_ref, m_ref):
+def contract(t_ref, c_got_ref, b_ref, out_ref, m_ref):
     ni, nj, nk = t_ref.shape
-    nb = nj // b_got_ref.shape[0]
-    c = gathered(c_got_ref, nk // c_got_ref.shape[0])
-    b = gathered(b_got_ref, nb)
+    nc = nk // c_got_ref.shape[0]
+    c = gathered(c_got_ref, nc)
+    b = b_ref[...]
     c_high = c.astype(bf16)
     c_low = (c - c_high.astype(f32)).astype(bf16)
     twice = jnp.concatenate([c_high, c_high], axis=0)
@@ -107,15 +95,15 @@
         both = jnp.concatenate([t_high, t_low], axis=1)
         value = dot(both, twice, ((1,), (0,)), None) + dot(t_high, c_low, ((1,), (0,)), None)
         m_ref[at : at + group, :] = jnp.sum(value.reshape(group, nj, W) * b[None], axis=1)
-    share = jnp.sum(b_got_ref[:, 3 * nb :, :], axis=0)
+    share = jnp.sum(c_got_ref[:, 3 * nc :, :], axis=0)
     out_ref[...] = jnp.broadcast_to(share[None], out_ref.shape)
     for q in range(3):
-        out_ref[:, 3 + q, :] = m_ref[:, q * 128 : (q + 1) * 128]
+        out_ref[:, 12 + q, :] = m_ref[:, q * 128 : (q + 1) * 128]
 
 
 def own_row(got_ref, out_ref):
-    total = jnp.sum(got_ref[...], axis=0)
-    flat = jnp.concatenate([total[3 + q : 4 + q] for q in range(3)], axis=1)
+    total = jnp.sum(got_ref[:, 8:16, :], axis=0)
+    flat = jnp.concatenate([total[4 + q : 5 + q] for q in range(3)], axis=1)
     pad = jnp.zeros((1, 128 - R), f32)
     row = [jnp.concatenate([flat[:, s * R : (s + 1) * R], pad], axis=1) for s in range(S)]
     out_ref[...] = jnp.broadcast_to(jnp.concatenate(row, axis=0)[None], out_ref.shape)
@@ -163,8 +151,9 @@
 
 
 def invert(got_ref, out_ref, z_ref):
-    for p in range(got_ref.shape[0]):
-        z_ref[3 * p : 3 * (p + 1), :] = got_ref[p, 0:3, :]
+    ka = lax.axis_size("ka")
+    for p in range(got_ref.shape[0] // ka):
+        z_ref[12 * p : 12 * (p + 1), :] = jnp.sum(got_ref[ka * p : ka * (p + 1), 0:12, :], axis=0)
     lane, row = lanes((R, 128)), rows((R, 128))
     fill = jnp.zeros((128 - R, 128), f32)
     blocks = []
@@ -218,11 +207,10 @@
     ia, ja, ka = (lax.axis_size(a) for a in ("ia", "ja", "ka"))
     nb, nc = factor_b.shape[0], factor_c.shape[0]
     cost = pl.CostEstimate(flops=int(1e10), bytes_accessed=int(4e7), transcendentals=0)
-    slots_c = call(prepare, [(ja, 3 * nc + 16, 128)])(factor_b, factor_c)[0]
+    slots_c, b_flat = call(prepare, [(ja, 3 * nc + 16, 128), (nb, W)], cost=cost)(factor_b, factor_c)
     got_c = lax.all_to_all(slots_c, "ja", 0, 0)
-    slots_b = call(middle, [(ka, 3 * nb + 8, 128)], cost=cost)(got_c, factor_b)[0]
-    got_b = lax.all_to_all(slots_b, "ka", 0, 0)
-    slots_m = call(contract, [(ja * ka, 8, 128)], scratch=[pltpu.VMEM((ni, W), f32)])(tensor, got_c, got_b)[0]
+    b_block = lax.all_gather(b_flat, "ka", axis=0, tiled=True)
+    slots_m = call(contract, [(ja * ka, 16, 128)], scratch=[pltpu.VMEM((ni, W), f32)])(tensor, got_c, b_block)[0]
     got_m = lax.all_to_all(slots_m, ("ja", "ka"), 0, 0)
     own = call(own_row, [(ja * ka, S, 128)])(got_m)[0]
     all_rows = lax.all_to_all(own, ("ja", "ka"), 0, 0)

time: 91 us -> 88.5 us (0.973)
  blocking collectives: 63.4 us -> 50 us
  starting transfers between devices: 14.1 us -> 24.3 us
    all_to_all x2 -> x0, blocking collectives: 36.3 us -> none  [the longest x1 19.6 us: shards(): got_b = lax.all_to_all(slots_b, 'ka', 0, 0)]
    all_gather x0 -> x1, blocking collectives: none -> 17.2 us  [shards(): b_block = lax.all_gather(b_flat, 'ka', axis=0, tiled=True)]
    all_to_all x0 -> x1, starting transfers between devices: none -> 7.65 us  [shards(): got_c = lax.all_to_all(slots_c, 'ja', 0, 0)]
    all_to_all x1, blocking collectives: 16.4 us -> 21.5 us  [shards(): got_m = lax.all_to_all(slots_m, ('ja', 'ka'), 0, 0)]
    ppermute x3, starting transfers between devices: 10.2 us -> 12.1 us  [shards(): lax.ppermute(inverse, 'ia', [(n, n ^ d) for n in range(ia)])]
    pallas_call x7 -> x6, Pallas kernels: 9.65 us -> 10.3 us  [run(): pl.pallas_call(body, out_shape=shapes, in_specs=[VMEM] * len(args), out_s...]
  transfers between devices with their start and end apart: 4 -> 5, of which waited for: 2 -> 2; matrix products, arithmetic and copies ran while one was open for 0% -> 0% of each run, Pallas kernels for 5% -> 5%
where the time goes in v12:
time: 88.5 us; the launch traced here: 87.9 us
  blocking collectives  50 us (56%)
  starting transfers between devices  24.3 us (27%)
  Pallas kernels  10.3 us (12%)
  local copies, waits for them, and re-layouts  1.59 us (2%)
  waiting for transfers between devices  1.06 us (1%)
    all_to_all x1, blocking collectives, shards(): got_m = lax.all_to_all(slots_m, ('ja', 'ka'), 0, 0)  21.5 us
    all_gather x1, blocking collectives, shards(): b_block = lax.all_gather(b_flat, 'ka', axis=0, tiled=True)  17.2 us
    ppermute x3, starting transfers between devices, shards(): lax.ppermute(inverse, 'ia', [(n, n ^ d) for n in range(ia)])  12.1 us
    all_to_all x1, blocking collectives, shards(): got_s = lax.all_to_all(squares, 'ia', 0, 0)  11.3 us
    pallas_call x6, Pallas kernels, run(): pl.pallas_call(body, out_shape=shapes, in_specs=[VMEM] * len(args), out_s...  10.3 us
    all_to_all x1, starting transfers between devices, shards(): got_c = lax.all_to_all(slots_c, 'ja', 0, 0)  7.65 us
    all_to_all x1, starting transfers between devices, shards(): all_rows = lax.all_to_all(own, ('ja', 'ka'), 0, 0)  4.53 us
  transfers between devices with their start and end apart: 5, of which 2 were waited for; matrix products, arithmetic and copies ran while one was open for 0% of the time, Pallas kernels for 5%

profile of v12, /device:TPU:1, one launch (start us, length us, event | category | flops | bytes accessed | tf_op | source)
XLA Modules:
  0.0 87.9 jit_solution(16288984237647108446)
XLA Ops:
  0.6 0.0 copy-start.1
  0.6 0.8 copy-done.1
  1.5 0.0 copy-start.2
  1.5 0.8 copy-done.2
  2.2 1.0 %shard_map.50 = (f32[8,64,128]{2,1,0:T(8,128)}, f32[32,384]{1,0:T(8,128)S(1)}) custom-call(f32[32,4,96]{2,1,0:T(4,128)S(1)} %copy-done.1, f32[16,4,96]{2,1,0:T(4,128)S(1)} %copy-done.2), custom_call_target="tpu_custom_call" | custom-call | flops 10000000000 | bytes 40000000 | tf_op jit(solution)/shard_map/pallas_call | solution.py:34
  3.3 7.7 %all-to-all-start = ((f32[8,64,128]{2,1,0:T(8,128)}), f32[8,64,128]{2,1,0:T(8,128)S(1)}, u32[]{:S(2)}, u32[]{:S(2)}) async-start(f32[8,64,128]{2,1,0:T(8,128)} %get-tuple-element.6), calls=%async_computation | async-start | bytes 524288 | tf_op jit(solution)/shard_map/all_to_all | solution.py:211
  10.9 17.2 %all_gather.3.b_ref = f32[128,384]{1,0:T(8,128)S(1)} all-gather(f32[32,384]{1,0:T(8,128)S(1)} %get-tuple-element.7), channel_id=1, replica_groups=mesh['ia'=16,'ja'=8,'ka'=4] {'ka'}, dimensions={0}, use_global_device_ids=true | all-gather | bytes 245760 | tf_op jit(solution)/shard_map/all_gather | solution.py:212
  28.1 0.0 all-to-all-done.c_got_ref
  28.1 0.0 copy-done
  28.1 2.1 %shard_map.51 = f32[32,16,128]{2,1,0:T(8,128)S(1)} custom-call(f32[32,128,128]{2,1,0:T(8,128)S(1)} %copy-done, f32[8,64,128]{2,1,0:T(8,128)S(1)} %all-to-all-done.c_got_ref, f32[128,384]{1,0:T(8,128)S(1)} %all_gather.3.b_ref), custom_call_target="tpu_custom_call" | custom-call | tf_op jit(solution)/shard_map/pallas_call | solution.py:34
  30.2 21.5 %all_to_all.20.got_ref = f32[32,16,128]{2,1,0:T(8,128)S(1)} all-to-all(f32[32,16,128]{2,1,0:T(8,128)S(1)} %shard_map.51), channel_id=1, replica_groups=mesh['ia'=16,'ja'=8,'ka'=4] {'ja','ka'}, dimensions={0} | all-to-all | bytes 524288 | tf_op jit(solution)/shard_map/all_to_all | solution.py:214
  51.7 0.7 shard_map.52.own_ref
  52.4 4.5 %all-to-all-start.2 = ((f32[32,4,128]{2,1,0:T(4,128)}), f32[32,4,128]{2,1,0:T(4,128)S(1)}, u32[]{:S(2)}, u32[]{:S(2)}) async-start(f32[32,4,128]{2,1,0:T(4,128)} %shard_map.52.own_ref), calls=%async_computation.2 | async-start | bytes 131072 | tf_op jit(solution)/shard_map/all_to_all | solution.py:216
  57.0 4.6 %shard_map.53.refs_0_ = f32[1,96,128]{2,1,0:T(8,128)S(1)} custom-call(f32[32,16,128]{2,1,0:T(8,128)S(1)} %all_to_all.20.got_ref), custom_call_target="tpu_custom_call" | custom-call | flops 10000000000 | bytes 40000000 | tf_op jit(solution)/shard_map/pallas_call | solution.py:34
  61.6 7.9 %collective-permute-start.2 = (f32[1,96,128]{2,1,0:T(8,128)S(1)}, f32[1,96,128]{2,1,0:T(8,128)S(1)}, u32[]{:S(2)}, u32[]{:S(2)}) collective-permute-start(f32[1,96,128]{2,1,0:T(8,128)S(1)} %shard_map.53.refs_0_), channel_id=1, source_target_pairs={{0,96},{32,64},{64,32},{96,0},{128,224},{160,192},{192,160},{224,1... | collective-permute-start | bytes 147464 | tf_op jit(solution)/shard_map/ppermute | solution.py:218
  69.5 2.2 %collective-permute-start.1 = (f32[1,96,128]{2,1,0:T(8,128)S(1)}, f32[1,96,128]{2,1,0:T(8,128)S(1)}, u32[]{:S(2)}, u32[]{:S(2)}) collective-permute-start(f32[1,96,128]{2,1,0:T(8,128)S(1)} %shard_map.53.refs_0_), channel_id=1, source_target_pairs={{0,64},{32,96},{64,0},{96,32},{128,192},{160,224},{192,128},{224,1... | collective-permute-start | bytes 147464 | tf_op jit(solution)/shard_map/ppermute | solution.py:218
  71.7 2.1 %collective-permute-start = (f32[1,96,128]{2,1,0:T(8,128)S(1)}, f32[1,96,128]{2,1,0:T(8,128)S(1)}, u32[]{:S(2)}, u32[]{:S(2)}) collective-permute-start(f32[1,96,128]{2,1,0:T(8,128)S(1)} %shard_map.53.refs_0_), channel_id=1, source_target_pairs={{0,32},{32,0},{64,96},{96,64},{128,160},{160,128},{192,224},{224,1... | collective-permute-start | bytes 147464 | tf_op jit(solution)/shard_map/ppermute | solution.py:218
  73.7 0.0 collective-permute-done.2.refs_3_
  73.8 0.6 collective-permute-done.1.refs_2_
  74.3 0.5 collective-permute-done.refs_1_
  74.8 0.0 all-to-all-done.2.m_ref
  74.8 1.2 %shard_map.54 = (f32[16,4,128]{2,1,0:T(4,128)S(1)}, f32[4,128]{1,0:T(4,128)S(1)}) custom-call(f32[32,4,128]{2,1,0:T(4,128)S(1)} %all-to-all-done.2.m_ref, f32[32,4,128]{2,1,0:T(4,128)} %shard_map.52.own_ref, f32[1,96,128]{2,1,0:T(8,128)S(1)} %shard_map.53.refs_0_, f32[1,96,128]{2,1,0:T(8,128)S(1)} %collective-permute-done.refs_1_, ...), custom_call_target="tpu_custom_call" | custom-call | tf_op jit(solution)/shard_map/pallas_call | solution.py:34
  76.0 11.3 %all_to_all.21.got_ref = f32[16,4,128]{2,1,0:T(4,128)S(1)} all-to-all(f32[16,4,128]{2,1,0:T(4,128)S(1)} %get-tuple-element.8), channel_id=1, replica_groups=mesh['ia'=16,'ja'=8,'ka'=4] {'ia'}, dimensions={0} | all-to-all | bytes 65536 | tf_op jit(solution)/shard_map/all_to_all | solution.py:220
  87.3 0.6 shard_map.55
  (1 shorter events, 0.0 us)
Async XLA Ops:
  0.6 0.8 copy-start.1
  1.5 0.8 copy-start.2
  2.2 25.8 %copy-start = (f32[32,128,128]{2,1,0:T(8,128)S(1)}, f32[32,128,128]{2,1,0:T(8,128)}, u32[]{:S(2)}) copy-start(f32[32,128,128]{2,1,0:T(8,128)} %t_ref.1) | copy-start | bytes 6291460
  3.3 24.8 %all-to-all-start = ((f32[8,64,128]{2,1,0:T(8,128)}), f32[8,64,128]{2,1,0:T(8,128)S(1)}, u32[]{:S(2)}, u32[]{:S(2)}) async-start(f32[8,64,128]{2,1,0:T(8,128)} %get-tuple-element.6), calls=%async_computation | async-start | bytes 524288 | tf_op jit(solution)/shard_map/all_to_all | solution.py:211
  52.4 22.4 %all-to-all-start.2 = ((f32[32,4,128]{2,1,0:T(4,128)}), f32[32,4,128]{2,1,0:T(4,128)S(1)}, u32[]{:S(2)}, u32[]{:S(2)}) async-start(f32[32,4,128]{2,1,0:T(4,128)} %shard_map.52.own_ref), calls=%async_computation.2 | async-start | bytes 131072 | tf_op jit(solution)/shard_map/all_to_all | solution.py:216
  61.6 12.2 %collective-permute-start.2 = (f32[1,96,128]{2,1,0:T(8,128)S(1)}, f32[1,96,128]{2,1,0:T(8,128)S(1)}, u32[]{:S(2)}, u32[]{:S(2)}) collective-permute-start(f32[1,96,128]{2,1,0:T(8,128)S(1)} %shard_map.53.refs_0_), channel_id=1, source_target_pairs={{0,96},{32,64},{64,32},{96,0},{128,224},{160,192},{192,160},{224,1... | collective-permute-start | bytes 147464 | tf_op jit(solution)/shard_map/ppermute | solution.py:218
  69.5 4.8 %collective-permute-start.1 = (f32[1,96,128]{2,1,0:T(8,128)S(1)}, f32[1,96,128]{2,1,0:T(8,128)S(1)}, u32[]{:S(2)}, u32[]{:S(2)}) collective-permute-start(f32[1,96,128]{2,1,0:T(8,128)S(1)} %shard_map.53.refs_0_), channel_id=1, source_target_pairs={{0,64},{32,96},{64,0},{96,32},{128,192},{160,224},{192,128},{224,1... | collective-permute-start | bytes 147464 | tf_op jit(solution)/shard_map/ppermute | solution.py:218
  71.7 3.1 %collective-permute-start = (f32[1,96,128]{2,1,0:T(8,128)S(1)}, f32[1,96,128]{2,1,0:T(8,128)S(1)}, u32[]{:S(2)}, u32[]{:S(2)}) collective-permute-start(f32[1,96,128]{2,1,0:T(8,128)S(1)} %shard_map.53.refs_0_), channel_id=1, source_target_pairs={{0,32},{32,0},{64,96},{96,64},{128,160},{160,128},{192,224},{224,1... | collective-permute-start | bytes 147464 | tf_op jit(solution)/shard_map/ppermute | solution.py:218

commit v13 on v12

--- a/solution.py
+++ b/solution.py
@@ -13,6 +13,7 @@
 S = 4
 W = S * R
 VMEM = pl.BlockSpec(memory_space=pltpu.VMEM)
+HBM = pl.BlockSpec(memory_space=pltpu.HBM)
 
 
 def dot(a, b, dims, precision=highest):
@@ -27,17 +28,17 @@
     return lax.broadcasted_iota(jnp.int32, shape, 0)
 
 
-def call(body, out, cost=None, scratch=()):
+def call(body, out, cost=None, scratch=(), hbm=0, limit=32):
     shapes = [jax.ShapeDtypeStruct(o, f32) for o in out]
 
     def run(*args):
         return pl.pallas_call(
             body,
             out_shape=shapes,
-            in_specs=[VMEM] * len(args),
+            in_specs=[HBM] * hbm + [VMEM] * (len(args) - hbm),
             out_specs=[VMEM] * len(shapes),
             scratch_shapes=list(scratch),
-            compiler_params=pltpu.CompilerParams(vmem_limit_bytes=32 * 1024 * 1024),
+            compiler_params=pltpu.CompilerParams(vmem_limit_bytes=limit * 1024 * 1024),
             cost_estimate=cost,
         )(*args)
 
@@ -55,7 +56,13 @@
     return out
 
 
-def prepare(fb_ref, fc_ref, out_ref, b_ref):
+def prepare(fb_hbm, fc_hbm, out_ref, b_ref, fb_ref, fc_ref, sems):
+    copy_b = pltpu.make_async_copy(fb_hbm, fb_ref, sems.at[0])
+    copy_c = pltpu.make_async_copy(fc_hbm, fc_ref, sems.at[1])
+    copy_b.start()
+    copy_c.start()
+    copy_b.wait()
+    copy_c.wait()
     peers, nc = out_ref.shape[0], fc_ref.shape[0]
     b = pick(start_of(), [fb_ref[:, s, :] for s in range(S)])
     c = pick(start_of(), [fc_ref[:, s, :] for s in range(S)])
@@ -207,7 +214,14 @@
     ia, ja, ka = (lax.axis_size(a) for a in ("ia", "ja", "ka"))
     nb, nc = factor_b.shape[0], factor_c.shape[0]
     cost = pl.CostEstimate(flops=int(1e10), bytes_accessed=int(4e7), transcendentals=0)
-    slots_c, b_flat = call(prepare, [(ja, 3 * nc + 16, 128), (nb, W)], cost=cost)(factor_b, factor_c)
+    slots_c, b_flat = call(
+        prepare,
+        [(ja, 3 * nc + 16, 128), (nb, W)],
+        cost=cost,
+        scratch=[pltpu.VMEM(factor_b.shape, f32), pltpu.VMEM(factor_c.shape, f32), pltpu.SemaphoreType.DMA((2,))],
+        hbm=2,
+        limit=56,
+    )(factor_b, factor_c)
     got_c = lax.all_to_all(slots_c, "ja", 0, 0)
     b_block = lax.all_gather(b_flat, "ka", axis=0, tiled=True)
     slots_m = call(contract, [(ja * ka, 16, 128)], scratch=[pltpu.VMEM((ni, W), f32)])(tensor, got_c, b_block)[0]

time: 88.5 us -> 88 us (level)
  local copies, waits for them, and re-layouts: 1.59 us -> 0.01 us
  Pallas kernels: 10.3 us -> 11.3 us
    unnamed x6 -> x2, local copies, waits for them, and re-layouts: 1.59 us -> 0.01 us
    pallas_call x6, Pallas kernels: 10.3 us -> 11.3 us  [run(): pl.pallas_call(body, out_shape=shapes, in_specs=[HBM] * hbm + [VMEM] * (l...]
where the time goes in v13:
time: 88 us; the launch traced here: 87.6 us
  blocking collectives  50.2 us (57%)
  starting transfers between devices  24.3 us (28%)
  Pallas kernels  11.3 us (13%)
  waiting for transfers between devices  1.05 us (1%)
    all_to_all x1, blocking collectives, shards(): got_m = lax.all_to_all(slots_m, ('ja', 'ka'), 0, 0)  21.5 us
    all_gather x1, blocking collectives, shards(): b_block = lax.all_gather(b_flat, 'ka', axis=0, tiled=True)  17.4 us
    ppermute x3, starting transfers between devices, shards(): lax.ppermute(inverse, 'ia', [(n, n ^ d) for n in range(ia)])  12.1 us
    all_to_all x1, blocking collectives, shards(): got_s = lax.all_to_all(squares, 'ia', 0, 0)  11.3 us
    pallas_call x6, Pallas kernels, run(): pl.pallas_call(body, out_shape=shapes, in_specs=[HBM] * hbm + [VMEM] * (l...  11.3 us
    all_to_all x1, starting transfers between devices, shards(): got_c = lax.all_to_all(slots_c, 'ja', 0, 0)  7.66 us
    all_to_all x1, starting transfers between devices, shards(): all_rows = lax.all_to_all(own, ('ja', 'ka'), 0, 0)  4.53 us
  transfers between devices with their start and end apart: 5, of which 2 were waited for; matrix products, arithmetic and copies ran while one was open for 0% of the time, Pallas kernels for 5%

profile of v13, /device:TPU:1, one launch (start us, length us, event | category | flops | bytes accessed | tf_op | source)
XLA Modules:
  0.0 87.6 jit_solution(14144922125673228816)
XLA Ops:
  0.6 0.0 copy-start
  0.6 2.0 %shard_map.50 = (f32[8,64,128]{2,1,0:T(8,128)}, f32[32,384]{1,0:T(8,128)}) custom-call(f32[32,4,96]{2,1,0:T(4,128)} %fb_hbm.1, f32[16,4,96]{2,1,0:T(4,128)} %fc_hbm.1), custom_call_target="tpu_custom_call" | custom-call | flops 10000000000 | bytes 40000000 | tf_op jit(solution)/shard_map/pallas_call | solution.py:35
  2.7 7.7 %all-to-all-start = ((f32[8,64,128]{2,1,0:T(8,128)}), f32[8,64,128]{2,1,0:T(8,128)S(1)}, u32[]{:S(2)}, u32[]{:S(2)}) async-start(f32[8,64,128]{2,1,0:T(8,128)} %get-tuple-element.6), calls=%async_computation | async-start | bytes 524288 | tf_op jit(solution)/shard_map/all_to_all | solution.py:225
  10.3 17.4 %all_gather.3.b_ref = f32[128,384]{1,0:T(8,128)S(1)} all-gather(f32[32,384]{1,0:T(8,128)} %get-tuple-element.7), channel_id=1, replica_groups=mesh['ia'=16,'ja'=8,'ka'=4] {'ka'}, dimensions={0}, use_global_device_ids=true | all-gather | bytes 245760 | tf_op jit(solution)/shard_map/all_gather | solution.py:226
  27.8 0.0 all-to-all-done.c_got_ref
  27.8 0.0 copy-done
  27.8 2.1 %shard_map.51 = f32[32,16,128]{2,1,0:T(8,128)S(1)} custom-call(f32[32,128,128]{2,1,0:T(8,128)S(1)} %copy-done, f32[8,64,128]{2,1,0:T(8,128)S(1)} %all-to-all-done.c_got_ref, f32[128,384]{1,0:T(8,128)S(1)} %all_gather.3.b_ref), custom_call_target="tpu_custom_call" | custom-call | tf_op jit(solution)/shard_map/pallas_call | solution.py:35
  29.9 21.5 %all_to_all.20.got_ref = f32[32,16,128]{2,1,0:T(8,128)S(1)} all-to-all(f32[32,16,128]{2,1,0:T(8,128)S(1)} %shard_map.51), channel_id=1, replica_groups=mesh['ia'=16,'ja'=8,'ka'=4] {'ja','ka'}, dimensions={0} | all-to-all | bytes 524288 | tf_op jit(solution)/shard_map/all_to_all | solution.py:228
  51.3 0.7 shard_map.52.own_ref
  52.1 4.5 %all-to-all-start.2 = ((f32[32,4,128]{2,1,0:T(4,128)}), f32[32,4,128]{2,1,0:T(4,128)S(1)}, u32[]{:S(2)}, u32[]{:S(2)}) async-start(f32[32,4,128]{2,1,0:T(4,128)} %shard_map.52.own_ref), calls=%async_computation.2 | async-start | bytes 131072 | tf_op jit(solution)/shard_map/all_to_all | solution.py:230
  56.6 4.6 %shard_map.53.refs_0_ = f32[1,96,128]{2,1,0:T(8,128)S(1)} custom-call(f32[32,16,128]{2,1,0:T(8,128)S(1)} %all_to_all.20.got_ref), custom_call_target="tpu_custom_call" | custom-call | flops 10000000000 | bytes 40000000 | tf_op jit(solution)/shard_map/pallas_call | solution.py:35
  61.2 7.9 %collective-permute-start.2 = (f32[1,96,128]{2,1,0:T(8,128)S(1)}, f32[1,96,128]{2,1,0:T(8,128)S(1)}, u32[]{:S(2)}, u32[]{:S(2)}) collective-permute-start(f32[1,96,128]{2,1,0:T(8,128)S(1)} %shard_map.53.refs_0_), channel_id=1, source_target_pairs={{0,96},{32,64},{64,32},{96,0},{128,224},{160,192},{192,160},{224,1... | collective-permute-start | bytes 147464 | tf_op jit(solution)/shard_map/ppermute | solution.py:232
  69.1 2.2 %collective-permute-start.1 = (f32[1,96,128]{2,1,0:T(8,128)S(1)}, f32[1,96,128]{2,1,0:T(8,128)S(1)}, u32[]{:S(2)}, u32[]{:S(2)}) collective-permute-start(f32[1,96,128]{2,1,0:T(8,128)S(1)} %shard_map.53.refs_0_), channel_id=1, source_target_pairs={{0,64},{32,96},{64,0},{96,32},{128,192},{160,224},{192,128},{224,1... | collective-permute-start | bytes 147464 | tf_op jit(solution)/shard_map/ppermute | solution.py:232
  71.3 2.1 %collective-permute-start = (f32[1,96,128]{2,1,0:T(8,128)S(1)}, f32[1,96,128]{2,1,0:T(8,128)S(1)}, u32[]{:S(2)}, u32[]{:S(2)}) collective-permute-start(f32[1,96,128]{2,1,0:T(8,128)S(1)} %shard_map.53.refs_0_), channel_id=1, source_target_pairs={{0,32},{32,0},{64,96},{96,64},{128,160},{160,128},{192,224},{224,1... | collective-permute-start | bytes 147464 | tf_op jit(solution)/shard_map/ppermute | solution.py:232
  73.4 0.0 collective-permute-done.2.refs_3_
  73.4 0.6 collective-permute-done.1.refs_2_
  74.0 0.5 collective-permute-done.refs_1_
  74.4 0.0 all-to-all-done.2.m_ref
  74.4 1.2 %shard_map.54 = (f32[16,4,128]{2,1,0:T(4,128)S(1)}, f32[4,128]{1,0:T(4,128)S(1)}) custom-call(f32[32,4,128]{2,1,0:T(4,128)S(1)} %all-to-all-done.2.m_ref, f32[32,4,128]{2,1,0:T(4,128)} %shard_map.52.own_ref, f32[1,96,128]{2,1,0:T(8,128)S(1)} %shard_map.53.refs_0_, f32[1,96,128]{2,1,0:T(8,128)S(1)} %collective-permute-done.refs_1_, ...), custom_call_target="tpu_custom_call" | custom-call | tf_op jit(solution)/shard_map/pallas_call | solution.py:35
  75.6 11.3 %all_to_all.21.got_ref = f32[16,4,128]{2,1,0:T(4,128)S(1)} all-to-all(f32[16,4,128]{2,1,0:T(4,128)S(1)} %get-tuple-element.8), channel_id=1, replica_groups=mesh['ia'=16,'ja'=8,'ka'=4] {'ia'}, dimensions={0} | all-to-all | bytes 65536 | tf_op jit(solution)/shard_map/all_to_all | solution.py:234
  86.9 0.6 shard_map.55
Async XLA Ops:
  0.6 27.1 %copy-start = (f32[32,128,128]{2,1,0:T(8,128)S(1)}, f32[32,128,128]{2,1,0:T(8,128)}, u32[]{:S(2)}) copy-start(f32[32,128,128]{2,1,0:T(8,128)} %t_ref.1) | copy-start | bytes 6291460
  2.7 25.1 %all-to-all-start = ((f32[8,64,128]{2,1,0:T(8,128)}), f32[8,64,128]{2,1,0:T(8,128)S(1)}, u32[]{:S(2)}, u32[]{:S(2)}) async-start(f32[8,64,128]{2,1,0:T(8,128)} %get-tuple-element.6), calls=%async_computation | async-start | bytes 524288 | tf_op jit(solution)/shard_map/all_to_all | solution.py:225
  52.1 22.4 %all-to-all-start.2 = ((f32[32,4,128]{2,1,0:T(4,128)}), f32[32,4,128]{2,1,0:T(4,128)S(1)}, u32[]{:S(2)}, u32[]{:S(2)}) async-start(f32[32,4,128]{2,1,0:T(4,128)} %shard_map.52.own_ref), calls=%async_computation.2 | async-start | bytes 131072 | tf_op jit(solution)/shard_map/all_to_all | solution.py:230
  61.2 12.2 %collective-permute-start.2 = (f32[1,96,128]{2,1,0:T(8,128)S(1)}, f32[1,96,128]{2,1,0:T(8,128)S(1)}, u32[]{:S(2)}, u32[]{:S(2)}) collective-permute-start(f32[1,96,128]{2,1,0:T(8,128)S(1)} %shard_map.53.refs_0_), channel_id=1, source_target_pairs={{0,96},{32,64},{64,32},{96,0},{128,224},{160,192},{192,160},{224,1... | collective-permute-start | bytes 147464 | tf_op jit(solution)/shard_map/ppermute | solution.py:232
  69.1 4.8 %collective-permute-start.1 = (f32[1,96,128]{2,1,0:T(8,128)S(1)}, f32[1,96,128]{2,1,0:T(8,128)S(1)}, u32[]{:S(2)}, u32[]{:S(2)}) collective-permute-start(f32[1,96,128]{2,1,0:T(8,128)S(1)} %shard_map.53.refs_0_), channel_id=1, source_target_pairs={{0,64},{32,96},{64,0},{96,32},{128,192},{160,224},{192,128},{224,1... | collective-permute-start | bytes 147464 | tf_op jit(solution)/shard_map/ppermute | solution.py:232
  71.3 3.1 %collective-permute-start = (f32[1,96,128]{2,1,0:T(8,128)S(1)}, f32[1,96,128]{2,1,0:T(8,128)S(1)}, u32[]{:S(2)}, u32[]{:S(2)}) collective-permute-start(f32[1,96,128]{2,1,0:T(8,128)S(1)} %shard_map.53.refs_0_), channel_id=1, source_target_pairs={{0,32},{32,0},{64,96},{96,64},{128,160},{160,128},{192,224},{224,1... | collective-permute-start | bytes 147464 | tf_op jit(solution)/shard_map/ppermute | solution.py:232

commit v14 on v13

--- a/solution.py
+++ b/solution.py
@@ -93,14 +93,13 @@
     b = b_ref[...]
     c_high = c.astype(bf16)
     c_low = (c - c_high.astype(f32)).astype(bf16)
-    twice = jnp.concatenate([c_high, c_high], axis=0)
+    parts = jnp.concatenate([c_high, c_high, c_low], axis=0)
     group = 8
     for at in range(0, ni, group):
         t = t_ref[at : at + group, :, :].reshape(group * nj, nk)
         t_high = t.astype(bf16)
         t_low = (t - t_high.astype(f32)).astype(bf16)
-        both = jnp.concatenate([t_high, t_low], axis=1)
-        value = dot(both, twice, ((1,), (0,)), None) + dot(t_high, c_low, ((1,), (0,)), None)
+        value = dot(jnp.concatenate([t_high, t_low, t_high], axis=1), parts, ((1,), (0,)), None)
         m_ref[at : at + group, :] = jnp.sum(value.reshape(group, nj, W) * b[None], axis=1)
     share = jnp.sum(c_got_ref[:, 3 * nc :, :], axis=0)
     out_ref[...] = jnp.broadcast_to(share[None], out_ref.shape)

time: 88 us -> 88 us (level)
  no operation moved by 1% of the time
where the time goes in v14:
time: 88 us; the launch traced here: 87.6 us
  blocking collectives  50.2 us (57%)
  starting transfers between devices  24.3 us (28%)
  Pallas kernels  11.3 us (13%)
  waiting for transfers between devices  1.05 us (1%)
    all_to_all x1, blocking collectives, shards(): got_m = lax.all_to_all(slots_m, ('ja', 'ka'), 0, 0)  21.5 us
    all_gather x1, blocking collectives, shards(): b_block = lax.all_gather(b_flat, 'ka', axis=0, tiled=True)  17.4 us
    ppermute x3, starting transfers between devices, shards(): lax.ppermute(inverse, 'ia', [(n, n ^ d) for n in range(ia)])  12.1 us
    all_to_all x1, blocking collectives, shards(): got_s = lax.all_to_all(squares, 'ia', 0, 0)  11.3 us
    pallas_call x6, Pallas kernels, run(): pl.pallas_call(body, out_shape=shapes, in_specs=[HBM] * hbm + [VMEM] * (l...  11.3 us
    all_to_all x1, starting transfers between devices, shards(): got_c = lax.all_to_all(slots_c, 'ja', 0, 0)  7.66 us
    all_to_all x1, starting transfers between devices, shards(): all_rows = lax.all_to_all(own, ('ja', 'ka'), 0, 0)  4.53 us
  transfers between devices with their start and end apart: 5, of which 2 were waited for; matrix products, arithmetic and copies ran while one was open for 0% of the time, Pallas kernels for 5%

profile of v14, /device:TPU:1, one launch (start us, length us, event | category | flops | bytes accessed | tf_op | source)
XLA Modules:
  0.0 87.6 jit_solution(12609608584744754539)
XLA Ops:
  0.6 0.0 copy-start
  0.6 2.0 %shard_map.50 = (f32[8,64,128]{2,1,0:T(8,128)}, f32[32,384]{1,0:T(8,128)}) custom-call(f32[32,4,96]{2,1,0:T(4,128)} %fb_hbm.1, f32[16,4,96]{2,1,0:T(4,128)} %fc_hbm.1), custom_call_target="tpu_custom_call" | custom-call | flops 10000000000 | bytes 40000000 | tf_op jit(solution)/shard_map/pallas_call | solution.py:35
  2.7 7.7 %all-to-all-start = ((f32[8,64,128]{2,1,0:T(8,128)}), f32[8,64,128]{2,1,0:T(8,128)S(1)}, u32[]{:S(2)}, u32[]{:S(2)}) async-start(f32[8,64,128]{2,1,0:T(8,128)} %get-tuple-element.6), calls=%async_computation | async-start | bytes 524288 | tf_op jit(solution)/shard_map/all_to_all | solution.py:224
  10.3 17.4 %all_gather.3.b_ref = f32[128,384]{1,0:T(8,128)S(1)} all-gather(f32[32,384]{1,0:T(8,128)} %get-tuple-element.7), channel_id=1, replica_groups=mesh['ia'=16,'ja'=8,'ka'=4] {'ka'}, dimensions={0}, use_global_device_ids=true | all-gather | bytes 245760 | tf_op jit(solution)/shard_map/all_gather | solution.py:225
  27.8 0.0 all-to-all-done.c_got_ref
  27.8 0.0 copy-done
  27.8 2.1 %shard_map.51 = f32[32,16,128]{2,1,0:T(8,128)S(1)} custom-call(f32[32,128,128]{2,1,0:T(8,128)S(1)} %copy-done, f32[8,64,128]{2,1,0:T(8,128)S(1)} %all-to-all-done.c_got_ref, f32[128,384]{1,0:T(8,128)S(1)} %all_gather.3.b_ref), custom_call_target="tpu_custom_call" | custom-call | tf_op jit(solution)/shard_map/pallas_call | solution.py:35
  29.9 21.5 %all_to_all.20.got_ref = f32[32,16,128]{2,1,0:T(8,128)S(1)} all-to-all(f32[32,16,128]{2,1,0:T(8,128)S(1)} %shard_map.51), channel_id=1, replica_groups=mesh['ia'=16,'ja'=8,'ka'=4] {'ja','ka'}, dimensions={0} | all-to-all | bytes 524288 | tf_op jit(solution)/shard_map/all_to_all | solution.py:227
  51.3 0.7 shard_map.52.own_ref
  52.1 4.5 %all-to-all-start.2 = ((f32[32,4,128]{2,1,0:T(4,128)}), f32[32,4,128]{2,1,0:T(4,128)S(1)}, u32[]{:S(2)}, u32[]{:S(2)}) async-start(f32[32,4,128]{2,1,0:T(4,128)} %shard_map.52.own_ref), calls=%async_computation.2 | async-start | bytes 131072 | tf_op jit(solution)/shard_map/all_to_all | solution.py:229
  56.6 4.6 %shard_map.53.refs_0_ = f32[1,96,128]{2,1,0:T(8,128)S(1)} custom-call(f32[32,16,128]{2,1,0:T(8,128)S(1)} %all_to_all.20.got_ref), custom_call_target="tpu_custom_call" | custom-call | flops 10000000000 | bytes 40000000 | tf_op jit(solution)/shard_map/pallas_call | solution.py:35
  61.2 7.9 %collective-permute-start.2 = (f32[1,96,128]{2,1,0:T(8,128)S(1)}, f32[1,96,128]{2,1,0:T(8,128)S(1)}, u32[]{:S(2)}, u32[]{:S(2)}) collective-permute-start(f32[1,96,128]{2,1,0:T(8,128)S(1)} %shard_map.53.refs_0_), channel_id=1, source_target_pairs={{0,96},{32,64},{64,32},{96,0},{128,224},{160,192},{192,160},{224,1... | collective-permute-start | bytes 147464 | tf_op jit(solution)/shard_map/ppermute | solution.py:231
  69.2 2.2 %collective-permute-start.1 = (f32[1,96,128]{2,1,0:T(8,128)S(1)}, f32[1,96,128]{2,1,0:T(8,128)S(1)}, u32[]{:S(2)}, u32[]{:S(2)}) collective-permute-start(f32[1,96,128]{2,1,0:T(8,128)S(1)} %shard_map.53.refs_0_), channel_id=1, source_target_pairs={{0,64},{32,96},{64,0},{96,32},{128,192},{160,224},{192,128},{224,1... | collective-permute-start | bytes 147464 | tf_op jit(solution)/shard_map/ppermute | solution.py:231
  71.3 2.1 %collective-permute-start = (f32[1,96,128]{2,1,0:T(8,128)S(1)}, f32[1,96,128]{2,1,0:T(8,128)S(1)}, u32[]{:S(2)}, u32[]{:S(2)}) collective-permute-start(f32[1,96,128]{2,1,0:T(8,128)S(1)} %shard_map.53.refs_0_), channel_id=1, source_target_pairs={{0,32},{32,0},{64,96},{96,64},{128,160},{160,128},{192,224},{224,1... | collective-permute-start | bytes 147464 | tf_op jit(solution)/shard_map/ppermute | solution.py:231
  73.4 0.0 collective-permute-done.2.refs_3_
  73.4 0.6 collective-permute-done.1.refs_2_
  74.0 0.5 collective-permute-done.refs_1_
  74.5 0.0 all-to-all-done.2.m_ref
  74.5 1.2 %shard_map.54 = (f32[16,4,128]{2,1,0:T(4,128)S(1)}, f32[4,128]{1,0:T(4,128)S(1)}) custom-call(f32[32,4,128]{2,1,0:T(4,128)S(1)} %all-to-all-done.2.m_ref, f32[32,4,128]{2,1,0:T(4,128)} %shard_map.52.own_ref, f32[1,96,128]{2,1,0:T(8,128)S(1)} %shard_map.53.refs_0_, f32[1,96,128]{2,1,0:T(8,128)S(1)} %collective-permute-done.refs_1_, ...), custom_call_target="tpu_custom_call" | custom-call | tf_op jit(solution)/shard_map/pallas_call | solution.py:35
  75.6 11.3 %all_to_all.21.got_ref = f32[16,4,128]{2,1,0:T(4,128)S(1)} all-to-all(f32[16,4,128]{2,1,0:T(4,128)S(1)} %get-tuple-element.8), channel_id=1, replica_groups=mesh['ia'=16,'ja'=8,'ka'=4] {'ia'}, dimensions={0} | all-to-all | bytes 65536 | tf_op jit(solution)/shard_map/all_to_all | solution.py:233
  86.9 0.6 shard_map.55
Async XLA Ops:
  0.6 27.1 %copy-start = (f32[32,128,128]{2,1,0:T(8,128)S(1)}, f32[32,128,128]{2,1,0:T(8,128)}, u32[]{:S(2)}) copy-start(f32[32,128,128]{2,1,0:T(8,128)} %t_ref.1) | copy-start | bytes 6291460
  2.7 25.1 %all-to-all-start = ((f32[8,64,128]{2,1,0:T(8,128)}), f32[8,64,128]{2,1,0:T(8,128)S(1)}, u32[]{:S(2)}, u32[]{:S(2)}) async-start(f32[8,64,128]{2,1,0:T(8,128)} %get-tuple-element.6), calls=%async_computation | async-start | bytes 524288 | tf_op jit(solution)/shard_map/all_to_all | solution.py:224
  52.1 22.4 %all-to-all-start.2 = ((f32[32,4,128]{2,1,0:T(4,128)}), f32[32,4,128]{2,1,0:T(4,128)S(1)}, u32[]{:S(2)}, u32[]{:S(2)}) async-start(f32[32,4,128]{2,1,0:T(4,128)} %shard_map.52.own_ref), calls=%async_computation.2 | async-start | bytes 131072 | tf_op jit(solution)/shard_map/all_to_all | solution.py:229
  61.2 12.2 %collective-permute-start.2 = (f32[1,96,128]{2,1,0:T(8,128)S(1)}, f32[1,96,128]{2,1,0:T(8,128)S(1)}, u32[]{:S(2)}, u32[]{:S(2)}) collective-permute-start(f32[1,96,128]{2,1,0:T(8,128)S(1)} %shard_map.53.refs_0_), channel_id=1, source_target_pairs={{0,96},{32,64},{64,32},{96,0},{128,224},{160,192},{192,160},{224,1... | collective-permute-start | bytes 147464 | tf_op jit(solution)/shard_map/ppermute | solution.py:231
  69.2 4.8 %collective-permute-start.1 = (f32[1,96,128]{2,1,0:T(8,128)S(1)}, f32[1,96,128]{2,1,0:T(8,128)S(1)}, u32[]{:S(2)}, u32[]{:S(2)}) collective-permute-start(f32[1,96,128]{2,1,0:T(8,128)S(1)} %shard_map.53.refs_0_), channel_id=1, source_target_pairs={{0,64},{32,96},{64,0},{96,32},{128,192},{160,224},{192,128},{224,1... | collective-permute-start | bytes 147464 | tf_op jit(solution)/shard_map/ppermute | solution.py:231
  71.3 3.1 %collective-permute-start = (f32[1,96,128]{2,1,0:T(8,128)S(1)}, f32[1,96,128]{2,1,0:T(8,128)S(1)}, u32[]{:S(2)}, u32[]{:S(2)}) collective-permute-start(f32[1,96,128]{2,1,0:T(8,128)S(1)} %shard_map.53.refs_0_), channel_id=1, source_target_pairs={{0,32},{32,0},{64,96},{96,64},{128,160},{160,128},{192,224},{224,1... | collective-permute-start | bytes 147464 | tf_op jit(solution)/shard_map/ppermute | solution.py:231

commit v15 on v13

--- a/solution.py
+++ b/solution.py
@@ -59,11 +59,15 @@
 def prepare(fb_hbm, fc_hbm, out_ref, b_ref, fb_ref, fc_ref, sems):
     copy_b = pltpu.make_async_copy(fb_hbm, fb_ref, sems.at[0])
     copy_c = pltpu.make_async_copy(fc_hbm, fc_ref, sems.at[1])
+    copy_c.start()
     copy_b.start()
-    copy_c.start()
-    copy_b.wait()
     copy_c.wait()
     peers, nc = out_ref.shape[0], fc_ref.shape[0]
+    c_flat = jnp.concatenate([fc_ref[:, s, :] for s in range(S)], axis=1)
+    for p in range(peers):
+        for q in range(3):
+            out_ref[p, q * nc : (q + 1) * nc, :] = c_flat[:, q * 128 : (q + 1) * 128]
+    copy_b.wait()
     b = pick(start_of(), [fb_ref[:, s, :] for s in range(S)])
     c = pick(start_of(), [fc_ref[:, s, :] for s in range(S)])
     wide_b = jnp.concatenate([b, jnp.zeros((b.shape[0], 128 - R), f32)], axis=1)
@@ -71,13 +75,10 @@
     gram_b = dot(b, wide_b, ((0,), (0,)))
     gram_c = dot(c, pltpu.roll(wide_c, 1, 1), ((0,), (0,)))
     z = jnp.where(lanes((R, 128)) <= rows((R, 128)), gram_b, gram_c)
-    c_flat = jnp.concatenate([fc_ref[:, s, :] for s in range(S)], axis=1)
     b_ref[...] = jnp.concatenate([fb_ref[:, s, :] for s in range(S)], axis=1)
     depth = R // peers
     fill = jnp.zeros((out_ref.shape[1] - 3 * nc - depth, 128), f32)
     for p in range(peers):
-        for q in range(3):
-            out_ref[p, q * nc : (q + 1) * nc, :] = c_flat[:, q * 128 : (q + 1) * 128]
         out_ref[p, 3 * nc :, :] = jnp.concatenate([z[p * depth : (p + 1) * depth], fill], axis=0)
 
 

time: 88 us -> 88 us (level)
  no operation moved by 1% of the time
where the time goes in v15:
time: 88 us; the launch traced here: 87.6 us
  blocking collectives  50.2 us (57%)
  starting transfers between devices  24.3 us (28%)
  Pallas kernels  11.3 us (13%)
  waiting for transfers between devices  1.05 us (1%)
    all_to_all x1, blocking collectives, shards(): got_m = lax.all_to_all(slots_m, ('ja', 'ka'), 0, 0)  21.5 us
    all_gather x1, blocking collectives, shards(): b_block = lax.all_gather(b_flat, 'ka', axis=0, tiled=True)  17.4 us
    ppermute x3, starting transfers between devices, shards(): lax.ppermute(inverse, 'ia', [(n, n ^ d) for n in range(ia)])  12.1 us
    all_to_all x1, blocking collectives, shards(): got_s = lax.all_to_all(squares, 'ia', 0, 0)  11.3 us
    pallas_call x6, Pallas kernels, run(): pl.pallas_call(body, out_shape=shapes, in_specs=[HBM] * hbm + [VMEM] * (l...  11.3 us
    all_to_all x1, starting transfers between devices, shards(): got_c = lax.all_to_all(slots_c, 'ja', 0, 0)  7.66 us
    all_to_all x1, starting transfers between devices, shards(): all_rows = lax.all_to_all(own, ('ja', 'ka'), 0, 0)  4.53 us
  transfers between devices with their start and end apart: 5, of which 2 were waited for; matrix products, arithmetic and copies ran while one was open for 0% of the time, Pallas kernels for 5%

profile of v15, /device:TPU:1, one launch (start us, length us, event | category | flops | bytes accessed | tf_op | source)
XLA Modules:
  0.0 87.6 jit_solution(352871924238075347)
XLA Ops:
  0.6 0.0 copy-start
  0.6 2.0 %shard_map.50 = (f32[8,64,128]{2,1,0:T(8,128)}, f32[32,384]{1,0:T(8,128)}) custom-call(f32[32,4,96]{2,1,0:T(4,128)} %fb_hbm.1, f32[16,4,96]{2,1,0:T(4,128)} %fc_hbm.1), custom_call_target="tpu_custom_call" | custom-call | flops 10000000000 | bytes 40000000 | tf_op jit(solution)/shard_map/pallas_call | solution.py:35
  2.7 7.7 %all-to-all-start = ((f32[8,64,128]{2,1,0:T(8,128)}), f32[8,64,128]{2,1,0:T(8,128)S(1)}, u32[]{:S(2)}, u32[]{:S(2)}) async-start(f32[8,64,128]{2,1,0:T(8,128)} %get-tuple-element.6), calls=%async_computation | async-start | bytes 524288 | tf_op jit(solution)/shard_map/all_to_all | solution.py:226
  10.4 17.4 %all_gather.3.b_ref = f32[128,384]{1,0:T(8,128)S(1)} all-gather(f32[32,384]{1,0:T(8,128)} %get-tuple-element.7), channel_id=1, replica_groups=mesh['ia'=16,'ja'=8,'ka'=4] {'ka'}, dimensions={0}, use_global_device_ids=true | all-gather | bytes 245760 | tf_op jit(solution)/shard_map/all_gather | solution.py:227
  27.8 0.0 all-to-all-done.c_got_ref
  27.8 0.0 copy-done
  27.8 2.1 %shard_map.51 = f32[32,16,128]{2,1,0:T(8,128)S(1)} custom-call(f32[32,128,128]{2,1,0:T(8,128)S(1)} %copy-done, f32[8,64,128]{2,1,0:T(8,128)S(1)} %all-to-all-done.c_got_ref, f32[128,384]{1,0:T(8,128)S(1)} %all_gather.3.b_ref), custom_call_target="tpu_custom_call" | custom-call | tf_op jit(solution)/shard_map/pallas_call | solution.py:35
  29.9 21.5 %all_to_all.20.got_ref = f32[32,16,128]{2,1,0:T(8,128)S(1)} all-to-all(f32[32,16,128]{2,1,0:T(8,128)S(1)} %shard_map.51), channel_id=1, replica_groups=mesh['ia'=16,'ja'=8,'ka'=4] {'ja','ka'}, dimensions={0} | all-to-all | bytes 524288 | tf_op jit(solution)/shard_map/all_to_all | solution.py:229
  51.4 0.7 shard_map.52.own_ref
  52.1 4.5 %all-to-all-start.2 = ((f32[32,4,128]{2,1,0:T(4,128)}), f32[32,4,128]{2,1,0:T(4,128)S(1)}, u32[]{:S(2)}, u32[]{:S(2)}) async-start(f32[32,4,128]{2,1,0:T(4,128)} %shard_map.52.own_ref), calls=%async_computation.2 | async-start | bytes 131072 | tf_op jit(solution)/shard_map/all_to_all | solution.py:231
  56.6 4.6 %shard_map.53.refs_0_ = f32[1,96,128]{2,1,0:T(8,128)S(1)} custom-call(f32[32,16,128]{2,1,0:T(8,128)S(1)} %all_to_all.20.got_ref), custom_call_target="tpu_custom_call" | custom-call | flops 10000000000 | bytes 40000000 | tf_op jit(solution)/shard_map/pallas_call | solution.py:35
  61.2 7.9 %collective-permute-start.2 = (f32[1,96,128]{2,1,0:T(8,128)S(1)}, f32[1,96,128]{2,1,0:T(8,128)S(1)}, u32[]{:S(2)}, u32[]{:S(2)}) collective-permute-start(f32[1,96,128]{2,1,0:T(8,128)S(1)} %shard_map.53.refs_0_), channel_id=1, source_target_pairs={{0,96},{32,64},{64,32},{96,0},{128,224},{160,192},{192,160},{224,1... | collective-permute-start | bytes 147464 | tf_op jit(solution)/shard_map/ppermute | solution.py:233
  69.2 2.2 %collective-permute-start.1 = (f32[1,96,128]{2,1,0:T(8,128)S(1)}, f32[1,96,128]{2,1,0:T(8,128)S(1)}, u32[]{:S(2)}, u32[]{:S(2)}) collective-permute-start(f32[1,96,128]{2,1,0:T(8,128)S(1)} %shard_map.53.refs_0_), channel_id=1, source_target_pairs={{0,64},{32,96},{64,0},{96,32},{128,192},{160,224},{192,128},{224,1... | collective-permute-start | bytes 147464 | tf_op jit(solution)/shard_map/ppermute | solution.py:233
  71.3 2.1 %collective-permute-start = (f32[1,96,128]{2,1,0:T(8,128)S(1)}, f32[1,96,128]{2,1,0:T(8,128)S(1)}, u32[]{:S(2)}, u32[]{:S(2)}) collective-permute-start(f32[1,96,128]{2,1,0:T(8,128)S(1)} %shard_map.53.refs_0_), channel_id=1, source_target_pairs={{0,32},{32,0},{64,96},{96,64},{128,160},{160,128},{192,224},{224,1... | collective-permute-start | bytes 147464 | tf_op jit(solution)/shard_map/ppermute | solution.py:233
  73.4 0.0 collective-permute-done.2.refs_3_
  73.4 0.6 collective-permute-done.1.refs_2_
  74.0 0.5 collective-permute-done.refs_1_
  74.5 0.0 all-to-all-done.2.m_ref
  74.5 1.2 %shard_map.54 = (f32[16,4,128]{2,1,0:T(4,128)S(1)}, f32[4,128]{1,0:T(4,128)S(1)}) custom-call(f32[32,4,128]{2,1,0:T(4,128)S(1)} %all-to-all-done.2.m_ref, f32[32,4,128]{2,1,0:T(4,128)} %shard_map.52.own_ref, f32[1,96,128]{2,1,0:T(8,128)S(1)} %shard_map.53.refs_0_, f32[1,96,128]{2,1,0:T(8,128)S(1)} %collective-permute-done.refs_1_, ...), custom_call_target="tpu_custom_call" | custom-call | tf_op jit(solution)/shard_map/pallas_call | solution.py:35
  75.6 11.3 %all_to_all.21.got_ref = f32[16,4,128]{2,1,0:T(4,128)S(1)} all-to-all(f32[16,4,128]{2,1,0:T(4,128)S(1)} %get-tuple-element.8), channel_id=1, replica_groups=mesh['ia'=16,'ja'=8,'ka'=4] {'ia'}, dimensions={0} | all-to-all | bytes 65536 | tf_op jit(solution)/shard_map/all_to_all | solution.py:235
  86.9 0.6 shard_map.55
Async XLA Ops:
  0.6 27.1 %copy-start = (f32[32,128,128]{2,1,0:T(8,128)S(1)}, f32[32,128,128]{2,1,0:T(8,128)}, u32[]{:S(2)}) copy-start(f32[32,128,128]{2,1,0:T(8,128)} %t_ref.1) | copy-start | bytes 6291460
  2.7 25.1 %all-to-all-start = ((f32[8,64,128]{2,1,0:T(8,128)}), f32[8,64,128]{2,1,0:T(8,128)S(1)}, u32[]{:S(2)}, u32[]{:S(2)}) async-start(f32[8,64,128]{2,1,0:T(8,128)} %get-tuple-element.6), calls=%async_computation | async-start | bytes 524288 | tf_op jit(solution)/shard_map/all_to_all | solution.py:226
  52.1 22.4 %all-to-all-start.2 = ((f32[32,4,128]{2,1,0:T(4,128)}), f32[32,4,128]{2,1,0:T(4,128)S(1)}, u32[]{:S(2)}, u32[]{:S(2)}) async-start(f32[32,4,128]{2,1,0:T(4,128)} %shard_map.52.own_ref), calls=%async_computation.2 | async-start | bytes 131072 | tf_op jit(solution)/shard_map/all_to_all | solution.py:231
  61.2 12.2 %collective-permute-start.2 = (f32[1,96,128]{2,1,0:T(8,128)S(1)}, f32[1,96,128]{2,1,0:T(8,128)S(1)}, u32[]{:S(2)}, u32[]{:S(2)}) collective-permute-start(f32[1,96,128]{2,1,0:T(8,128)S(1)} %shard_map.53.refs_0_), channel_id=1, source_target_pairs={{0,96},{32,64},{64,32},{96,0},{128,224},{160,192},{192,160},{224,1... | collective-permute-start | bytes 147464 | tf_op jit(solution)/shard_map/ppermute | solution.py:233
  69.2 4.8 %collective-permute-start.1 = (f32[1,96,128]{2,1,0:T(8,128)S(1)}, f32[1,96,128]{2,1,0:T(8,128)S(1)}, u32[]{:S(2)}, u32[]{:S(2)}) collective-permute-start(f32[1,96,128]{2,1,0:T(8,128)S(1)} %shard_map.53.refs_0_), channel_id=1, source_target_pairs={{0,64},{32,96},{64,0},{96,32},{128,192},{160,224},{192,128},{224,1... | collective-permute-start | bytes 147464 | tf_op jit(solution)/shard_map/ppermute | solution.py:233
  71.3 3.1 %collective-permute-start = (f32[1,96,128]{2,1,0:T(8,128)S(1)}, f32[1,96,128]{2,1,0:T(8,128)S(1)}, u32[]{:S(2)}, u32[]{:S(2)}) collective-permute-start(f32[1,96,128]{2,1,0:T(8,128)S(1)} %shard_map.53.refs_0_), channel_id=1, source_target_pairs={{0,32},{32,0},{64,96},{96,64},{128,160},{160,128},{192,224},{224,1... | collective-permute-start | bytes 147464 | tf_op jit(solution)/shard_map/ppermute | solution.py:233
